TPU v7x, 512 devices: a whole 4x4x16 slice. The times are simulated.
512 devices in a mesh: section: 8 (over z_hi, x), dp: 64 (over z_lo, y, core).
Axes of the slice: x: 4, y: 4, z: 16 (z_hi: 2, z_lo: 8; z = z_hi * 8 + z_lo), core: 2. Of those that a mesh axis runs over, the one named last changes fastest.
Arguments:
- inputs: bfloat16 [8192, 512], P('dp'), may hold values from -16 to 16
- targets: bfloat16 [8192, 512], P('dp'), may hold values from -6 to 6
- w_in: bfloat16 [8, 512, 2048], P('section', 'dp'), may hold values from -0.25 to 0.25
- w_out: bfloat16 [8, 2048, 512], P('section', 'dp'), may hold values from -0.125 to 0.125
- probes: bfloat16 [8, 512, 2048], P('section'), may hold values from -1 to 1, as said below
Outputs:
- diagonal: float32 [8, 512, 2048], P('section', 'dp')
Inputs may be any that keep to these rules, and one draw needn't show every extreme that they name: `probes`: every entry is -1 or +1.
All inputs are finite; a program needn't handle non-finite values.
Results may differ from a plain program's by a relative error of at most 0.01.
Values may be sent and summed in bfloat16 or wider, within the bound.
No kernel may reach another device: no remote copies, remote signals or barrier semaphores. Data moves between devices by JAX's collectives and lax.ppermute only.
A program may use at most 64 MiB of HBM per device.

v0:
```python
import functools
import itertools

import jax
import jax.numpy as jnp
from jax import lax
from jax.experimental import pallas as pl
from jax.experimental.pallas import tpu as pltpu
from jax.sharding import Mesh, PartitionSpec as P

EPSILON = 1e-05
SQRT_HALF = 0.7071067811865476
INV_ROOT_TWO_PI = 0.3989422804014327
CONTRACT_FIRST = (((0,), (0,)), ((), ()))

NAMES = ("zh", "x", "b4", "b2", "b1", "y", "c")
SIZES = (2, 4, 2, 2, 2, 4, 2)
SECTION = ("zh", "x")
DP = ("b4", "b2", "b1", "y", "c")
LAYERS = 8
FEATURES = 512
HIDDEN = 2048
MICRO = 2
ROWS = 128 // MICRO
UNROLL = 1
TURN_TICK = 3
TOKENS = 8192
CHUNK = 1024
CHUNKS = HIDDEN // CHUNK
VMEM_BYTES = 4 * 1024 * 1024
WHOLE = pl.BlockSpec(memory_space=pltpu.VMEM)
SMEM = pl.BlockSpec(memory_space=pltpu.SMEM)


def flat(place):
    index = 0
    for size, at in zip(SIZES, place):
        index = index * size + at
    return index


def routed(value, route):
    pairs = []
    for place in itertools.product(*(range(size) for size in SIZES)):
        there = route(*place)
        if there is not None:
            pairs.append((flat(place), flat(there)))
    return lax.ppermute(value, NAMES, pairs)


def swap_b4(zh, x, b4, b2, b1, y, c):
    return (zh, x, 1 - b4, b2, b1, y, c)


def goal_route(zh, x, b4, b2, b1, y, c):
    return (zh, x, 1 - b4, 1 - b2, 1 - b1, y, c) if (zh, x) == (1, 3) else None


def swap_b2(zh, x, b4, b2, b1, y, c):
    return (zh, x, b4, 1 - b2, b1, y, c)


def swap_b1(zh, x, b4, b2, b1, y, c):
    return (zh, x, b4, b2, 1 - b1, y, c)


def swap_even(zh, x, b4, b2, b1, y, c):
    return (zh, x, b4, b2, b1, y ^ 1, c)


def swap_odd(zh, x, b4, b2, b1, y, c):
    return (zh, x, b4, b2, b1, y ^ 3, c)


def swap_core(zh, x, b4, b2, b1, y, c):
    return (zh, x, b4, b2, b1, y, 1 - c)


def up_from(section):
    def route(zh, x, b4, b2, b1, y, c):
        if x != section % 4 or (x == 3 and zh == 1):
            return None
        if x == 3:
            return (1, 0, 1 - b4, 1 - b2, 1 - b1, y, c)
        return (zh, x + 1, b4, b2, b1, y, c)

    return route


def down_from(section):
    def route(zh, x, b4, b2, b1, y, c):
        if x != section % 4 or (x == 0 and zh == 0):
            return None
        if x == 0:
            return (0, 3, 1 - b4, 1 - b2, 1 - b1, y, c)
        return (zh, x - 1, b4, b2, b1, y, c)

    return route


def merged(own, other, bit):
    first = bit == 0
    return jnp.concatenate([jnp.where(first, own, other), jnp.where(first, other, own)], axis=0)


def merged_outer(own, other):
    y = lax.axis_index("y")
    outer = (y == 0) | (y == 3)
    rows = own.shape[0] // 2
    own_a, own_b, oth_a, oth_b = own[:rows], own[rows:], other[:rows], other[rows:]
    return jnp.concatenate(
        [
            jnp.where(outer, own_a, oth_a),
            jnp.where(outer, oth_a, own_a),
            jnp.where(outer, oth_b, own_b),
            jnp.where(outer, own_b, oth_b),
        ],
        axis=0,
    )


def gathered(block, even_first, beside=None):
    results = ()
    block = merged(block, routed(block, swap_b4), lax.axis_index("b4"))
    block = merged(block, routed(block, swap_b2), lax.axis_index("b2"))
    block = merged(block, routed(block, swap_b1), lax.axis_index("b1"))
    y = lax.axis_index("y")
    if even_first:
        if beside is not None:
            block, results = beside(block)
        block = merged(block, routed(block, swap_even), y % 2)
        block, *results = lax.optimization_barrier((block, *results))
        block = merged(block, routed(block, swap_odd), y // 2)
    else:
        block = merged(block, routed(block, swap_odd), y // 2)
        block = merged_outer(block, routed(block, swap_even))
    return block, routed(block, swap_core), *results


def row_mean(values):
    return jnp.mean(values, axis=-1, keepdims=True)


def columns(chunk):
    return pl.ds(pl.multiple_of(chunk * CHUNK, CHUNK), CHUNK)


def opening_kernel(this_core, inputs, probe, order, lhs, preact_t):
    position = lax.broadcasted_iota(jnp.int32, (FEATURES, FEATURES), 1)
    natural = lax.broadcasted_iota(jnp.int32, (FEATURES, FEATURES), 0)
    core, y = (position // 256) ^ this_core[0], (position // 64) % 4
    b1, b2, b4, row = (position // 32) % 2, (position // 16) % 2, (position // 8) % 2, position % 8
    at = (b4 * 4 + b2 * 2 + b1) * 64 + y * 16 + core * 8 + row
    order[...] = jnp.where(natural == at, 1.0, 0.0).astype(jnp.bfloat16)
    inflow = inputs[...].astype(jnp.float32)
    centred = inflow - row_mean(inflow)
    normed = (centred * lax.rsqrt(row_mean(centred * centred) + EPSILON)).astype(jnp.bfloat16)
    lhs[...] = jnp.dot(normed, order[...], preferred_element_type=jnp.float32).astype(jnp.bfloat16)

    def step(chunk, carry):
        preact_t[:, columns(chunk)] = jnp.dot(normed, probe[:, columns(chunk)], preferred_element_type=jnp.float32)
        return carry

    lax.fori_loop(0, CHUNKS, step, 0)


def opening_call(core, inputs, probe):
    rows = inputs.shape[0]
    return pl.pallas_call(
        opening_kernel,
        out_shape=[
            jax.ShapeDtypeStruct((FEATURES, FEATURES), jnp.bfloat16),
            jax.ShapeDtypeStruct((rows, FEATURES), jnp.bfloat16),
            jax.ShapeDtypeStruct((rows, HIDDEN), jnp.float32),
        ],
        in_specs=[SMEM] + [WHOLE] * 2,
        out_specs=[WHOLE] * 3,
        compiler_params=PARAMS,
        name="opening",
    )(core, inputs, probe)


def gelu_slopes(preact, preact_t, slope_out, chunk):
    normal_cdf = 0.5 * (1.0 + lax.erf(preact * SQRT_HALF))
    density = INV_ROOT_TWO_PI * jnp.exp(-0.5 * preact * preact)
    slope = normal_cdf + preact * density
    slope_out[0, :, columns(chunk)] = slope
    slope_out[1, :, columns(chunk)] = density * (2.0 - preact * preact) * preact_t
    return jnp.concatenate([preact * normal_cdf, slope * preact_t], axis=0).astype(jnp.bfloat16)


def halves_product(lhs, own_in, other_in, now):
    return jnp.dot(lhs[:, OWN_HALF], own_in[:, now], preferred_element_type=jnp.float32) + jnp.dot(
        lhs[:, OTHER_HALF], other_in[:, now], preferred_element_type=jnp.float32
    )


def first_kernel(micro, section, inputs, opening_lhs, opening_t, own_in, other_in, w_out, pair_out, slope_out, acc):
    rows = slice(micro * ROWS, (micro + 1) * ROWS)

    @pl.when(section[0] == 0)
    def _():
        acc[:ROWS] = inputs[rows].astype(jnp.float32)
        acc[ROWS:] = jnp.zeros((ROWS, FEATURES), jnp.float32)

        def step(chunk, carry):
            preact = halves_product(opening_lhs[rows], own_in, other_in, columns(chunk))
            hidden = gelu_slopes(preact, opening_t[rows, columns(chunk)], slope_out, chunk)
            acc[...] += jnp.dot(hidden, w_out[columns(chunk), :], preferred_element_type=jnp.float32)
            return carry

        lax.fori_loop(0, CHUNKS, step, 0, unroll=UNROLL)
        pair_out[0] = acc[:ROWS].astype(jnp.bfloat16)
        pair_out[1] = acc[ROWS:].astype(jnp.bfloat16)


def forward_kernel(tick, *refs):
    last = tick == LAYERS - 1
    section, pair, own_in, other_in, probe, w_out, order = refs[:7]
    refs = refs[7:]
    if last:
        goal, refs = refs[0], refs[1:]
    pair_out, norm, stat, slope_out, natural, lhs, acc = refs

    @pl.when(section[0] == tick)
    def _():
        inflow = pair[0].astype(jnp.float32)
        inflow_t = pair[1].astype(jnp.float32)
        centred = inflow - row_mean(inflow)
        rscale = lax.rsqrt(row_mean(centred * centred) + EPSILON)
        normed = centred * rscale
        tangent_dot = row_mean(normed * inflow_t)
        normed_t = rscale * (inflow_t - row_mean(inflow_t) - normed * tangent_dot)
        norm[0] = normed
        norm[1] = normed_t
        stat[0] = jnp.broadcast_to(rscale, (ROWS, 128))
        stat[1] = jnp.broadcast_to(tangent_dot, (ROWS, 128))
        acc[:ROWS] = inflow
        acc[ROWS:] = inflow_t
        natural[:ROWS] = normed.astype(jnp.bfloat16)
        natural[ROWS:] = normed_t.astype(jnp.bfloat16)
        lhs[...] = jnp.dot(natural[...], order[...], preferred_element_type=jnp.float32).astype(jnp.bfloat16)

        def step(chunk, carry):
            both = halves_product(lhs[...], own_in, other_in, columns(chunk))
            preact_t = both[ROWS:] + jnp.dot(
                natural[:ROWS], probe[:, columns(chunk)], preferred_element_type=jnp.float32
            )
            hidden = gelu_slopes(both[:ROWS], preact_t, slope_out, chunk)
            acc[...] += jnp.dot(hidden, w_out[columns(chunk), :], preferred_element_type=jnp.float32)
            return carry

        lax.fori_loop(0, CHUNKS, step, 0, unroll=UNROLL)
        if last:
            pair_out[0] = ((acc[:ROWS] - goal[...].astype(jnp.float32)) / TOKENS).astype(jnp.bfloat16)
            pair_out[1] = (acc[ROWS:] / TOKENS).astype(jnp.bfloat16)
        else:
            pair_out[0] = acc[:ROWS].astype(jnp.bfloat16)
            pair_out[1] = acc[ROWS:].astype(jnp.bfloat16)


NORM = jax.ShapeDtypeStruct((2, ROWS, FEATURES), jnp.float32)
STAT = jax.ShapeDtypeStruct((2, ROWS, 128), jnp.float32)
SLOPE = jax.ShapeDtypeStruct((2, ROWS, HIDDEN), jnp.float32)
PAIR = jax.ShapeDtypeStruct((2, ROWS, FEATURES), jnp.bfloat16)
GRADS = jax.ShapeDtypeStruct((2 * ROWS, HIDDEN), jnp.bfloat16)
PARAMS = pltpu.CompilerParams(vmem_limit_bytes=VMEM_BYTES)


def first_call(micro, section, inputs, opening_lhs, opening_t, own_in, other_in, w_out):
    return pl.pallas_call(
        functools.partial(first_kernel, micro),
        out_shape=[PAIR, SLOPE],
        in_specs=[SMEM] + [WHOLE] * 6,
        out_specs=[WHOLE] * 2,
        scratch_shapes=[pltpu.VMEM((2 * ROWS, FEATURES), jnp.float32)],
        compiler_params=PARAMS,
        name="layer_up_0",
    )(section, inputs, opening_lhs, opening_t, own_in, other_in, w_out)


def forward_call(tick, section, pair, own_in, other_in, probe, w_out, order, goal):
    operands = [section, pair, own_in, other_in, probe, w_out, order] + ([goal] if tick == LAYERS - 1 else [])
    return pl.pallas_call(
        functools.partial(forward_kernel, tick),
        out_shape=[PAIR, NORM, STAT, SLOPE],
        in_specs=[SMEM] + [WHOLE] * (len(operands) - 1),
        out_specs=[WHOLE] * 4,
        scratch_shapes=[
            pltpu.VMEM((2 * ROWS, FEATURES), jnp.bfloat16),
            pltpu.VMEM((2 * ROWS, FEATURES), jnp.bfloat16),
            pltpu.VMEM((2 * ROWS, FEATURES), jnp.float32),
        ],
        compiler_params=PARAMS,
        name=f"layer_up_{tick}",
    )(*operands)


def turned_kernel(own_in, other_in, probe, w_out, order, token, w_in_t, probe_t, w_out_t):
    by_place = (((0,), (1,)), ((), ()))

    def step(index, carry):
        now = pl.ds(pl.multiple_of(index * FEATURES, FEATURES), FEATURES)
        own = lax.dot_general(own_in[:, now], order[:, OWN_HALF], by_place, preferred_element_type=jnp.float32)
        other = lax.dot_general(other_in[:, now], order[:, OTHER_HALF], by_place, preferred_element_type=jnp.float32)
        w_in_t[now, :] = (own + other).astype(jnp.bfloat16)
        probe_t[now, :] = probe[:, now].T
        w_out_t[:, now] = w_out[now, :].T
        return carry

    lax.fori_loop(0, HIDDEN // FEATURES, step, 0)


def turned_call(own_in, other_in, probe, w_out, order, token):
    tall = jax.ShapeDtypeStruct((HIDDEN, FEATURES), jnp.bfloat16)
    wide = jax.ShapeDtypeStruct((FEATURES, HIDDEN), jnp.bfloat16)
    return pl.pallas_call(
        turned_kernel,
        out_shape=[tall, tall, wide],
        in_specs=[WHOLE] * 5 + [pl.BlockSpec(memory_space=pl.ANY)],
        out_specs=[WHOLE] * 3,
        compiler_params=PARAMS,
        name="turned_weights",
    )(own_in, other_in, probe, w_out, order, token)


def hidden_grads(pair, w_out_t, slope, chunk):
    both = jnp.dot(
        pair[...].reshape(2 * ROWS, FEATURES), w_out_t[:, columns(chunk)], preferred_element_type=jnp.float32
    )
    grad_hidden, grad_hidden_t = both[:ROWS], both[ROWS:]
    slope_chunk = slope[0, :, columns(chunk)]
    grad_pre = grad_hidden * slope_chunk
    grad_pre_t = grad_hidden_t * slope_chunk + grad_hidden * slope[1, :, columns(chunk)]
    return grad_pre.astype(jnp.bfloat16), grad_pre_t.astype(jnp.bfloat16)


def norm_apply(values, normed, rscale):
    return rscale * (values - row_mean(values) - normed * row_mean(normed * values))


def backward_kernel(tick, *refs):
    section, pair, w_in_t, probe_t, w_out_t, norm, stat, slope = refs[:8]
    pair_out, grads, acc, acc_t = refs[8:]

    @pl.when(section[0] == LAYERS - 1 - tick)
    def _():
        acc[...] = jnp.zeros_like(acc)
        acc_t[...] = jnp.zeros_like(acc_t)

        def step(chunk, carry):
            low_grad, low_grad_t = hidden_grads(pair, w_out_t, slope, chunk)
            both = jnp.concatenate([low_grad_t, low_grad], axis=0)
            grads[:, columns(chunk)] = both
            acc[...] += jnp.dot(both, w_in_t[columns(chunk), :], preferred_element_type=jnp.float32)
            acc_t[...] += jnp.dot(low_grad, probe_t[columns(chunk), :], preferred_element_type=jnp.float32)
            return carry

        lax.fori_loop(0, CHUNKS, step, 0, unroll=UNROLL)
        normed, normed_t = norm[0], norm[1]
        rscale, tangent_dot = stat[0][:, :1], stat[1][:, :1]
        grad_norm = acc[ROWS:]
        grad_norm_t = acc[:ROWS] + acc_t[...]
        through = norm_apply(grad_norm, normed, rscale)
        through_t = (
            norm_apply(grad_norm_t, normed, rscale)
            - rscale * tangent_dot * through
            - rscale * (normed_t * row_mean(normed * grad_norm) + normed * row_mean(normed_t * grad_norm))
        )
        pair_out[0] = (pair[0].astype(jnp.float32) + through).astype(jnp.bfloat16)
        pair_out[1] = (pair[1].astype(jnp.float32) + through_t).astype(jnp.bfloat16)


def backward_call(tick, section, pair, w_in_t, probe_t, w_out_t, kept):
    operands = [section, pair, w_in_t, probe_t, w_out_t, *kept]
    return pl.pallas_call(
        functools.partial(backward_kernel, tick),
        out_shape=[PAIR, GRADS],
        in_specs=[SMEM] + [WHOLE] * (len(operands) - 1),
        out_specs=[WHOLE] * 2,
        scratch_shapes=[
            pltpu.VMEM((2 * ROWS, FEATURES), jnp.float32),
            pltpu.VMEM((ROWS, FEATURES), jnp.float32),
        ],
        compiler_params=PARAMS,
        name=f"layer_down_{tick}",
    )(*operands)


OWN_HALF = slice(0, FEATURES // 2)
OTHER_HALF = slice(FEATURES // 2, FEATURES)


def curvature_operands(micro, section, pair, w_out_t, slope, order, opening_lhs, norms, grads, lhs, rhs):
    @pl.when(section[0] == 0)
    def _():
        lhs[:ROWS] = opening_lhs[micro * ROWS : (micro + 1) * ROWS]
        lhs[ROWS:] = jnp.zeros((ROWS, FEATURES), jnp.bfloat16)

        def bottom(chunk, carry):
            low_grad, low_grad_t = hidden_grads(pair, w_out_t, slope, chunk)
            rhs[:, columns(chunk)] = jnp.concatenate([low_grad_t, low_grad], axis=0)
            return carry

        lax.fori_loop(0, CHUNKS, bottom, 0, unroll=UNROLL)

    for layer in range(1, LAYERS):

        @pl.when(section[0] == layer)
        def _():
            both = norms[layer - 1][...].reshape(2 * ROWS, FEATURES).astype(jnp.bfloat16)
            lhs[...] = jnp.dot(both, order[...], preferred_element_type=jnp.float32).astype(jnp.bfloat16)
            rhs[...] = grads[LAYERS - 1 - layer][...]


def curvature_kernel(micro, final, *refs):
    section, pair, w_out_t, slope, order, opening_lhs = refs[:6]
    norms, refs = refs[6 : 5 + LAYERS], refs[5 + LAYERS :]
    grads, refs = refs[: LAYERS - 1], refs[LAYERS - 1 :]
    if final:
        away_in, stay_in, refs = refs[0], refs[1], refs[2:]
    away, stay, lhs, rhs = refs
    curvature_operands(micro, section, pair, w_out_t, slope, order, opening_lhs, norms, grads, lhs, rhs)

    def step(chunk, carry):
        now = columns(chunk)

        def product(half):
            return lax.dot_general(lhs[:, half], rhs[:, now], CONTRACT_FIRST, preferred_element_type=jnp.float32)

        if final:
            away[:, now] = (away_in[:, now] + product(OTHER_HALF)).astype(jnp.bfloat16)
            stay[:, now] = stay_in[:, now] + product(OWN_HALF)
        else:
            away[:, now] = product(OTHER_HALF)
            stay[:, now] = product(OWN_HALF)
        return carry

    lax.fori_loop(0, CHUNKS, step, 0, unroll=UNROLL)


def curvature_call(micro, section, pair, w_out_t, slope, order, opening_lhs, norms, grads, sums):
    half = (FEATURES // 2, HIDDEN)
    final = bool(sums)
    operands = [section, pair, w_out_t, slope, order, opening_lhs, *norms, *grads, *sums]
    return pl.pallas_call(
        functools.partial(curvature_kernel, micro, final),
        out_shape=[
            jax.ShapeDtypeStruct(half, jnp.bfloat16 if final else jnp.float32),
            jax.ShapeDtypeStruct(half, jnp.float32),
        ],
        in_specs=[SMEM] + [WHOLE] * (len(operands) - 1),
        out_specs=[WHOLE] * 2,
        scratch_shapes=[
            pltpu.VMEM((2 * ROWS, FEATURES), jnp.bfloat16),
            pltpu.VMEM((2 * ROWS, HIDDEN), jnp.bfloat16),
        ],
        compiler_params=PARAMS,
        name="curvature_last" if final else "curvature_first",
    )(*operands)


def shards(inputs, targets, w_in, w_out, probes):
    section = jnp.reshape(lax.axis_index(SECTION), (1,)).astype(jnp.int32)
    core = jnp.reshape(lax.axis_index("c"), (1,)).astype(jnp.int32)
    probe = probes[0]

    def opening(block):
        block, inputs_now = lax.optimization_barrier((block, inputs))
        return block, opening_call(core, inputs_now, probe)

    own_in, other_in, order, opening_lhs, opening_t = gathered(w_in[0], True, opening)
    full_out = merged(*gathered(w_out[0], False), lax.axis_index("c"))
    full_out = (
        full_out.reshape(2, 4, 2, 2, 2, 32, FEATURES).transpose(4, 3, 2, 1, 0, 5, 6).reshape(HIDDEN, FEATURES)
    )
    goal = routed(targets, goal_route)
    pairs, slopes, kept, grads = [None] * MICRO, [], [], []
    for micro in range(MICRO):
        kept.append([])
        grads.append([])
    for tick in range(LAYERS):
        for micro in range(MICRO):
            if tick == 0:
                pairs[micro], slope = first_call(
                    micro, section, inputs, opening_lhs, opening_t, own_in, other_in, full_out
                )
                slopes.append(slope)
            else:
                goal_now = goal[micro * ROWS : (micro + 1) * ROWS]
                pairs[micro], *stores = forward_call(
                    tick, section, pairs[micro], own_in, other_in, probe, full_out, order, goal_now
                )
                kept[micro].append(stores)
            if tick < LAYERS - 1:
                pairs[micro] = routed(pairs[micro], up_from(tick))
        if tick == TURN_TICK:
            turned = turned_call(own_in, other_in, probe, full_out, order, kept[-1][-1][0])
    for tick in range(LAYERS - 1):
        for micro in range(MICRO):
            pairs[micro], low_grads = backward_call(
                tick, section, pairs[micro], *turned, kept[micro][LAYERS - 2 - tick]
            )
            grads[micro].append(low_grads)
            pairs[micro] = routed(pairs[micro], down_from(LAYERS - 1 - tick))
    sums = ()
    for micro in range(MICRO):
        norms = [stores[0] for stores in kept[micro]]
        sums = curvature_call(
            micro, section, pairs[micro], turned[2], slopes[micro], order, opening_lhs, norms, grads[micro], sums
        )
    away, stay = sums
    other = routed(away, swap_core)
    summed = (stay + other.astype(jnp.float32)).astype(jnp.bfloat16)
    summed = lax.all_to_all(summed.reshape(4, 64, HIDDEN), "y", 0, 0, tiled=True)
    summed = jnp.sum(summed.astype(jnp.float32), axis=0).astype(jnp.bfloat16)
    summed = lax.all_to_all(summed.reshape(8, 8, HIDDEN), ("b1", "b2", "b4"), 0, 0, tiled=True)
    summed = jnp.sum(summed.astype(jnp.float32), axis=0)
    probe_own = lax.dynamic_slice_in_dim(probe, lax.axis_index(DP) * 8, 8, 0)
    return (probe_own.astype(jnp.float32) * summed)[None]


def solution(mesh):
    fine = Mesh(mesh.devices.reshape(SIZES), NAMES)
    return jax.shard_map(
        shards,
        mesh=fine,
        in_specs=(
            P(DP, None),
            P(DP, None),
            P(SECTION, DP, None),
            P(SECTION, DP, None),
            P(SECTION, None, None),
        ),
        out_specs=P(SECTION, DP, None),
        check_vma=False,
    )
```

profile of v0, /device:TPU:8, one launch (start us, length us, event | category | flops | bytes accessed | tf_op | source)
XLA Modules:
  0.0 257.4 jit_solution(17963284869469682856)
XLA Ops:
  0.0 9.2 %collective-permute-start.6 = (bf16[32,512]{1,0:T(8,128)(2,1)}, bf16[32,512]{1,0:T(8,128)(2,1)S(1)}, u32[]{:S(2)}, u32[]{:S(2)}) collective-permute-start(bf16[32,512]{1,0:T(8,128)(2,1)} %bitcast.52), channel_id=1, source_target_pairs={{0,32},{1,33},{2,34},{3,35},{4,36},{5,37},{6,38},{7,39},{8,40},{9,... | collective-permute-start | bytes 98312 | tf_op jit(solution)/shard_map/ppermute | solution.py:48
  9.2 1.9 collective-permute-start
  12.1 5.5 %collective-permute-start.7 = (bf16[64,512]{1,0:T(8,128)(2,1)S(1)}, bf16[64,512]{1,0:T(8,128)(2,1)S(1)}, u32[]{:S(2)}, u32[]{:S(2)}) collective-permute-start(bf16[64,512]{1,0:T(8,128)(2,1)S(1)} %pad_maximum_fusion.10), channel_id=1, source_target_pairs={{0,16},{1,17},{2,18},{3,19},{4,20},{5,21},{6,22},{7,23},{8,24},{9,... | collective-permute-start | bytes 196616 | tf_op jit(solution)/shard_map/ppermute | solution.py:48
  17.6 1.9 collective-permute-done
  20.3 5.2 %collective-permute-start.1 = (bf16[16,2048]{1,0:T(8,128)(2,1)S(1)}, bf16[16,2048]{1,0:T(8,128)(2,1)S(1)}, u32[]{:S(2)}, u32[]{:S(2)}) collective-permute-start(bf16[16,2048]{1,0:T(8,128)(2,1)S(1)} %pad_maximum_fusion.9), channel_id=1, source_target_pairs={{0,16},{1,17},{2,18},{3,19},{4,20},{5,21},{6,22},{7,23},{8,24},{9,... | collective-permute-start | bytes 196616 | tf_op jit(solution)/shard_map/ppermute | solution.py:48
  25.6 3.4 %collective-permute-start.8 = (bf16[128,512]{1,0:T(8,128)(2,1)S(1)}, bf16[128,512]{1,0:T(8,128)(2,1)S(1)}, u32[]{:S(2)}, u32[]{:S(2)}) collective-permute-start(bf16[128,512]{1,0:T(8,128)(2,1)S(1)} %pad_maximum_fusion.8), channel_id=1, source_target_pairs={{0,8},{1,9},{2,10},{3,11},{4,12},{5,13},{6,14},{7,15},{8,0},{9,1},... | collective-permute-start | bytes 393224 | tf_op jit(solution)/shard_map/ppermute | solution.py:48
  29.1 2.5 collective-permute-start.2
  31.6 1.9 collective-permute-done.8
  33.6 3.5 %collective-permute-start.9 = (bf16[256,512]{1,0:T(8,128)(2,1)S(1)}, bf16[256,512]{1,0:T(8,128)(2,1)S(1)}, u32[]{:S(2)}, u32[]{:S(2)}) collective-permute-start(bf16[256,512]{1,0:T(8,128)(2,1)S(1)} %pad_maximum_fusion.6), channel_id=1, source_target_pairs={{0,6},{1,7},{2,4},{3,5},{4,2},{5,3},{6,0},{7,1},{8,14},{9,15},{10,... | collective-permute-start | bytes 786440 | tf_op jit(solution)/shard_map/ppermute | solution.py:48
  37.2 3.8 %collective-permute-start.3 = (bf16[64,2048]{1,0:T(8,128)(2,1)S(1)}, bf16[64,2048]{1,0:T(8,128)(2,1)S(1)}, u32[]{:S(2)}, u32[]{:S(2)}) collective-permute-start(bf16[64,2048]{1,0:T(8,128)(2,1)S(1)} %pad_maximum_fusion.5), channel_id=1, source_target_pairs={{0,2},{1,3},{2,0},{3,1},{4,6},{5,7},{6,4},{7,5},{8,10},{9,11},{10,... | collective-permute-start | bytes 786440 | tf_op jit(solution)/shard_map/ppermute | solution.py:48
  44.7 2.0 collective-permute-start.10
  46.9 3.9 %collective-permute-start.4 = (bf16[128,2048]{1,0:T(8,128)(2,1)S(1)}, bf16[128,2048]{1,0:T(8,128)(2,1)}, u32[]{:S(2)}, u32[]{:S(2)}) collective-permute-start(bf16[128,2048]{1,0:T(8,128)(2,1)S(1)} %pad_maximum_fusion.3), channel_id=1, source_target_pairs={{0,6},{1,7},{2,4},{3,5},{4,2},{5,3},{6,0},{7,1},{8,14},{9,15},{10,... | collective-permute-start | bytes 1572872 | tf_op jit(solution)/shard_map/ppermute | solution.py:48
  50.8 6.0 %collective-permute-done.10 = bf16[512,512]{1,0:T(8,128)(2,1)} collective-permute-done((bf16[512,512]{1,0:T(8,128)(2,1)}, bf16[512,512]{1,0:T(8,128)(2,1)}, u32[]{:S(2)}, u32[]{:S(2)}) %collective-permute-start.10) | collective-permute-done | bytes 524320 | tf_op jit(solution)/shard_map/ppermute | solution.py:48
  59.1 1.9 collective-permute-start.11
  62.3 2.4 collective-permute-start.5
  64.7 1.9 broadcast_select_fusion.1
  68.0 2.5 layer_up_0.3
  70.5 2.2 collective-permute-start.27
  72.7 2.5 layer_up_0.2
  75.2 1.3 collective-permute-start.12
  76.6 1.2 layer_up_1.3
  81.3 1.2 layer_up_2.3
  83.3 1.2 layer_up_2.2
  85.2 1.2 layer_up_3.3
  87.1 1.2 layer_up_3.2
  89.0 1.2 layer_up_4.3
  90.2 8.0 %collective-permute-start.31 = (bf16[2,64,512]{2,1,0:T(8,128)(2,1)S(1)}, bf16[2,64,512]{2,1,0:T(8,128)(2,1)S(1)}, u32[]{:S(2)}, u32[]{:S(2)}) collective-permute-start(bf16[2,64,512]{2,1,0:T(8,128)(2,1)S(1)} %get-tuple-element.169), channel_id=1, source_target_pairs={{0,64},{1,65},{2,66},{3,67},{4,68},{5,69},{6,70},{7,71},{8,72},{9,... | collective-permute-start | bytes 393224 | tf_op jit(solution)/shard_map/ppermute | solution.py:48
  98.2 1.2 layer_up_4.2
  99.5 1.3 collective-permute-start.16
  104.0 1.2 layer_up_5.2
  106.5 1.2 layer_up_6.3
  108.5 1.2 layer_up_6.2
  110.4 3.3 %turned_weights.1 = (bf16[2048,512]{1,0:T(8,128)(2,1)S(1)}, bf16[2048,512]{1,0:T(8,128)(2,1)S(1)}, bf16[512,2048]{1,0:T(8,128)(2,1)S(1)}) custom-call(bf16[256,2048]{1,0:T(8,128)(2,1)S(1)} %pad_maximum_fusion.1.own_in.refs_2_, bf16[256,2048]{1,0:T(8,128)(2,1)} %collective-permute-done.5.other_in.refs_3_, bf16[512,2048]{1,0:T(8,128)(2,1)S(1)} %bitcast.47, ...), custom_call_target="tpu_custom_call" | custom-call | tf_op jit(solution)/shard_map/turned_weights/pallas_call | solution.py:317
  113.7 1.2 layer_up_7.3
  119.0 1.3 collective-permute-start.36
  120.3 1.3 collective-permute-start.22
  121.6 35.1 %collective-permute-done.36.refs_1_ = bf16[2,64,512]{2,1,0:T(8,128)(2,1)S(1)} collective-permute-done((bf16[2,64,512]{2,1,0:T(8,128)(2,1)S(1)}, bf16[2,64,512]{2,1,0:T(8,128)(2,1)S(1)}, u32[]{:S(2)}, u32[]{:S(2)}) %collective-permute-start.36) | collective-permute-done | bytes 131104 | tf_op jit(solution)/shard_map/ppermute | solution.py:48
  161.9 1.3 collective-permute-start.40
  163.2 1.3 collective-permute-start.26
  164.5 40.5 %collective-permute-done.40.refs_1_ = bf16[2,64,512]{2,1,0:T(8,128)(2,1)S(1)} collective-permute-done((bf16[2,64,512]{2,1,0:T(8,128)(2,1)S(1)}, bf16[2,64,512]{2,1,0:T(8,128)(2,1)S(1)}, u32[]{:S(2)}, u32[]{:S(2)}) %collective-permute-start.40) | collective-permute-done | bytes 131104 | tf_op jit(solution)/shard_map/ppermute | solution.py:48
  205.0 1.6 curvature_first.1
  206.6 1.3 collective-permute-done.26.refs_1_
  207.9 1.6 curvature_last.1
  209.6 1.9 collective-permute-start.41
  211.5 2.6 %collective-permute-done.41 = bf16[256,2048]{1,0:T(8,128)(2,1)S(1)} collective-permute-done((bf16[256,2048]{1,0:T(8,128)(2,1)S(1)}, bf16[256,2048]{1,0:T(8,128)(2,1)S(1)}, u32[]{:S(2)}, u32[]{:S(2)}) %collective-permute-start.41) | collective-permute-done | bytes 1048608 | tf_op jit(solution)/shard_map/ppermute | solution.py:48
  214.4 18.1 %all_to_all.10 = bf16[4,64,2048]{2,1,0:T(8,128)(2,1)S(1)} all-to-all(bf16[4,64,2048]{2,1,0:T(8,128)(2,1)S(1)} %bitcast.51), channel_id=1, replica_groups=mesh['zh'=2,'x'=4,'b4'=2,'b2'=2,'b1'=2,'y'=4,'c'=2] {'y'}, dimensions={0} | all-to-all | bytes 2097152 | tf_op jit(solution)/shard_map/all_to_all | solution.py:515
  233.4 7.8 %all-to-all-start.1 = ((bf16[8,8,2048]{2,1,0:T(8,128)(2,1)}), bf16[8,8,2048]{2,1,0:T(8,128)(2,1)S(1)}, u32[]{:S(2)}, u32[]{:S(2)}) async-start(bf16[8,8,2048]{2,1,0:T(8,128)(2,1)} %bitcast.10), calls=%async_computation.1 | async-start | bytes 524288 | tf_op jit(solution)/shard_map/all_to_all | solution.py:517
  241.2 15.5 %all-to-all-done.1 = bf16[8,8,2048]{2,1,0:T(8,128)(2,1)S(1)} async-done(((bf16[8,8,2048]{2,1,0:T(8,128)(2,1)}), bf16[8,8,2048]{2,1,0:T(8,128)(2,1)S(1)}, u32[]{:S(2)}, u32[]{:S(2)}) %all-to-all-start.1) | async-done | bytes 262176 | tf_op jit(solution)/shard_map/all_to_all | solution.py:517
  (123 shorter events, 33.4 us)
Async XLA Ops:
  0.0 41.0 %copy-start.5 = (bf16[128,512]{1,0:T(8,128)(2,1)S(1)}, bf16[128,512]{1,0:T(8,128)(2,1)}, u32[]{:S(2)}) copy-start(bf16[128,512]{1,0:T(8,128)(2,1)} %inputs.4) | copy-start | bytes 393220
  0.0 41.0 %copy-start = (bf16[1,512,2048]{2,1,0:T(8,128)(2,1)S(1)}, bf16[1,512,2048]{2,1,0:T(8,128)(2,1)}, u32[]{:S(2)}) copy-start(bf16[1,512,2048]{2,1,0:T(8,128)(2,1)} %param.9) | copy-start | bytes 6291460
  0.0 11.3 %collective-permute-start.6 = (bf16[32,512]{1,0:T(8,128)(2,1)}, bf16[32,512]{1,0:T(8,128)(2,1)S(1)}, u32[]{:S(2)}, u32[]{:S(2)}) collective-permute-start(bf16[32,512]{1,0:T(8,128)(2,1)} %bitcast.52), channel_id=1, source_target_pairs={{0,32},{1,33},{2,34},{3,35},{4,36},{5,37},{6,38},{7,39},{8,40},{9,... | collective-permute-start | bytes 98312 | tf_op jit(solution)/shard_map/ppermute | solution.py:48
  9.2 10.3 %collective-permute-start = (bf16[8,2048]{1,0:T(8,128)(2,1)}, bf16[8,2048]{1,0:T(8,128)(2,1)S(1)}, u32[]{:S(2)}, u32[]{:S(2)}) collective-permute-start(bf16[8,2048]{1,0:T(8,128)(2,1)} %bitcast.53), channel_id=1, source_target_pairs={{0,32},{1,33},{2,34},{3,35},{4,36},{5,37},{6,38},{7,39},{8,40},{9,... | collective-permute-start | bytes 98312 | tf_op jit(solution)/shard_map/ppermute | solution.py:48
  12.1 13.4 %collective-permute-start.7 = (bf16[64,512]{1,0:T(8,128)(2,1)S(1)}, bf16[64,512]{1,0:T(8,128)(2,1)S(1)}, u32[]{:S(2)}, u32[]{:S(2)}) collective-permute-start(bf16[64,512]{1,0:T(8,128)(2,1)S(1)} %pad_maximum_fusion.10), channel_id=1, source_target_pairs={{0,16},{1,17},{2,18},{3,19},{4,20},{5,21},{6,22},{7,23},{8,24},{9,... | collective-permute-start | bytes 196616 | tf_op jit(solution)/shard_map/ppermute | solution.py:48
  20.3 8.8 %collective-permute-start.1 = (bf16[16,2048]{1,0:T(8,128)(2,1)S(1)}, bf16[16,2048]{1,0:T(8,128)(2,1)S(1)}, u32[]{:S(2)}, u32[]{:S(2)}) collective-permute-start(bf16[16,2048]{1,0:T(8,128)(2,1)S(1)} %pad_maximum_fusion.9), channel_id=1, source_target_pairs={{0,16},{1,17},{2,18},{3,19},{4,20},{5,21},{6,22},{7,23},{8,24},{9,... | collective-permute-start | bytes 196616 | tf_op jit(solution)/shard_map/ppermute | solution.py:48
  25.6 7.9 %collective-permute-start.8 = (bf16[128,512]{1,0:T(8,128)(2,1)S(1)}, bf16[128,512]{1,0:T(8,128)(2,1)S(1)}, u32[]{:S(2)}, u32[]{:S(2)}) collective-permute-start(bf16[128,512]{1,0:T(8,128)(2,1)S(1)} %pad_maximum_fusion.8), channel_id=1, source_target_pairs={{0,8},{1,9},{2,10},{3,11},{4,12},{5,13},{6,14},{7,15},{8,0},{9,1},... | collective-permute-start | bytes 393224 | tf_op jit(solution)/shard_map/ppermute | solution.py:48
  29.1 8.0 %collective-permute-start.2 = (bf16[32,2048]{1,0:T(8,128)(2,1)S(1)}, bf16[32,2048]{1,0:T(8,128)(2,1)S(1)}, u32[]{:S(2)}, u32[]{:S(2)}) collective-permute-start(bf16[32,2048]{1,0:T(8,128)(2,1)S(1)} %pad_maximum_fusion.7), channel_id=1, source_target_pairs={{0,8},{1,9},{2,10},{3,11},{4,12},{5,13},{6,14},{7,15},{8,0},{9,1},... | collective-permute-start | bytes 393224 | tf_op jit(solution)/shard_map/ppermute | solution.py:48
  33.6 10.2 %collective-permute-start.9 = (bf16[256,512]{1,0:T(8,128)(2,1)S(1)}, bf16[256,512]{1,0:T(8,128)(2,1)S(1)}, u32[]{:S(2)}, u32[]{:S(2)}) collective-permute-start(bf16[256,512]{1,0:T(8,128)(2,1)S(1)} %pad_maximum_fusion.6), channel_id=1, source_target_pairs={{0,6},{1,7},{2,4},{3,5},{4,2},{5,3},{6,0},{7,1},{8,14},{9,15},{10,... | collective-permute-start | bytes 786440 | tf_op jit(solution)/shard_map/ppermute | solution.py:48
  37.2 9.6 %collective-permute-start.3 = (bf16[64,2048]{1,0:T(8,128)(2,1)S(1)}, bf16[64,2048]{1,0:T(8,128)(2,1)S(1)}, u32[]{:S(2)}, u32[]{:S(2)}) collective-permute-start(bf16[64,2048]{1,0:T(8,128)(2,1)S(1)} %pad_maximum_fusion.5), channel_id=1, source_target_pairs={{0,2},{1,3},{2,0},{3,1},{4,6},{5,7},{6,4},{7,5},{8,10},{9,11},{10,... | collective-permute-start | bytes 786440 | tf_op jit(solution)/shard_map/ppermute | solution.py:48
  44.7 12.1 %collective-permute-start.10 = (bf16[512,512]{1,0:T(8,128)(2,1)}, bf16[512,512]{1,0:T(8,128)(2,1)}, u32[]{:S(2)}, u32[]{:S(2)}) collective-permute-start(bf16[512,512]{1,0:T(8,128)(2,1)} %pad_maximum_fusion.4), channel_id=1, source_target_pairs={{0,2},{1,3},{2,0},{3,1},{4,6},{5,7},{6,4},{7,5},{8,10},{9,11},{10,... | collective-permute-start | bytes 1572872 | tf_op jit(solution)/shard_map/ppermute | solution.py:48
  46.9 14.2 %collective-permute-start.4 = (bf16[128,2048]{1,0:T(8,128)(2,1)S(1)}, bf16[128,2048]{1,0:T(8,128)(2,1)}, u32[]{:S(2)}, u32[]{:S(2)}) collective-permute-start(bf16[128,2048]{1,0:T(8,128)(2,1)S(1)} %pad_maximum_fusion.3), channel_id=1, source_target_pairs={{0,6},{1,7},{2,4},{3,5},{4,2},{5,3},{6,0},{7,1},{8,14},{9,15},{10,... | collective-permute-start | bytes 1572872 | tf_op jit(solution)/shard_map/ppermute | solution.py:48
  57.9 4.3 %copy-start.6 = (bf16[256,512]{1,0:T(8,128)(2,1)}, bf16[256,512]{1,0:T(8,128)(2,1)S(1)}, u32[]{:S(2)}) copy-start(bf16[256,512]{1,0:T(8,128)(2,1)S(1)} %get-tuple-element.217) | copy-start | bytes 786436
  57.9 4.3 %copy-start.7 = (bf16[256,512]{1,0:T(8,128)(2,1)}, bf16[256,512]{1,0:T(8,128)(2,1)S(1)}, u32[]{:S(2)}) copy-start(bf16[256,512]{1,0:T(8,128)(2,1)S(1)} %get-tuple-element.218) | copy-start | bytes 786436
  59.1 5.6 %collective-permute-start.11 = (bf16[1024,512]{1,0:T(8,128)(2,1)}, bf16[1024,512]{1,0:T(8,128)(2,1)}, u32[]{:S(2)}, u32[]{:S(2)}) collective-permute-start(bf16[1024,512]{1,0:T(8,128)(2,1)} %pad_maximum_fusion.2), channel_id=1, source_target_pairs={{0,1},{1,0},{2,3},{3,2},{4,5},{5,4},{6,7},{7,6},{8,9},{9,8},{10,11... | collective-permute-start | bytes 3145736 | tf_op jit(solution)/shard_map/ppermute | solution.py:48
  62.3 4.8 %collective-permute-start.5 = (bf16[256,2048]{1,0:T(8,128)(2,1)S(1)}, bf16[256,2048]{1,0:T(8,128)(2,1)}, u32[]{:S(2)}, u32[]{:S(2)}) collective-permute-start(bf16[256,2048]{1,0:T(8,128)(2,1)S(1)} %pad_maximum_fusion.1.own_in.refs_2_), channel_id=1, source_target_pairs={{0,1},{1,0},{2,3},{3,2},{4,5},{5,4},{6,7},{7,6},{8,9},{9,8},{10,11... | collective-permute-start | bytes 3145736 | tf_op jit(solution)/shard_map/ppermute | solution.py:48
  70.5 6.1 %copy-start.2 = (bf16[512,512]{1,0:T(8,128)(2,1)S(1)}, bf16[512,512]{1,0:T(8,128)(2,1)}, u32[]{:S(2)}) copy-start(bf16[512,512]{1,0:T(8,128)(2,1)} %copy-done.1) | copy-start | bytes 1572868
  70.5 6.1 %collective-permute-start.27 = (bf16[2,64,512]{2,1,0:T(8,128)(2,1)S(1)}, bf16[2,64,512]{2,1,0:T(8,128)(2,1)S(1)}, u32[]{:S(2)}, u32[]{:S(2)}) collective-permute-start(bf16[2,64,512]{2,1,0:T(8,128)(2,1)S(1)} %get-tuple-element.165), channel_id=1, source_target_pairs={{0,64},{1,65},{2,66},{3,67},{4,68},{5,69},{6,70},{7,71},{8,72},{9,... | collective-permute-start | bytes 393224 | tf_op jit(solution)/shard_map/ppermute | solution.py:48
  75.2 4.2 %collective-permute-start.12 = (bf16[2,64,512]{2,1,0:T(8,128)(2,1)S(1)}, bf16[2,64,512]{2,1,0:T(8,128)(2,1)S(1)}, u32[]{:S(2)}, u32[]{:S(2)}) collective-permute-start(bf16[2,64,512]{2,1,0:T(8,128)(2,1)S(1)} %get-tuple-element.117), channel_id=1, source_target_pairs={{0,64},{1,65},{2,66},{3,67},{4,68},{5,69},{6,70},{7,71},{8,72},{9,... | collective-permute-start | bytes 393224 | tf_op jit(solution)/shard_map/ppermute | solution.py:48
  77.8 3.5 %collective-permute-start.28 = (bf16[2,64,512]{2,1,0:T(8,128)(2,1)S(1)}, bf16[2,64,512]{2,1,0:T(8,128)(2,1)S(1)}, u32[]{:S(2)}, u32[]{:S(2)}) collective-permute-start(bf16[2,64,512]{2,1,0:T(8,128)(2,1)S(1)} %get-tuple-element.166), channel_id=1, source_target_pairs={{64,128},{65,129},{66,130},{67,131},{68,132},{69,133},{70,134},{71... | collective-permute-start | bytes 393224 | tf_op jit(solution)/shard_map/ppermute | solution.py:48
  80.7 2.6 collective-permute-start.13
  82.6 2.6 collective-permute-start.29
  84.5 2.6 collective-permute-start.14
  86.4 2.6 collective-permute-start.30
  88.3 9.9 %collective-permute-start.15 = (bf16[2,64,512]{2,1,0:T(8,128)(2,1)S(1)}, bf16[2,64,512]{2,1,0:T(8,128)(2,1)S(1)}, u32[]{:S(2)}, u32[]{:S(2)}) collective-permute-start(bf16[2,64,512]{2,1,0:T(8,128)(2,1)S(1)} %get-tuple-element.121), channel_id=1, source_target_pairs={{192,312},{193,313},{194,314},{195,315},{196,316},{197,317},{198,3... | collective-permute-start | bytes 393224 | tf_op jit(solution)/shard_map/ppermute | solution.py:48
  90.2 11.7 %collective-permute-start.31 = (bf16[2,64,512]{2,1,0:T(8,128)(2,1)S(1)}, bf16[2,64,512]{2,1,0:T(8,128)(2,1)S(1)}, u32[]{:S(2)}, u32[]{:S(2)}) collective-permute-start(bf16[2,64,512]{2,1,0:T(8,128)(2,1)S(1)} %get-tuple-element.169), channel_id=1, source_target_pairs={{0,64},{1,65},{2,66},{3,67},{4,68},{5,69},{6,70},{7,71},{8,72},{9,... | collective-permute-start | bytes 393224 | tf_op jit(solution)/shard_map/ppermute | solution.py:48
  99.5 4.5 %collective-permute-start.16 = (bf16[2,64,512]{2,1,0:T(8,128)(2,1)S(1)}, bf16[2,64,512]{2,1,0:T(8,128)(2,1)S(1)}, u32[]{:S(2)}, u32[]{:S(2)}) collective-permute-start(bf16[2,64,512]{2,1,0:T(8,128)(2,1)S(1)} %get-tuple-element.122), channel_id=1, source_target_pairs={{0,64},{1,65},{2,66},{3,67},{4,68},{5,69},{6,70},{7,71},{8,72},{9,... | collective-permute-start | bytes 393224 | tf_op jit(solution)/shard_map/ppermute | solution.py:48
  103.2 3.4 %collective-permute-start.32 = (bf16[2,64,512]{2,1,0:T(8,128)(2,1)S(1)}, bf16[2,64,512]{2,1,0:T(8,128)(2,1)S(1)}, u32[]{:S(2)}, u32[]{:S(2)}) collective-permute-start(bf16[2,64,512]{2,1,0:T(8,128)(2,1)S(1)} %get-tuple-element.170), channel_id=1, source_target_pairs={{64,128},{65,129},{66,130},{67,131},{68,132},{69,133},{70,134},{71... | collective-permute-start | bytes 393224 | tf_op jit(solution)/shard_map/ppermute | solution.py:48
  105.2 3.3 %collective-permute-start.17 = (bf16[2,64,512]{2,1,0:T(8,128)(2,1)S(1)}, bf16[2,64,512]{2,1,0:T(8,128)(2,1)S(1)}, u32[]{:S(2)}, u32[]{:S(2)}) collective-permute-start(bf16[2,64,512]{2,1,0:T(8,128)(2,1)S(1)} %get-tuple-element.123), channel_id=1, source_target_pairs={{64,128},{65,129},{66,130},{67,131},{68,132},{69,133},{70,134},{71... | collective-permute-start | bytes 393224 | tf_op jit(solution)/shard_map/ppermute | solution.py:48
  105.9 4.5 %collective-permute-start.19 = (bf16[128,512]{1,0:T(8,128)(2,1)S(1)}, bf16[128,512]{1,0:T(8,128)(2,1)S(1)}, u32[]{:S(2)}, u32[]{:S(2)}) collective-permute-start(bf16[128,512]{1,0:T(8,128)(2,1)S(1)} %copy-done.10), channel_id=1, source_target_pairs={{448,504},{449,505},{450,506},{451,507},{452,508},{453,509},{454,5... | collective-permute-start | bytes 393224 | tf_op jit(solution)/shard_map/ppermute | solution.py:48
  107.8 5.9 %collective-permute-start.33 = (bf16[2,64,512]{2,1,0:T(8,128)(2,1)S(1)}, bf16[2,64,512]{2,1,0:T(8,128)(2,1)S(1)}, u32[]{:S(2)}, u32[]{:S(2)}) collective-permute-start(bf16[2,64,512]{2,1,0:T(8,128)(2,1)S(1)} %get-tuple-element.171), channel_id=1, source_target_pairs={{128,192},{129,193},{130,194},{131,195},{132,196},{133,197},{134,1... | collective-permute-start | bytes 393224 | tf_op jit(solution)/shard_map/ppermute | solution.py:48
  109.7 5.9 %collective-permute-start.18 = (bf16[2,64,512]{2,1,0:T(8,128)(2,1)S(1)}, bf16[2,64,512]{2,1,0:T(8,128)(2,1)S(1)}, u32[]{:S(2)}, u32[]{:S(2)}) collective-permute-start(bf16[2,64,512]{2,1,0:T(8,128)(2,1)S(1)} %get-tuple-element.124), channel_id=1, source_target_pairs={{128,192},{129,193},{130,194},{131,195},{132,196},{133,197},{134,1... | collective-permute-start | bytes 393224 | tf_op jit(solution)/shard_map/ppermute | solution.py:48
  115.0 2.6 collective-permute-start.34
  116.9 1.4 collective-permute-start.20
  117.6 1.4 collective-permute-start.35
  118.3 2.0 collective-permute-start.21
  119.0 37.8 %collective-permute-start.36 = (bf16[2,64,512]{2,1,0:T(8,128)(2,1)S(1)}, bf16[2,64,512]{2,1,0:T(8,128)(2,1)S(1)}, u32[]{:S(2)}, u32[]{:S(2)}) collective-permute-start(bf16[2,64,512]{2,1,0:T(8,128)(2,1)S(1)} %get-tuple-element.184), channel_id=1, source_target_pairs={{64,0},{65,1},{66,2},{67,3},{68,4},{69,5},{70,6},{71,7},{72,8},{73... | collective-permute-start | bytes 393224 | tf_op jit(solution)/shard_map/ppermute | solution.py:48
  120.3 37.8 %collective-permute-start.22 = (bf16[2,64,512]{2,1,0:T(8,128)(2,1)S(1)}, bf16[2,64,512]{2,1,0:T(8,128)(2,1)S(1)}, u32[]{:S(2)}, u32[]{:S(2)}) collective-permute-start(bf16[2,64,512]{2,1,0:T(8,128)(2,1)S(1)} %get-tuple-element.141), channel_id=1, source_target_pairs={{64,0},{65,1},{66,2},{67,3},{68,4},{69,5},{70,6},{71,7},{72,8},{73... | collective-permute-start | bytes 393224 | tf_op jit(solution)/shard_map/ppermute | solution.py:48
  156.7 2.1 collective-permute-start.37
  158.1 1.4 collective-permute-start.23
  158.8 1.4 collective-permute-start.38
  159.5 1.4 collective-permute-start.24
  160.2 1.6 collective-permute-start.39
  161.2 2.0 collective-permute-start.25
  161.9 43.1 %collective-permute-start.40 = (bf16[2,64,512]{2,1,0:T(8,128)(2,1)S(1)}, bf16[2,64,512]{2,1,0:T(8,128)(2,1)S(1)}, u32[]{:S(2)}, u32[]{:S(2)}) collective-permute-start(bf16[2,64,512]{2,1,0:T(8,128)(2,1)S(1)} %get-tuple-element.200), channel_id=1, source_target_pairs={{64,0},{65,1},{66,2},{67,3},{68,4},{69,5},{70,6},{71,7},{72,8},{73... | collective-permute-start | bytes 393224 | tf_op jit(solution)/shard_map/ppermute | solution.py:48
  163.2 44.7 %collective-permute-start.26 = (bf16[2,64,512]{2,1,0:T(8,128)(2,1)S(1)}, bf16[2,64,512]{2,1,0:T(8,128)(2,1)S(1)}, u32[]{:S(2)}, u32[]{:S(2)}) collective-permute-start(bf16[2,64,512]{2,1,0:T(8,128)(2,1)S(1)} %get-tuple-element.156), channel_id=1, source_target_pairs={{64,0},{65,1},{66,2},{67,3},{68,4},{69,5},{70,6},{71,7},{72,8},{73... | collective-permute-start | bytes 393224 | tf_op jit(solution)/shard_map/ppermute | solution.py:48
  209.6 4.6 %collective-permute-start.41 = (bf16[256,2048]{1,0:T(8,128)(2,1)S(1)}, bf16[256,2048]{1,0:T(8,128)(2,1)S(1)}, u32[]{:S(2)}, u32[]{:S(2)}) collective-permute-start(bf16[256,2048]{1,0:T(8,128)(2,1)S(1)} %get-tuple-element.212), channel_id=1, source_target_pairs={{0,1},{1,0},{2,3},{3,2},{4,5},{5,4},{6,7},{7,6},{8,9},{9,8},{10,11... | collective-permute-start | bytes 3145736 | tf_op jit(solution)/shard_map/ppermute | solution.py:48
  233.4 23.4 %all-to-all-start.1 = ((bf16[8,8,2048]{2,1,0:T(8,128)(2,1)}), bf16[8,8,2048]{2,1,0:T(8,128)(2,1)S(1)}, u32[]{:S(2)}, u32[]{:S(2)}) async-start(bf16[8,8,2048]{2,1,0:T(8,128)(2,1)} %bitcast.10), calls=%async_computation.1 | async-start | bytes 524288 | tf_op jit(solution)/shard_map/all_to_all | solution.py:517
  (6 other events, 14.2 us)
where the time goes:
time: 259 us; the launch traced here: 257 us
  waiting for transfers between devices  108 us (42%)
  starting transfers between devices  87.1 us (34%)
  Pallas kernels  30.1 us (12%)
  blocking collectives  18.1 us (7%)
  other arithmetic  10.1 us (4%)
  local copies, waits for them, and re-layouts  2.95 us (1%)
    ppermute x42, waiting for transfers between devices, routed(): return lax.ppermute(value, NAMES, pairs)  92.5 us
    ppermute x42, starting transfers between devices, routed(): return lax.ppermute(value, NAMES, pairs)  79.3 us
    all_to_all x1, blocking collectives, shards(): lax.all_to_all(summed.reshape(4, 64, HIDDEN), 'y', 0, 0, tiled=True)  18.1 us
    pallas_call x14, Pallas kernels, forward_call(): pl.pallas_call(functools.partial(forward_kernel, tick), out_shape=[PAIR,...  17.2 us
    all_to_all x1, waiting for transfers between devices, shards(): lax.all_to_all(summed.reshape(8, 8, HIDDEN), ('b1', 'b2', 'b4'), 0, 0, ti...  15.5 us
    all_to_all x1, starting transfers between devices, shards(): lax.all_to_all(summed.reshape(8, 8, HIDDEN), ('b1', 'b2', 'b4'), 0, 0, ti...  7.82 us
  transfers between devices with their start and end apart: 43, of which 13 were waited for; matrix products, arithmetic and copies ran while one was open for 3% of the time, Pallas kernels for 10%

commit v1 on v0

--- a/solution.py
+++ b/solution.py
@@ -17,6 +17,8 @@
 SIZES = (2, 4, 2, 2, 2, 4, 2)
 SECTION = ("zh", "x")
 DP = ("b4", "b2", "b1", "y", "c")
+PLACES = 6
+SECTION_AT = 5
 LAYERS = 8
 FEATURES = 512
 HIDDEN = 2048
@@ -98,43 +100,59 @@
     return route
 
 
-def merged(own, other, bit):
-    first = bit == 0
-    return jnp.concatenate([jnp.where(first, own, other), jnp.where(first, other, own)], axis=0)
-
-
-def merged_outer(own, other):
-    y = lax.axis_index("y")
-    outer = (y == 0) | (y == 3)
-    rows = own.shape[0] // 2
-    own_a, own_b, oth_a, oth_b = own[:rows], own[rows:], other[:rows], other[rows:]
-    return jnp.concatenate(
-        [
-            jnp.where(outer, own_a, oth_a),
-            jnp.where(outer, oth_a, own_a),
-            jnp.where(outer, oth_b, own_b),
-            jnp.where(outer, own_b, oth_b),
-        ],
-        axis=0,
-    )
-
-
-def gathered(block, even_first, beside=None):
-    results = ()
-    block = merged(block, routed(block, swap_b4), lax.axis_index("b4"))
-    block = merged(block, routed(block, swap_b2), lax.axis_index("b2"))
-    block = merged(block, routed(block, swap_b1), lax.axis_index("b1"))
-    y = lax.axis_index("y")
-    if even_first:
-        if beside is not None:
-            block, results = beside(block)
-        block = merged(block, routed(block, swap_even), y % 2)
-        block, *results = lax.optimization_barrier((block, *results))
-        block = merged(block, routed(block, swap_odd), y // 2)
-    else:
-        block = merged(block, routed(block, swap_odd), y // 2)
-        block = merged_outer(block, routed(block, swap_even))
-    return block, routed(block, swap_core), *results
+def doubled(block, route):
+    return jnp.concatenate([block, routed(block, route)], axis=0)
+
+
+def gathered(block, even_first):
+    for route in (swap_b4, swap_b2, swap_b1) + ((swap_even, swap_odd) if even_first else (swap_odd, swap_even)):
+        block = doubled(block, route)
+    return block, routed(block, swap_core)
+
+
+def natural_block(place, b4, b2, b1, y, c):
+    z = (b4 ^ place[0]) * 4 + (b2 ^ place[1]) * 2 + (b1 ^ place[2])
+    return z * 8 + (y ^ place[3]) * 2 + (c ^ place[4])
+
+
+def settled_kernel(place_in, block_in, place, block):
+    for index in range(PLACES):
+        place[index] = place_in[index]
+    block[...] = block_in[...]
+
+
+def settled_call(place, block):
+    return pl.pallas_call(
+        settled_kernel,
+        out_shape=[
+            jax.ShapeDtypeStruct(place.shape, place.dtype),
+            jax.ShapeDtypeStruct(block.shape, block.dtype),
+        ],
+        in_specs=[SMEM, WHOLE],
+        out_specs=[SMEM, WHOLE],
+        compiler_params=PARAMS,
+        name="settled",
+    )(place, block)
+
+
+def placed_kernel(place, own_out, other_out, full_out):
+    rows = HIDDEN // 64
+    for core, half in enumerate((own_out, other_out)):
+        for index in range(32):
+            odd, even = index // 8 % 2, index // 16
+            there = natural_block(place, index % 2, index // 2 % 2, index // 4 % 2, even ^ (odd * 3), core)
+            full_out[pl.ds(pl.multiple_of(there * rows, rows), rows), :] = half[index * rows : (index + 1) * rows, :]
+
+
+def placed_call(place, own_out, other_out):
+    return pl.pallas_call(
+        placed_kernel,
+        out_shape=jax.ShapeDtypeStruct((HIDDEN, FEATURES), jnp.bfloat16),
+        in_specs=[SMEM] + [WHOLE] * 2,
+        out_specs=WHOLE,
+        compiler_params=PARAMS,
+        name="placed_w_out",
+    )(place, own_out, other_out)
 
 
 def row_mean(values):
@@ -145,17 +163,22 @@
     return pl.ds(pl.multiple_of(chunk * CHUNK, CHUNK), CHUNK)
 
 
-def opening_kernel(this_core, inputs, probe, order, lhs, preact_t):
-    position = lax.broadcasted_iota(jnp.int32, (FEATURES, FEATURES), 1)
+def one_hot(natural_row):
     natural = lax.broadcasted_iota(jnp.int32, (FEATURES, FEATURES), 0)
-    core, y = (position // 256) ^ this_core[0], (position // 64) % 4
-    b1, b2, b4, row = (position // 32) % 2, (position // 16) % 2, (position // 8) % 2, position % 8
-    at = (b4 * 4 + b2 * 2 + b1) * 64 + y * 16 + core * 8 + row
-    order[...] = jnp.where(natural == at, 1.0, 0.0).astype(jnp.bfloat16)
+    return jnp.where(natural == natural_row, 1.0, 0.0).astype(jnp.bfloat16)
+
+
+def opening_kernel(place, inputs, probe, order, curvature_order, normed_out, preact_t):
+    at = lax.broadcasted_iota(jnp.int32, (FEATURES, FEATURES), 1)
+    row, b4, b2, b1 = at % 8, (at // 8) % 2, (at // 16) % 2, (at // 32) % 2
+    even, odd, core = (at // 64) % 2, (at // 128) % 2, at // 256
+    order[...] = one_hot(natural_block(place, b4, b2, b1, even ^ (odd * 3), core) * 8 + row)
+    block = (b4 * 4 + b2 * 2 + b1) * 8 + ((at // 64) % 4) * 2 + (core ^ place[4])
+    curvature_order[...] = one_hot(block * 8 + row)
     inflow = inputs[...].astype(jnp.float32)
     centred = inflow - row_mean(inflow)
     normed = (centred * lax.rsqrt(row_mean(centred * centred) + EPSILON)).astype(jnp.bfloat16)
-    lhs[...] = jnp.dot(normed, order[...], preferred_element_type=jnp.float32).astype(jnp.bfloat16)
+    normed_out[...] = normed
 
     def step(chunk, carry):
         preact_t[:, columns(chunk)] = jnp.dot(normed, probe[:, columns(chunk)], preferred_element_type=jnp.float32)
@@ -164,20 +187,22 @@
     lax.fori_loop(0, CHUNKS, step, 0)
 
 
-def opening_call(core, inputs, probe):
+def opening_call(place, inputs, probe):
     rows = inputs.shape[0]
+    order = jax.ShapeDtypeStruct((FEATURES, FEATURES), jnp.bfloat16)
     return pl.pallas_call(
         opening_kernel,
         out_shape=[
-            jax.ShapeDtypeStruct((FEATURES, FEATURES), jnp.bfloat16),
+            order,
+            order,
             jax.ShapeDtypeStruct((rows, FEATURES), jnp.bfloat16),
             jax.ShapeDtypeStruct((rows, HIDDEN), jnp.float32),
         ],
         in_specs=[SMEM] + [WHOLE] * 2,
-        out_specs=[WHOLE] * 3,
+        out_specs=[WHOLE] * 4,
         compiler_params=PARAMS,
         name="opening",
-    )(core, inputs, probe)
+    )(place, inputs, probe)
 
 
 def gelu_slopes(preact, preact_t, slope_out, chunk):
@@ -195,16 +220,17 @@
     )
 
 
-def first_kernel(micro, section, inputs, opening_lhs, opening_t, own_in, other_in, w_out, pair_out, slope_out, acc):
+def first_kernel(micro, place, inputs, opening_n, opening_t, order, own_in, other_in, w_out, pair_out, slope_out, lhs, acc):
     rows = slice(micro * ROWS, (micro + 1) * ROWS)
 
-    @pl.when(section[0] == 0)
+    @pl.when(place[SECTION_AT] == 0)
     def _():
+        lhs[...] = jnp.dot(opening_n[rows], order[...], preferred_element_type=jnp.float32).astype(jnp.bfloat16)
         acc[:ROWS] = inputs[rows].astype(jnp.float32)
         acc[ROWS:] = jnp.zeros((ROWS, FEATURES), jnp.float32)
 
         def step(chunk, carry):
-            preact = halves_product(opening_lhs[rows], own_in, other_in, columns(chunk))
+            preact = halves_product(lhs[...], own_in, other_in, columns(chunk))
             hidden = gelu_slopes(preact, opening_t[rows, columns(chunk)], slope_out, chunk)
             acc[...] += jnp.dot(hidden, w_out[columns(chunk), :], preferred_element_type=jnp.float32)
             return carry
@@ -216,13 +242,13 @@
 
 def forward_kernel(tick, *refs):
     last = tick == LAYERS - 1
-    section, pair, own_in, other_in, probe, w_out, order = refs[:7]
+    place, pair, own_in, other_in, probe, w_out, order = refs[:7]
     refs = refs[7:]
     if last:
         goal, refs = refs[0], refs[1:]
     pair_out, norm, stat, slope_out, natural, lhs, acc = refs
 
-    @pl.when(section[0] == tick)
+    @pl.when(place[SECTION_AT] == tick)
     def _():
         inflow = pair[0].astype(jnp.float32)
         inflow_t = pair[1].astype(jnp.float32)
@@ -267,20 +293,23 @@
 PARAMS = pltpu.CompilerParams(vmem_limit_bytes=VMEM_BYTES)
 
 
-def first_call(micro, section, inputs, opening_lhs, opening_t, own_in, other_in, w_out):
+def first_call(micro, place, inputs, opening_n, opening_t, order, own_in, other_in, w_out):
     return pl.pallas_call(
         functools.partial(first_kernel, micro),
         out_shape=[PAIR, SLOPE],
-        in_specs=[SMEM] + [WHOLE] * 6,
+        in_specs=[SMEM] + [WHOLE] * 7,
         out_specs=[WHOLE] * 2,
-        scratch_shapes=[pltpu.VMEM((2 * ROWS, FEATURES), jnp.float32)],
+        scratch_shapes=[
+            pltpu.VMEM((ROWS, FEATURES), jnp.bfloat16),
+            pltpu.VMEM((2 * ROWS, FEATURES), jnp.float32),
+        ],
         compiler_params=PARAMS,
         name="layer_up_0",
-    )(section, inputs, opening_lhs, opening_t, own_in, other_in, w_out)
-
-
-def forward_call(tick, section, pair, own_in, other_in, probe, w_out, order, goal):
-    operands = [section, pair, own_in, other_in, probe, w_out, order] + ([goal] if tick == LAYERS - 1 else [])
+    )(place, inputs, opening_n, opening_t, order, own_in, other_in, w_out)
+
+
+def forward_call(tick, place, pair, own_in, other_in, probe, w_out, order, goal):
+    operands = [place, pair, own_in, other_in, probe, w_out, order] + ([goal] if tick == LAYERS - 1 else [])
     return pl.pallas_call(
         functools.partial(forward_kernel, tick),
         out_shape=[PAIR, NORM, STAT, SLOPE],
@@ -340,10 +369,10 @@
 
 
 def backward_kernel(tick, *refs):
-    section, pair, w_in_t, probe_t, w_out_t, norm, stat, slope = refs[:8]
+    place, pair, w_in_t, probe_t, w_out_t, norm, stat, slope = refs[:8]
     pair_out, grads, acc, acc_t = refs[8:]
 
-    @pl.when(section[0] == LAYERS - 1 - tick)
+    @pl.when(place[SECTION_AT] == LAYERS - 1 - tick)
     def _():
         acc[...] = jnp.zeros_like(acc)
         acc_t[...] = jnp.zeros_like(acc_t)
@@ -371,8 +400,8 @@
         pair_out[1] = (pair[1].astype(jnp.float32) + through_t).astype(jnp.bfloat16)
 
 
-def backward_call(tick, section, pair, w_in_t, probe_t, w_out_t, kept):
-    operands = [section, pair, w_in_t, probe_t, w_out_t, *kept]
+def backward_call(tick, place, pair, w_in_t, probe_t, w_out_t, kept):
+    operands = [place, pair, w_in_t, probe_t, w_out_t, *kept]
     return pl.pallas_call(
         functools.partial(backward_kernel, tick),
         out_shape=[PAIR, GRADS],
@@ -391,10 +420,11 @@
 OTHER_HALF = slice(FEATURES // 2, FEATURES)
 
 
-def curvature_operands(micro, section, pair, w_out_t, slope, order, opening_lhs, norms, grads, lhs, rhs):
-    @pl.when(section[0] == 0)
+def curvature_operands(micro, place, pair, w_out_t, slope, order, opening_n, norms, grads, lhs, rhs):
+    @pl.when(place[SECTION_AT] == 0)
     def _():
-        lhs[:ROWS] = opening_lhs[micro * ROWS : (micro + 1) * ROWS]
+        rows = slice(micro * ROWS, (micro + 1) * ROWS)
+        lhs[:ROWS] = jnp.dot(opening_n[rows], order[...], preferred_element_type=jnp.float32).astype(jnp.bfloat16)
         lhs[ROWS:] = jnp.zeros((ROWS, FEATURES), jnp.bfloat16)
 
         def bottom(chunk, carry):
@@ -406,7 +436,7 @@
 
     for layer in range(1, LAYERS):
 
-        @pl.when(section[0] == layer)
+        @pl.when(place[SECTION_AT] == layer)
         def _():
             both = norms[layer - 1][...].reshape(2 * ROWS, FEATURES).astype(jnp.bfloat16)
             lhs[...] = jnp.dot(both, order[...], preferred_element_type=jnp.float32).astype(jnp.bfloat16)
@@ -414,13 +444,13 @@
 
 
 def curvature_kernel(micro, final, *refs):
-    section, pair, w_out_t, slope, order, opening_lhs = refs[:6]
+    place, pair, w_out_t, slope, order, opening_n = refs[:6]
     norms, refs = refs[6 : 5 + LAYERS], refs[5 + LAYERS :]
     grads, refs = refs[: LAYERS - 1], refs[LAYERS - 1 :]
     if final:
         away_in, stay_in, refs = refs[0], refs[1], refs[2:]
     away, stay, lhs, rhs = refs
-    curvature_operands(micro, section, pair, w_out_t, slope, order, opening_lhs, norms, grads, lhs, rhs)
+    curvature_operands(micro, place, pair, w_out_t, slope, order, opening_n, norms, grads, lhs, rhs)
 
     def step(chunk, carry):
         now = columns(chunk)
@@ -439,10 +469,10 @@
     lax.fori_loop(0, CHUNKS, step, 0, unroll=UNROLL)
 
 
-def curvature_call(micro, section, pair, w_out_t, slope, order, opening_lhs, norms, grads, sums):
+def curvature_call(micro, place, pair, w_out_t, slope, order, opening_n, norms, grads, sums):
     half = (FEATURES // 2, HIDDEN)
     final = bool(sums)
-    operands = [section, pair, w_out_t, slope, order, opening_lhs, *norms, *grads, *sums]
+    operands = [place, pair, w_out_t, slope, order, opening_n, *norms, *grads, *sums]
     return pl.pallas_call(
         functools.partial(curvature_kernel, micro, final),
         out_shape=[
@@ -461,19 +491,12 @@
 
 
 def shards(inputs, targets, w_in, w_out, probes):
-    section = jnp.reshape(lax.axis_index(SECTION), (1,)).astype(jnp.int32)
-    core = jnp.reshape(lax.axis_index("c"), (1,)).astype(jnp.int32)
+    place = jnp.stack([lax.axis_index(name) for name in (*DP, SECTION)]).astype(jnp.int32)
+    place, out_block = settled_call(place, w_out[0])
     probe = probes[0]
-
-    def opening(block):
-        block, inputs_now = lax.optimization_barrier((block, inputs))
-        return block, opening_call(core, inputs_now, probe)
-
-    own_in, other_in, order, opening_lhs, opening_t = gathered(w_in[0], True, opening)
-    full_out = merged(*gathered(w_out[0], False), lax.axis_index("c"))
-    full_out = (
-        full_out.reshape(2, 4, 2, 2, 2, 32, FEATURES).transpose(4, 3, 2, 1, 0, 5, 6).reshape(HIDDEN, FEATURES)
-    )
+    own_in, other_in = gathered(w_in[0], True)
+    full_out = placed_call(place, *gathered(out_block, False))
+    order, curvature_order, opening_n, opening_t = opening_call(place, inputs, probe)
     goal = routed(targets, goal_route)
     pairs, slopes, kept, grads = [None] * MICRO, [], [], []
     for micro in range(MICRO):
@@ -483,13 +506,13 @@
         for micro in range(MICRO):
             if tick == 0:
                 pairs[micro], slope = first_call(
-                    micro, section, inputs, opening_lhs, opening_t, own_in, other_in, full_out
+                    micro, place, inputs, opening_n, opening_t, order, own_in, other_in, full_out
                 )
                 slopes.append(slope)
             else:
                 goal_now = goal[micro * ROWS : (micro + 1) * ROWS]
                 pairs[micro], *stores = forward_call(
-                    tick, section, pairs[micro], own_in, other_in, probe, full_out, order, goal_now
+                    tick, place, pairs[micro], own_in, other_in, probe, full_out, order, goal_now
                 )
                 kept[micro].append(stores)
             if tick < LAYERS - 1:
@@ -499,7 +522,7 @@
     for tick in range(LAYERS - 1):
         for micro in range(MICRO):
             pairs[micro], low_grads = backward_call(
-                tick, section, pairs[micro], *turned, kept[micro][LAYERS - 2 - tick]
+                tick, place, pairs[micro], *turned, kept[micro][LAYERS - 2 - tick]
             )
             grads[micro].append(low_grads)
             pairs[micro] = routed(pairs[micro], down_from(LAYERS - 1 - tick))
@@ -507,7 +530,7 @@
     for micro in range(MICRO):
         norms = [stores[0] for stores in kept[micro]]
         sums = curvature_call(
-            micro, section, pairs[micro], turned[2], slopes[micro], order, opening_lhs, norms, grads[micro], sums
+            micro, place, pairs[micro], turned[2], slopes[micro], curvature_order, opening_n, norms, grads[micro], sums
         )
     away, stay = sums
     other = routed(away, swap_core)

time: 259 us -> 255 us (0.985)
  other arithmetic: 10.1 us -> 3.5 us
  waiting for transfers between devices: 108 us -> 113 us
    pallas_call x14, Pallas kernels: 17.2 us -> 7.89 us  [forward_call(): pl.pallas_call(functools.partial(forward_kernel, tick), out_shape=[PAIR,...]
    pallas_call x14, Pallas kernels: 0.33 us -> 7.93 us  [backward_call(): pl.pallas_call(functools.partial(backward_kernel, tick), out_shape=[PAIR,...]
    select_n x11 -> x0, other arithmetic: 5.93 us -> none  [the longest x10 4.83 us: merged(): jnp.where(first, own, other)]
    ppermute x42, waiting for transfers between devices: 92.5 us -> 97.8 us  [routed(): return lax.ppermute(value, NAMES, pairs)]
    all_to_all x1, starting transfers between devices: 7.82 us -> 4.97 us  [shards(): lax.all_to_all(summed.reshape(8, 8, HIDDEN), ('b1', 'b2', 'b4'), 0, 0, ti...]
    pallas_call x1 -> x3, Pallas kernels: 1.01 us -> 3.66 us  [the longest x1 1.81 us: opening_call(): pl.pallas_call(opening_kernel, out_shape=[order, order, jax.ShapeDtypeStr...]
  transfers between devices with their start and end apart: 43 -> 43, of which waited for: 13 -> 16; matrix products, arithmetic and copies ran while one was open for 3% -> 1% of each run, Pallas kernels for 10% -> 10%
where the time goes in v1:
time: 255 us; the launch traced here: 254 us
  waiting for transfers between devices  113 us (44%)
  starting transfers between devices  85.1 us (33%)
  Pallas kernels  30.2 us (12%)
  blocking collectives  19.1 us (7%)
  other arithmetic  3.5 us (1%)
    ppermute x42, waiting for transfers between devices, routed(): return lax.ppermute(value, NAMES, pairs)  97.8 us
    ppermute x42, starting transfers between devices, routed(): return lax.ppermute(value, NAMES, pairs)  80.1 us
    all_to_all x1, blocking collectives, shards(): lax.all_to_all(summed.reshape(4, 64, HIDDEN), 'y', 0, 0, tiled=True)  19.1 us
    all_to_all x1, waiting for transfers between devices, shards(): lax.all_to_all(summed.reshape(8, 8, HIDDEN), ('b1', 'b2', 'b4'), 0, 0, ti...  15.5 us
    pallas_call x14, Pallas kernels, backward_call(): pl.pallas_call(functools.partial(backward_kernel, tick), out_shape=[PAIR,...  7.93 us
    pallas_call x14, Pallas kernels, forward_call(): pl.pallas_call(functools.partial(forward_kernel, tick), out_shape=[PAIR,...  7.89 us
  transfers between devices with their start and end apart: 43, of which 16 were waited for; matrix products, arithmetic and copies ran while one was open for 1% of the time, Pallas kernels for 10%

profile of v1, /device:TPU:8, one launch (start us, length us, event | category | flops | bytes accessed | tf_op | source)
XLA Modules:
  0.0 254.2 jit_solution(6379546052291187631)
XLA Ops:
  0.1 0.8 copy-done.2
  0.8 1.1 settled.1
  2.0 9.1 %collective-permute-start.6 = (bf16[32,512]{1,0:T(8,128)(2,1)S(1)}, bf16[32,512]{1,0:T(8,128)(2,1)S(1)}, u32[]{:S(2)}, u32[]{:S(2)}) collective-permute-start(bf16[32,512]{1,0:T(8,128)(2,1)S(1)} %get-tuple-element.110), channel_id=1, source_target_pairs={{0,32},{1,33},{2,34},{3,35},{4,36},{5,37},{6,38},{7,39},{8,40},{9,... | collective-permute-start | bytes 98312 | tf_op jit(solution)/shard_map/ppermute | solution.py:50
  11.1 1.9 collective-permute-start
  13.0 0.8 constant_dynamic-update-slice_fusion.4
  13.8 5.2 %collective-permute-start.7 = (bf16[64,512]{1,0:T(8,128)(2,1)S(1)}, bf16[64,512]{1,0:T(8,128)(2,1)S(1)}, u32[]{:S(2)}, u32[]{:S(2)}) collective-permute-start(bf16[64,512]{1,0:T(8,128)(2,1)S(1)} %pad_maximum_fusion.5), channel_id=1, source_target_pairs={{0,16},{1,17},{2,18},{3,19},{4,20},{5,21},{6,22},{7,23},{8,24},{9,... | collective-permute-start | bytes 196616 | tf_op jit(solution)/shard_map/ppermute | solution.py:50
  19.0 2.4 collective-permute-done
  21.4 0.8 pad_maximum_fusion.4
  22.2 5.2 %collective-permute-start.1 = (bf16[16,2048]{1,0:T(8,128)(2,1)S(1)}, bf16[16,2048]{1,0:T(8,128)(2,1)S(1)}, u32[]{:S(2)}, u32[]{:S(2)}) collective-permute-start(bf16[16,2048]{1,0:T(8,128)(2,1)S(1)} %pad_maximum_fusion.4), channel_id=1, source_target_pairs={{0,16},{1,17},{2,18},{3,19},{4,20},{5,21},{6,22},{7,23},{8,24},{9,... | collective-permute-start | bytes 196616 | tf_op jit(solution)/shard_map/ppermute | solution.py:50
  27.4 3.5 %collective-permute-start.8 = (bf16[128,512]{1,0:T(8,128)(2,1)S(1)}, bf16[128,512]{1,0:T(8,128)(2,1)S(1)}, u32[]{:S(2)}, u32[]{:S(2)}) collective-permute-start(bf16[128,512]{1,0:T(8,128)(2,1)S(1)} %pad_maximum_fusion.3), channel_id=1, source_target_pairs={{0,8},{1,9},{2,10},{3,11},{4,12},{5,13},{6,14},{7,15},{8,0},{9,1},... | collective-permute-start | bytes 393224 | tf_op jit(solution)/shard_map/ppermute | solution.py:50
  31.0 0.8 pad_maximum_fusion.2
  31.7 2.8 %collective-permute-start.2 = (bf16[32,2048]{1,0:T(8,128)(2,1)S(1)}, bf16[32,2048]{1,0:T(8,128)(2,1)S(1)}, u32[]{:S(2)}, u32[]{:S(2)}) collective-permute-start(bf16[32,2048]{1,0:T(8,128)(2,1)S(1)} %pad_maximum_fusion.2), channel_id=1, source_target_pairs={{0,8},{1,9},{2,10},{3,11},{4,12},{5,13},{6,14},{7,15},{8,0},{9,1},... | collective-permute-start | bytes 393224 | tf_op jit(solution)/shard_map/ppermute | solution.py:50
  34.6 3.5 %collective-permute-start.9 = (bf16[256,512]{1,0:T(8,128)(2,1)S(1)}, bf16[256,512]{1,0:T(8,128)(2,1)S(1)}, u32[]{:S(2)}, u32[]{:S(2)}) collective-permute-start(bf16[256,512]{1,0:T(8,128)(2,1)S(1)} %pad_maximum_fusion.1), channel_id=1, source_target_pairs={{0,6},{1,7},{2,4},{3,5},{4,2},{5,3},{6,0},{7,1},{8,14},{9,15},{10,... | collective-permute-start | bytes 786440 | tf_op jit(solution)/shard_map/ppermute | solution.py:50
  38.6 3.3 %collective-permute-start.3 = (bf16[64,2048]{1,0:T(8,128)(2,1)S(1)}, bf16[64,2048]{1,0:T(8,128)(2,1)S(1)}, u32[]{:S(2)}, u32[]{:S(2)}) collective-permute-start(bf16[64,2048]{1,0:T(8,128)(2,1)S(1)} %pad_maximum_fusion), channel_id=1, source_target_pairs={{0,2},{1,3},{2,0},{3,1},{4,6},{5,7},{6,4},{7,5},{8,10},{9,11},{10,... | collective-permute-start | bytes 786440 | tf_op jit(solution)/shard_map/ppermute | solution.py:50
  42.1 0.8 collective-permute-done.9
  43.0 3.6 %collective-permute-start.10 = (bf16[512,512]{1,0:T(8,128)(2,1)S(1)}, bf16[512,512]{1,0:T(8,128)(2,1)S(1)}, u32[]{:S(2)}, u32[]{:S(2)}) collective-permute-start(bf16[512,512]{1,0:T(8,128)(2,1)S(1)} %get-tuple-element.207), channel_id=1, source_target_pairs={{0,2},{1,3},{2,0},{3,1},{4,6},{5,7},{6,4},{7,5},{8,10},{9,11},{10,... | collective-permute-start | bytes 1572872 | tf_op jit(solution)/shard_map/ppermute | solution.py:50
  46.5 3.1 %collective-permute-done.3 = bf16[64,2048]{1,0:T(8,128)(2,1)S(1)} collective-permute-done((bf16[64,2048]{1,0:T(8,128)(2,1)S(1)}, bf16[64,2048]{1,0:T(8,128)(2,1)S(1)}, u32[]{:S(2)}, u32[]{:S(2)}) %collective-permute-start.3) | collective-permute-done | bytes 262176 | tf_op jit(solution)/shard_map/ppermute | solution.py:50
  49.7 3.5 %collective-permute-start.4 = (bf16[128,2048]{1,0:T(8,128)(2,1)S(1)}, bf16[128,2048]{1,0:T(8,128)(2,1)S(1)}, u32[]{:S(2)}, u32[]{:S(2)}) collective-permute-start(bf16[128,2048]{1,0:T(8,128)(2,1)S(1)} %get-tuple-element.209), channel_id=1, source_target_pairs={{0,6},{1,7},{2,4},{3,5},{4,2},{5,3},{6,0},{7,1},{8,14},{9,15},{10,... | collective-permute-start | bytes 1572872 | tf_op jit(solution)/shard_map/ppermute | solution.py:50
  53.2 4.2 %collective-permute-done.10 = bf16[512,512]{1,0:T(8,128)(2,1)S(1)} collective-permute-done((bf16[512,512]{1,0:T(8,128)(2,1)S(1)}, bf16[512,512]{1,0:T(8,128)(2,1)S(1)}, u32[]{:S(2)}, u32[]{:S(2)}) %collective-permute-start.10) | collective-permute-done | bytes 524320 | tf_op jit(solution)/shard_map/ppermute | solution.py:50
  57.5 1.9 collective-permute-start.11
  59.4 1.4 collective-permute-done.4
  60.8 1.9 collective-permute-start.5
  62.8 1.8 opening.1
  65.4 2.0 layer_up_0.3
  67.4 2.0 collective-permute-start.27
  69.4 2.0 layer_up_0.2
  71.3 1.3 collective-permute-start.12
  73.9 2.1 collective-permute-done.12.refs_1_
  82.8 8.8 %collective-permute-start.31 = (bf16[2,64,512]{2,1,0:T(8,128)(2,1)S(1)}, bf16[2,64,512]{2,1,0:T(8,128)(2,1)S(1)}, u32[]{:S(2)}, u32[]{:S(2)}) collective-permute-start(bf16[2,64,512]{2,1,0:T(8,128)(2,1)S(1)} %get-tuple-element.163), channel_id=1, source_target_pairs={{0,64},{1,65},{2,66},{3,67},{4,68},{5,69},{6,70},{7,71},{8,72},{9,... | collective-permute-start | bytes 393224 | tf_op jit(solution)/shard_map/ppermute | solution.py:50
  92.2 1.3 collective-permute-start.16
  93.5 2.0 collective-permute-done.31.refs_1_
  96.0 0.8 collective-permute-start.32
  101.5 2.0 turned_weights.1
  110.2 1.3 collective-permute-start.36
  112.1 1.3 collective-permute-start.22
  113.4 35.5 %collective-permute-done.36.refs_1_ = bf16[2,64,512]{2,1,0:T(8,128)(2,1)S(1)} collective-permute-done((bf16[2,64,512]{2,1,0:T(8,128)(2,1)S(1)}, bf16[2,64,512]{2,1,0:T(8,128)(2,1)S(1)}, u32[]{:S(2)}, u32[]{:S(2)}) %collective-permute-start.36) | collective-permute-done | bytes 131104 | tf_op jit(solution)/shard_map/ppermute | solution.py:50
  155.5 0.8 layer_down_5.2
  157.5 1.3 collective-permute-start.40
  159.4 1.3 collective-permute-start.26
  160.7 42.6 %collective-permute-done.40.refs_1_ = bf16[2,64,512]{2,1,0:T(8,128)(2,1)S(1)} collective-permute-done((bf16[2,64,512]{2,1,0:T(8,128)(2,1)S(1)}, bf16[2,64,512]{2,1,0:T(8,128)(2,1)S(1)}, u32[]{:S(2)}, u32[]{:S(2)}) %collective-permute-start.40) | collective-permute-done | bytes 131104 | tf_op jit(solution)/shard_map/ppermute | solution.py:50
  203.3 2.4 curvature_first.1
  205.7 2.4 curvature_last.1
  208.1 1.9 collective-permute-start.41
  210.0 2.6 %collective-permute-done.41 = bf16[256,2048]{1,0:T(8,128)(2,1)S(1)} collective-permute-done((bf16[256,2048]{1,0:T(8,128)(2,1)S(1)}, bf16[256,2048]{1,0:T(8,128)(2,1)S(1)}, u32[]{:S(2)}, u32[]{:S(2)}) %collective-permute-start.41) | collective-permute-done | bytes 1048608 | tf_op jit(solution)/shard_map/ppermute | solution.py:50
  212.9 19.1 %all_to_all.10 = bf16[4,64,2048]{2,1,0:T(8,128)(2,1)S(1)} all-to-all(bf16[4,64,2048]{2,1,0:T(8,128)(2,1)S(1)} %bitcast.32), channel_id=1, replica_groups=mesh['zh'=2,'x'=4,'b4'=2,'b2'=2,'b1'=2,'y'=4,'c'=2] {'y'}, dimensions={0} | all-to-all | bytes 2097152 | tf_op jit(solution)/shard_map/all_to_all | solution.py:538
  232.0 0.9 reduce_sum.23
  233.0 5.0 %all-to-all-start.1 = ((bf16[8,8,2048]{2,1,0:T(8,128)(2,1)}), bf16[8,8,2048]{2,1,0:T(8,128)(2,1)S(1)}, u32[]{:S(2)}, u32[]{:S(2)}) async-start(bf16[8,8,2048]{2,1,0:T(8,128)(2,1)} %bitcast.10), calls=%async_computation.1 | async-start | bytes 524288 | tf_op jit(solution)/shard_map/all_to_all | solution.py:540
  237.9 15.5 %all-to-all-done.1 = bf16[8,8,2048]{2,1,0:T(8,128)(2,1)S(1)} async-done(((bf16[8,8,2048]{2,1,0:T(8,128)(2,1)}), bf16[8,8,2048]{2,1,0:T(8,128)(2,1)S(1)}, u32[]{:S(2)}, u32[]{:S(2)}) %all-to-all-start.1) | async-done | bytes 262176 | tf_op jit(solution)/shard_map/all_to_all | solution.py:540
  (109 shorter events, 31.6 us)
Async XLA Ops:
  0.0 38.6 %copy-start.3 = (bf16[1,8,2048]{2,1,0:T(8,128)(2,1)S(1)}, bf16[1,8,2048]{2,1,0:T(8,128)(2,1)}, u32[]{:S(2)}) copy-start(bf16[1,8,2048]{2,1,0:T(8,128)(2,1)} %param.7) | copy-start | bytes 98308
  0.1 0.8 copy-start.2
  2.0 11.8 %collective-permute-start.6 = (bf16[32,512]{1,0:T(8,128)(2,1)S(1)}, bf16[32,512]{1,0:T(8,128)(2,1)S(1)}, u32[]{:S(2)}, u32[]{:S(2)}) collective-permute-start(bf16[32,512]{1,0:T(8,128)(2,1)S(1)} %get-tuple-element.110), channel_id=1, source_target_pairs={{0,32},{1,33},{2,34},{3,35},{4,36},{5,37},{6,38},{7,39},{8,40},{9,... | collective-permute-start | bytes 98312 | tf_op jit(solution)/shard_map/ppermute | solution.py:50
  11.1 10.3 %collective-permute-start = (bf16[8,2048]{1,0:T(8,128)(2,1)}, bf16[8,2048]{1,0:T(8,128)(2,1)S(1)}, u32[]{:S(2)}, u32[]{:S(2)}) collective-permute-start(bf16[8,2048]{1,0:T(8,128)(2,1)} %bitcast.33), channel_id=1, source_target_pairs={{0,32},{1,33},{2,34},{3,35},{4,36},{5,37},{6,38},{7,39},{8,40},{9,... | collective-permute-start | bytes 98312 | tf_op jit(solution)/shard_map/ppermute | solution.py:50
  13.8 13.6 %collective-permute-start.7 = (bf16[64,512]{1,0:T(8,128)(2,1)S(1)}, bf16[64,512]{1,0:T(8,128)(2,1)S(1)}, u32[]{:S(2)}, u32[]{:S(2)}) collective-permute-start(bf16[64,512]{1,0:T(8,128)(2,1)S(1)} %pad_maximum_fusion.5), channel_id=1, source_target_pairs={{0,16},{1,17},{2,18},{3,19},{4,20},{5,21},{6,22},{7,23},{8,24},{9,... | collective-permute-start | bytes 196616 | tf_op jit(solution)/shard_map/ppermute | solution.py:50
  22.2 8.8 %collective-permute-start.1 = (bf16[16,2048]{1,0:T(8,128)(2,1)S(1)}, bf16[16,2048]{1,0:T(8,128)(2,1)S(1)}, u32[]{:S(2)}, u32[]{:S(2)}) collective-permute-start(bf16[16,2048]{1,0:T(8,128)(2,1)S(1)} %pad_maximum_fusion.4), channel_id=1, source_target_pairs={{0,16},{1,17},{2,18},{3,19},{4,20},{5,21},{6,22},{7,23},{8,24},{9,... | collective-permute-start | bytes 196616 | tf_op jit(solution)/shard_map/ppermute | solution.py:50
  27.4 7.2 %collective-permute-start.8 = (bf16[128,512]{1,0:T(8,128)(2,1)S(1)}, bf16[128,512]{1,0:T(8,128)(2,1)S(1)}, u32[]{:S(2)}, u32[]{:S(2)}) collective-permute-start(bf16[128,512]{1,0:T(8,128)(2,1)S(1)} %pad_maximum_fusion.3), channel_id=1, source_target_pairs={{0,8},{1,9},{2,10},{3,11},{4,12},{5,13},{6,14},{7,15},{8,0},{9,1},... | collective-permute-start | bytes 393224 | tf_op jit(solution)/shard_map/ppermute | solution.py:50
  31.7 6.9 %collective-permute-start.2 = (bf16[32,2048]{1,0:T(8,128)(2,1)S(1)}, bf16[32,2048]{1,0:T(8,128)(2,1)S(1)}, u32[]{:S(2)}, u32[]{:S(2)}) collective-permute-start(bf16[32,2048]{1,0:T(8,128)(2,1)S(1)} %pad_maximum_fusion.2), channel_id=1, source_target_pairs={{0,8},{1,9},{2,10},{3,11},{4,12},{5,13},{6,14},{7,15},{8,0},{9,1},... | collective-permute-start | bytes 393224 | tf_op jit(solution)/shard_map/ppermute | solution.py:50
  34.6 8.3 %collective-permute-start.9 = (bf16[256,512]{1,0:T(8,128)(2,1)S(1)}, bf16[256,512]{1,0:T(8,128)(2,1)S(1)}, u32[]{:S(2)}, u32[]{:S(2)}) collective-permute-start(bf16[256,512]{1,0:T(8,128)(2,1)S(1)} %pad_maximum_fusion.1), channel_id=1, source_target_pairs={{0,6},{1,7},{2,4},{3,5},{4,2},{5,3},{6,0},{7,1},{8,14},{9,15},{10,... | collective-permute-start | bytes 786440 | tf_op jit(solution)/shard_map/ppermute | solution.py:50
  38.6 11.0 %collective-permute-start.3 = (bf16[64,2048]{1,0:T(8,128)(2,1)S(1)}, bf16[64,2048]{1,0:T(8,128)(2,1)S(1)}, u32[]{:S(2)}, u32[]{:S(2)}) collective-permute-start(bf16[64,2048]{1,0:T(8,128)(2,1)S(1)} %pad_maximum_fusion), channel_id=1, source_target_pairs={{0,2},{1,3},{2,0},{3,1},{4,6},{5,7},{6,4},{7,5},{8,10},{9,11},{10,... | collective-permute-start | bytes 786440 | tf_op jit(solution)/shard_map/ppermute | solution.py:50
  42.0 20.7 %copy-start = (bf16[1,512,2048]{2,1,0:T(8,128)(2,1)S(1)}, bf16[1,512,2048]{2,1,0:T(8,128)(2,1)}, u32[]{:S(2)}) copy-start(bf16[1,512,2048]{2,1,0:T(8,128)(2,1)} %param.9) | copy-start | bytes 6291460
  42.0 20.7 %copy-start.1 = (bf16[128,512]{1,0:T(8,128)(2,1)S(1)}, bf16[128,512]{1,0:T(8,128)(2,1)}, u32[]{:S(2)}) copy-start(bf16[128,512]{1,0:T(8,128)(2,1)} %inputs.5) | copy-start | bytes 393220
  43.0 14.5 %collective-permute-start.10 = (bf16[512,512]{1,0:T(8,128)(2,1)S(1)}, bf16[512,512]{1,0:T(8,128)(2,1)S(1)}, u32[]{:S(2)}, u32[]{:S(2)}) collective-permute-start(bf16[512,512]{1,0:T(8,128)(2,1)S(1)} %get-tuple-element.207), channel_id=1, source_target_pairs={{0,2},{1,3},{2,0},{3,1},{4,6},{5,7},{6,4},{7,5},{8,10},{9,11},{10,... | collective-permute-start | bytes 1572872 | tf_op jit(solution)/shard_map/ppermute | solution.py:50
  49.7 11.1 %collective-permute-start.4 = (bf16[128,2048]{1,0:T(8,128)(2,1)S(1)}, bf16[128,2048]{1,0:T(8,128)(2,1)S(1)}, u32[]{:S(2)}, u32[]{:S(2)}) collective-permute-start(bf16[128,2048]{1,0:T(8,128)(2,1)S(1)} %get-tuple-element.209), channel_id=1, source_target_pairs={{0,6},{1,7},{2,4},{3,5},{4,2},{5,3},{6,0},{7,1},{8,14},{9,15},{10,... | collective-permute-start | bytes 1572872 | tf_op jit(solution)/shard_map/ppermute | solution.py:50
  57.5 7.1 %collective-permute-start.11 = (bf16[1024,512]{1,0:T(8,128)(2,1)S(1)}, bf16[1024,512]{1,0:T(8,128)(2,1)S(1)}, u32[]{:S(2)}, u32[]{:S(2)}) collective-permute-start(bf16[1024,512]{1,0:T(8,128)(2,1)S(1)} %constant_dynamic-update-slice_fusion.16.own_out), channel_id=1, source_target_pairs={{0,1},{1,0},{2,3},{3,2},{4,5},{5,4},{6,7},{7,6},{8,9},{9,8},{10,11... | collective-permute-start | bytes 3145736 | tf_op jit(solution)/shard_map/ppermute | solution.py:50
  60.8 4.6 %collective-permute-start.5 = (bf16[256,2048]{1,0:T(8,128)(2,1)S(1)}, bf16[256,2048]{1,0:T(8,128)(2,1)S(1)}, u32[]{:S(2)}, u32[]{:S(2)}) collective-permute-start(bf16[256,2048]{1,0:T(8,128)(2,1)S(1)} %constant_dynamic-update-slice_fusion.5.own_in.refs_2_), channel_id=1, source_target_pairs={{0,1},{1,0},{2,3},{3,2},{4,5},{5,4},{6,7},{7,6},{8,9},{9,8},{10,11... | collective-permute-start | bytes 3145736 | tf_op jit(solution)/shard_map/ppermute | solution.py:50
  67.4 5.3 %collective-permute-start.27 = (bf16[2,64,512]{2,1,0:T(8,128)(2,1)S(1)}, bf16[2,64,512]{2,1,0:T(8,128)(2,1)S(1)}, u32[]{:S(2)}, u32[]{:S(2)}) collective-permute-start(bf16[2,64,512]{2,1,0:T(8,128)(2,1)S(1)} %get-tuple-element.159), channel_id=1, source_target_pairs={{0,64},{1,65},{2,66},{3,67},{4,68},{5,69},{6,70},{7,71},{8,72},{9,... | collective-permute-start | bytes 393224 | tf_op jit(solution)/shard_map/ppermute | solution.py:50
  71.3 4.7 %collective-permute-start.12 = (bf16[2,64,512]{2,1,0:T(8,128)(2,1)S(1)}, bf16[2,64,512]{2,1,0:T(8,128)(2,1)S(1)}, u32[]{:S(2)}, u32[]{:S(2)}) collective-permute-start(bf16[2,64,512]{2,1,0:T(8,128)(2,1)S(1)} %get-tuple-element.111), channel_id=1, source_target_pairs={{0,64},{1,65},{2,66},{3,67},{4,68},{5,69},{6,70},{7,71},{8,72},{9,... | collective-permute-start | bytes 393224 | tf_op jit(solution)/shard_map/ppermute | solution.py:50
  73.3 4.0 %collective-permute-start.28 = (bf16[2,64,512]{2,1,0:T(8,128)(2,1)S(1)}, bf16[2,64,512]{2,1,0:T(8,128)(2,1)S(1)}, u32[]{:S(2)}, u32[]{:S(2)}) collective-permute-start(bf16[2,64,512]{2,1,0:T(8,128)(2,1)S(1)} %get-tuple-element.160), channel_id=1, source_target_pairs={{64,128},{65,129},{66,130},{67,131},{68,132},{69,133},{70,134},{71... | collective-permute-start | bytes 393224 | tf_op jit(solution)/shard_map/ppermute | solution.py:50
  76.5 1.9 collective-permute-start.13
  77.8 1.9 collective-permute-start.29
  79.0 1.9 collective-permute-start.14
  80.3 1.9 collective-permute-start.30
  81.5 10.1 %collective-permute-start.15 = (bf16[2,64,512]{2,1,0:T(8,128)(2,1)S(1)}, bf16[2,64,512]{2,1,0:T(8,128)(2,1)S(1)}, u32[]{:S(2)}, u32[]{:S(2)}) collective-permute-start(bf16[2,64,512]{2,1,0:T(8,128)(2,1)S(1)} %get-tuple-element.114), channel_id=1, source_target_pairs={{192,312},{193,313},{194,314},{195,315},{196,316},{197,317},{198,3... | collective-permute-start | bytes 393224 | tf_op jit(solution)/shard_map/ppermute | solution.py:50
  82.8 12.7 %collective-permute-start.31 = (bf16[2,64,512]{2,1,0:T(8,128)(2,1)S(1)}, bf16[2,64,512]{2,1,0:T(8,128)(2,1)S(1)}, u32[]{:S(2)}, u32[]{:S(2)}) collective-permute-start(bf16[2,64,512]{2,1,0:T(8,128)(2,1)S(1)} %get-tuple-element.163), channel_id=1, source_target_pairs={{0,64},{1,65},{2,66},{3,67},{4,68},{5,69},{6,70},{7,71},{8,72},{9,... | collective-permute-start | bytes 393224 | tf_op jit(solution)/shard_map/ppermute | solution.py:50
  92.2 4.7 %collective-permute-start.16 = (bf16[2,64,512]{2,1,0:T(8,128)(2,1)S(1)}, bf16[2,64,512]{2,1,0:T(8,128)(2,1)S(1)}, u32[]{:S(2)}, u32[]{:S(2)}) collective-permute-start(bf16[2,64,512]{2,1,0:T(8,128)(2,1)S(1)} %get-tuple-element.115), channel_id=1, source_target_pairs={{0,64},{1,65},{2,66},{3,67},{4,68},{5,69},{6,70},{7,71},{8,72},{9,... | collective-permute-start | bytes 393224 | tf_op jit(solution)/shard_map/ppermute | solution.py:50
  96.0 2.1 copy-start.4
  96.0 2.8 %collective-permute-start.32 = (bf16[2,64,512]{2,1,0:T(8,128)(2,1)S(1)}, bf16[2,64,512]{2,1,0:T(8,128)(2,1)S(1)}, u32[]{:S(2)}, u32[]{:S(2)}) collective-permute-start(bf16[2,64,512]{2,1,0:T(8,128)(2,1)S(1)} %get-tuple-element.164), channel_id=1, source_target_pairs={{64,128},{65,129},{66,130},{67,131},{68,132},{69,133},{70,134},{71... | collective-permute-start | bytes 393224 | tf_op jit(solution)/shard_map/ppermute | solution.py:50
  97.4 2.8 %collective-permute-start.17 = (bf16[2,64,512]{2,1,0:T(8,128)(2,1)S(1)}, bf16[2,64,512]{2,1,0:T(8,128)(2,1)S(1)}, u32[]{:S(2)}, u32[]{:S(2)}) collective-permute-start(bf16[2,64,512]{2,1,0:T(8,128)(2,1)S(1)} %get-tuple-element.116), channel_id=1, source_target_pairs={{64,128},{65,129},{66,130},{67,131},{68,132},{69,133},{70,134},{71... | collective-permute-start | bytes 393224 | tf_op jit(solution)/shard_map/ppermute | solution.py:50
  98.1 3.4 %collective-permute-start.19 = (bf16[128,512]{1,0:T(8,128)(2,1)S(1)}, bf16[128,512]{1,0:T(8,128)(2,1)S(1)}, u32[]{:S(2)}, u32[]{:S(2)}) collective-permute-start(bf16[128,512]{1,0:T(8,128)(2,1)S(1)} %copy-done.4), channel_id=1, source_target_pairs={{448,504},{449,505},{450,506},{451,507},{452,508},{453,509},{454,5... | collective-permute-start | bytes 393224 | tf_op jit(solution)/shard_map/ppermute | solution.py:50
  99.5 4.0 %collective-permute-start.33 = (bf16[2,64,512]{2,1,0:T(8,128)(2,1)S(1)}, bf16[2,64,512]{2,1,0:T(8,128)(2,1)S(1)}, u32[]{:S(2)}, u32[]{:S(2)}) collective-permute-start(bf16[2,64,512]{2,1,0:T(8,128)(2,1)S(1)} %get-tuple-element.165), channel_id=1, source_target_pairs={{128,192},{129,193},{130,194},{131,195},{132,196},{133,197},{134,1... | collective-permute-start | bytes 393224 | tf_op jit(solution)/shard_map/ppermute | solution.py:50
  100.8 4.6 %collective-permute-start.18 = (bf16[2,64,512]{2,1,0:T(8,128)(2,1)S(1)}, bf16[2,64,512]{2,1,0:T(8,128)(2,1)S(1)}, u32[]{:S(2)}, u32[]{:S(2)}) collective-permute-start(bf16[2,64,512]{2,1,0:T(8,128)(2,1)S(1)} %get-tuple-element.117), channel_id=1, source_target_pairs={{128,192},{129,193},{130,194},{131,195},{132,196},{133,197},{134,1... | collective-permute-start | bytes 393224 | tf_op jit(solution)/shard_map/ppermute | solution.py:50
  104.7 2.5 collective-permute-start.34
  106.5 1.9 collective-permute-start.20
  107.7 1.9 collective-permute-start.35
  109.0 2.5 %collective-permute-start.21 = (bf16[2,64,512]{2,1,0:T(8,128)(2,1)S(1)}, bf16[2,64,512]{2,1,0:T(8,128)(2,1)S(1)}, u32[]{:S(2)}, u32[]{:S(2)}) collective-permute-start(bf16[2,64,512]{2,1,0:T(8,128)(2,1)S(1)} %get-tuple-element.130), channel_id=1, source_target_pairs={{128,64},{129,65},{130,66},{131,67},{132,68},{133,69},{134,70},{13... | collective-permute-start | bytes 393224 | tf_op jit(solution)/shard_map/ppermute | solution.py:50
  110.2 38.7 %collective-permute-start.36 = (bf16[2,64,512]{2,1,0:T(8,128)(2,1)S(1)}, bf16[2,64,512]{2,1,0:T(8,128)(2,1)S(1)}, u32[]{:S(2)}, u32[]{:S(2)}) collective-permute-start(bf16[2,64,512]{2,1,0:T(8,128)(2,1)S(1)} %get-tuple-element.178), channel_id=1, source_target_pairs={{64,0},{65,1},{66,2},{67,3},{68,4},{69,5},{70,6},{71,7},{72,8},{73... | collective-permute-start | bytes 393224 | tf_op jit(solution)/shard_map/ppermute | solution.py:50
  112.1 38.4 %collective-permute-start.22 = (bf16[2,64,512]{2,1,0:T(8,128)(2,1)S(1)}, bf16[2,64,512]{2,1,0:T(8,128)(2,1)S(1)}, u32[]{:S(2)}, u32[]{:S(2)}) collective-permute-start(bf16[2,64,512]{2,1,0:T(8,128)(2,1)S(1)} %get-tuple-element.134), channel_id=1, source_target_pairs={{64,0},{65,1},{66,2},{67,3},{68,4},{69,5},{70,6},{71,7},{72,8},{73... | collective-permute-start | bytes 393224 | tf_op jit(solution)/shard_map/ppermute | solution.py:50
  149.5 2.3 collective-permute-start.37
  151.0 1.9 collective-permute-start.23
  152.3 1.9 collective-permute-start.38
  153.5 1.9 collective-permute-start.24
  154.8 2.1 collective-permute-start.39
  156.2 2.5 %collective-permute-start.25 = (bf16[2,64,512]{2,1,0:T(8,128)(2,1)S(1)}, bf16[2,64,512]{2,1,0:T(8,128)(2,1)S(1)}, u32[]{:S(2)}, u32[]{:S(2)}) collective-permute-start(bf16[2,64,512]{2,1,0:T(8,128)(2,1)S(1)} %get-tuple-element.145), channel_id=1, source_target_pairs={{128,64},{129,65},{130,66},{131,67},{132,68},{133,69},{134,70},{13... | collective-permute-start | bytes 393224 | tf_op jit(solution)/shard_map/ppermute | solution.py:50
  157.5 45.8 %collective-permute-start.40 = (bf16[2,64,512]{2,1,0:T(8,128)(2,1)S(1)}, bf16[2,64,512]{2,1,0:T(8,128)(2,1)S(1)}, u32[]{:S(2)}, u32[]{:S(2)}) collective-permute-start(bf16[2,64,512]{2,1,0:T(8,128)(2,1)S(1)} %get-tuple-element.194), channel_id=1, source_target_pairs={{64,0},{65,1},{66,2},{67,3},{68,4},{69,5},{70,6},{71,7},{72,8},{73... | collective-permute-start | bytes 393224 | tf_op jit(solution)/shard_map/ppermute | solution.py:50
  159.4 46.3 %collective-permute-start.26 = (bf16[2,64,512]{2,1,0:T(8,128)(2,1)S(1)}, bf16[2,64,512]{2,1,0:T(8,128)(2,1)S(1)}, u32[]{:S(2)}, u32[]{:S(2)}) collective-permute-start(bf16[2,64,512]{2,1,0:T(8,128)(2,1)S(1)} %get-tuple-element.149), channel_id=1, source_target_pairs={{64,0},{65,1},{66,2},{67,3},{68,4},{69,5},{70,6},{71,7},{72,8},{73... | collective-permute-start | bytes 393224 | tf_op jit(solution)/shard_map/ppermute | solution.py:50
  208.1 4.6 %collective-permute-start.41 = (bf16[256,2048]{1,0:T(8,128)(2,1)S(1)}, bf16[256,2048]{1,0:T(8,128)(2,1)S(1)}, u32[]{:S(2)}, u32[]{:S(2)}) collective-permute-start(bf16[256,2048]{1,0:T(8,128)(2,1)S(1)} %get-tuple-element.206), channel_id=1, source_target_pairs={{0,1},{1,0},{2,3},{3,2},{4,5},{5,4},{6,7},{7,6},{8,9},{9,8},{10,11... | collective-permute-start | bytes 3145736 | tf_op jit(solution)/shard_map/ppermute | solution.py:50
  233.0 20.5 %all-to-all-start.1 = ((bf16[8,8,2048]{2,1,0:T(8,128)(2,1)}), bf16[8,8,2048]{2,1,0:T(8,128)(2,1)S(1)}, u32[]{:S(2)}, u32[]{:S(2)}) async-start(bf16[8,8,2048]{2,1,0:T(8,128)(2,1)} %bitcast.10), calls=%async_computation.1 | async-start | bytes 524288 | tf_op jit(solution)/shard_map/all_to_all | solution.py:540

commit v2 on v1

--- a/solution.py
+++ b/solution.py
@@ -18,13 +18,14 @@
 SECTION = ("zh", "x")
 DP = ("b4", "b2", "b1", "y", "c")
 PLACES = 6
-SECTION_AT = 5
 LAYERS = 8
 FEATURES = 512
 HIDDEN = 2048
 MICRO = 2
 ROWS = 128 // MICRO
-UNROLL = 1
+UNROLL_UP = 1
+UNROLL_DOWN = 2
+UNROLL_LAST = 2
 TURN_TICK = 3
 TOKENS = 8192
 CHUNK = 1024
@@ -111,31 +112,29 @@
 
 
 def natural_block(place, b4, b2, b1, y, c):
-    z = (b4 ^ place[0]) * 4 + (b2 ^ place[1]) * 2 + (b1 ^ place[2])
-    return z * 8 + (y ^ place[3]) * 2 + (c ^ place[4])
-
-
-def settled_kernel(place_in, block_in, place, block):
-    for index in range(PLACES):
-        place[index] = place_in[index]
+    z = (b4 ^ place[0][0]) * 4 + (b2 ^ place[1][0]) * 2 + (b1 ^ place[2][0])
+    return z * 8 + (y ^ place[3][0]) * 2 + (c ^ place[4][0])
+
+
+def settled_kernel(*refs):
+    block_in, block = refs[PLACES:]
     block[...] = block_in[...]
 
 
 def settled_call(place, block):
     return pl.pallas_call(
         settled_kernel,
-        out_shape=[
-            jax.ShapeDtypeStruct(place.shape, place.dtype),
-            jax.ShapeDtypeStruct(block.shape, block.dtype),
-        ],
-        in_specs=[SMEM, WHOLE],
-        out_specs=[SMEM, WHOLE],
+        out_shape=jax.ShapeDtypeStruct(block.shape, block.dtype),
+        in_specs=[SMEM] * PLACES + [WHOLE],
+        out_specs=WHOLE,
         compiler_params=PARAMS,
         name="settled",
-    )(place, block)
-
-
-def placed_kernel(place, own_out, other_out, full_out):
+    )(*place, block)
+
+
+def placed_kernel(*refs):
+    place = refs[:PLACES]
+    own_out, other_out, full_out = refs[PLACES:]
     rows = HIDDEN // 64
     for core, half in enumerate((own_out, other_out)):
         for index in range(32):
@@ -148,11 +147,11 @@
     return pl.pallas_call(
         placed_kernel,
         out_shape=jax.ShapeDtypeStruct((HIDDEN, FEATURES), jnp.bfloat16),
-        in_specs=[SMEM] + [WHOLE] * 2,
+        in_specs=[SMEM] * PLACES + [WHOLE] * 2,
         out_specs=WHOLE,
         compiler_params=PARAMS,
         name="placed_w_out",
-    )(place, own_out, other_out)
+    )(*place, own_out, other_out)
 
 
 def row_mean(values):
@@ -168,12 +167,14 @@
     return jnp.where(natural == natural_row, 1.0, 0.0).astype(jnp.bfloat16)
 
 
-def opening_kernel(place, inputs, probe, order, curvature_order, normed_out, preact_t):
+def opening_kernel(*refs):
+    place = refs[:PLACES]
+    inputs, probe, order, curvature_order, normed_out, preact_t = refs[PLACES:]
     at = lax.broadcasted_iota(jnp.int32, (FEATURES, FEATURES), 1)
     row, b4, b2, b1 = at % 8, (at // 8) % 2, (at // 16) % 2, (at // 32) % 2
     even, odd, core = (at // 64) % 2, (at // 128) % 2, at // 256
     order[...] = one_hot(natural_block(place, b4, b2, b1, even ^ (odd * 3), core) * 8 + row)
-    block = (b4 * 4 + b2 * 2 + b1) * 8 + ((at // 64) % 4) * 2 + (core ^ place[4])
+    block = (b4 * 4 + b2 * 2 + b1) * 8 + ((at // 64) % 4) * 2 + (core ^ place[4][0])
     curvature_order[...] = one_hot(block * 8 + row)
     inflow = inputs[...].astype(jnp.float32)
     centred = inflow - row_mean(inflow)
@@ -198,11 +199,11 @@
             jax.ShapeDtypeStruct((rows, FEATURES), jnp.bfloat16),
             jax.ShapeDtypeStruct((rows, HIDDEN), jnp.float32),
         ],
-        in_specs=[SMEM] + [WHOLE] * 2,
+        in_specs=[SMEM] * PLACES + [WHOLE] * 2,
         out_specs=[WHOLE] * 4,
         compiler_params=PARAMS,
         name="opening",
-    )(place, inputs, probe)
+    )(*place, inputs, probe)
 
 
 def gelu_slopes(preact, preact_t, slope_out, chunk):
@@ -220,10 +221,10 @@
     )
 
 
-def first_kernel(micro, place, inputs, opening_n, opening_t, order, own_in, other_in, w_out, pair_out, slope_out, lhs, acc):
+def first_kernel(micro, section, inputs, opening_n, opening_t, order, own_in, other_in, w_out, pair_out, slope_out, lhs, acc):
     rows = slice(micro * ROWS, (micro + 1) * ROWS)
 
-    @pl.when(place[SECTION_AT] == 0)
+    @pl.when(section[0] == 0)
     def _():
         lhs[...] = jnp.dot(opening_n[rows], order[...], preferred_element_type=jnp.float32).astype(jnp.bfloat16)
         acc[:ROWS] = inputs[rows].astype(jnp.float32)
@@ -235,20 +236,20 @@
             acc[...] += jnp.dot(hidden, w_out[columns(chunk), :], preferred_element_type=jnp.float32)
             return carry
 
-        lax.fori_loop(0, CHUNKS, step, 0, unroll=UNROLL)
+        lax.fori_loop(0, CHUNKS, step, 0, unroll=UNROLL_LAST)
         pair_out[0] = acc[:ROWS].astype(jnp.bfloat16)
         pair_out[1] = acc[ROWS:].astype(jnp.bfloat16)
 
 
 def forward_kernel(tick, *refs):
     last = tick == LAYERS - 1
-    place, pair, own_in, other_in, probe, w_out, order = refs[:7]
+    section, pair, own_in, other_in, probe, w_out, order = refs[:7]
     refs = refs[7:]
     if last:
         goal, refs = refs[0], refs[1:]
     pair_out, norm, stat, slope_out, natural, lhs, acc = refs
 
-    @pl.when(place[SECTION_AT] == tick)
+    @pl.when(section[0] == tick)
     def _():
         inflow = pair[0].astype(jnp.float32)
         inflow_t = pair[1].astype(jnp.float32)
@@ -276,7 +277,7 @@
             acc[...] += jnp.dot(hidden, w_out[columns(chunk), :], preferred_element_type=jnp.float32)
             return carry
 
-        lax.fori_loop(0, CHUNKS, step, 0, unroll=UNROLL)
+        lax.fori_loop(0, CHUNKS, step, 0, unroll=UNROLL_UP)
         if last:
             pair_out[0] = ((acc[:ROWS] - goal[...].astype(jnp.float32)) / TOKENS).astype(jnp.bfloat16)
             pair_out[1] = (acc[ROWS:] / TOKENS).astype(jnp.bfloat16)
@@ -293,7 +294,7 @@
 PARAMS = pltpu.CompilerParams(vmem_limit_bytes=VMEM_BYTES)
 
 
-def first_call(micro, place, inputs, opening_n, opening_t, order, own_in, other_in, w_out):
+def first_call(micro, section, inputs, opening_n, opening_t, order, own_in, other_in, w_out):
     return pl.pallas_call(
         functools.partial(first_kernel, micro),
         out_shape=[PAIR, SLOPE],
@@ -305,11 +306,11 @@
         ],
         compiler_params=PARAMS,
         name="layer_up_0",
-    )(place, inputs, opening_n, opening_t, order, own_in, other_in, w_out)
-
-
-def forward_call(tick, place, pair, own_in, other_in, probe, w_out, order, goal):
-    operands = [place, pair, own_in, other_in, probe, w_out, order] + ([goal] if tick == LAYERS - 1 else [])
+    )(section, inputs, opening_n, opening_t, order, own_in, other_in, w_out)
+
+
+def forward_call(tick, section, pair, own_in, other_in, probe, w_out, order, goal):
+    operands = [section, pair, own_in, other_in, probe, w_out, order] + ([goal] if tick == LAYERS - 1 else [])
     return pl.pallas_call(
         functools.partial(forward_kernel, tick),
         out_shape=[PAIR, NORM, STAT, SLOPE],
@@ -369,10 +370,10 @@
 
 
 def backward_kernel(tick, *refs):
-    place, pair, w_in_t, probe_t, w_out_t, norm, stat, slope = refs[:8]
+    section, pair, w_in_t, probe_t, w_out_t, norm, stat, slope = refs[:8]
     pair_out, grads, acc, acc_t = refs[8:]
 
-    @pl.when(place[SECTION_AT] == LAYERS - 1 - tick)
+    @pl.when(section[0] == LAYERS - 1 - tick)
     def _():
         acc[...] = jnp.zeros_like(acc)
         acc_t[...] = jnp.zeros_like(acc_t)
@@ -385,7 +386,7 @@
             acc_t[...] += jnp.dot(low_grad, probe_t[columns(chunk), :], preferred_element_type=jnp.float32)
             return carry
 
-        lax.fori_loop(0, CHUNKS, step, 0, unroll=UNROLL)
+        lax.fori_loop(0, CHUNKS, step, 0, unroll=UNROLL_DOWN)
         normed, normed_t = norm[0], norm[1]
         rscale, tangent_dot = stat[0][:, :1], stat[1][:, :1]
         grad_norm = acc[ROWS:]
@@ -400,8 +401,8 @@
         pair_out[1] = (pair[1].astype(jnp.float32) + through_t).astype(jnp.bfloat16)
 
 
-def backward_call(tick, place, pair, w_in_t, probe_t, w_out_t, kept):
-    operands = [place, pair, w_in_t, probe_t, w_out_t, *kept]
+def backward_call(tick, section, pair, w_in_t, probe_t, w_out_t, kept):
+    operands = [section, pair, w_in_t, probe_t, w_out_t, *kept]
     return pl.pallas_call(
         functools.partial(backward_kernel, tick),
         out_shape=[PAIR, GRADS],
@@ -420,8 +421,8 @@
 OTHER_HALF = slice(FEATURES // 2, FEATURES)
 
 
-def curvature_operands(micro, place, pair, w_out_t, slope, order, opening_n, norms, grads, lhs, rhs):
-    @pl.when(place[SECTION_AT] == 0)
+def curvature_operands(micro, section, pair, w_out_t, slope, order, opening_n, norms, grads, lhs, rhs):
+    @pl.when(section[0] == 0)
     def _():
         rows = slice(micro * ROWS, (micro + 1) * ROWS)
         lhs[:ROWS] = jnp.dot(opening_n[rows], order[...], preferred_element_type=jnp.float32).astype(jnp.bfloat16)
@@ -432,11 +433,11 @@
             rhs[:, columns(chunk)] = jnp.concatenate([low_grad_t, low_grad], axis=0)
             return carry
 
-        lax.fori_loop(0, CHUNKS, bottom, 0, unroll=UNROLL)
+        lax.fori_loop(0, CHUNKS, bottom, 0, unroll=UNROLL_LAST)
 
     for layer in range(1, LAYERS):
 
-        @pl.when(place[SECTION_AT] == layer)
+        @pl.when(section[0] == layer)
         def _():
             both = norms[layer - 1][...].reshape(2 * ROWS, FEATURES).astype(jnp.bfloat16)
             lhs[...] = jnp.dot(both, order[...], preferred_element_type=jnp.float32).astype(jnp.bfloat16)
@@ -444,13 +445,13 @@
 
 
 def curvature_kernel(micro, final, *refs):
-    place, pair, w_out_t, slope, order, opening_n = refs[:6]
+    section, pair, w_out_t, slope, order, opening_n = refs[:6]
     norms, refs = refs[6 : 5 + LAYERS], refs[5 + LAYERS :]
     grads, refs = refs[: LAYERS - 1], refs[LAYERS - 1 :]
     if final:
         away_in, stay_in, refs = refs[0], refs[1], refs[2:]
     away, stay, lhs, rhs = refs
-    curvature_operands(micro, place, pair, w_out_t, slope, order, opening_n, norms, grads, lhs, rhs)
+    curvature_operands(micro, section, pair, w_out_t, slope, order, opening_n, norms, grads, lhs, rhs)
 
     def step(chunk, carry):
         now = columns(chunk)
@@ -466,13 +467,13 @@
             stay[:, now] = product(OWN_HALF)
         return carry
 
-    lax.fori_loop(0, CHUNKS, step, 0, unroll=UNROLL)
-
-
-def curvature_call(micro, place, pair, w_out_t, slope, order, opening_n, norms, grads, sums):
+    lax.fori_loop(0, CHUNKS, step, 0, unroll=UNROLL_LAST)
+
+
+def curvature_call(micro, section, pair, w_out_t, slope, order, opening_n, norms, grads, sums):
     half = (FEATURES // 2, HIDDEN)
     final = bool(sums)
-    operands = [place, pair, w_out_t, slope, order, opening_n, *norms, *grads, *sums]
+    operands = [section, pair, w_out_t, slope, order, opening_n, *norms, *grads, *sums]
     return pl.pallas_call(
         functools.partial(curvature_kernel, micro, final),
         out_shape=[
@@ -491,8 +492,9 @@
 
 
 def shards(inputs, targets, w_in, w_out, probes):
-    place = jnp.stack([lax.axis_index(name) for name in (*DP, SECTION)]).astype(jnp.int32)
-    place, out_block = settled_call(place, w_out[0])
+    place = [jnp.reshape(lax.axis_index(name), (1,)).astype(jnp.int32) for name in (*DP, SECTION)]
+    section = place[-1]
+    out_block = settled_call(place, w_out[0])
     probe = probes[0]
     own_in, other_in = gathered(w_in[0], True)
     full_out = placed_call(place, *gathered(out_block, False))
@@ -506,13 +508,13 @@
         for micro in range(MICRO):
             if tick == 0:
                 pairs[micro], slope = first_call(
-                    micro, place, inputs, opening_n, opening_t, order, own_in, other_in, full_out
+                    micro, section, inputs, opening_n, opening_t, order, own_in, other_in, full_out
                 )
                 slopes.append(slope)
             else:
                 goal_now = goal[micro * ROWS : (micro + 1) * ROWS]
                 pairs[micro], *stores = forward_call(
-                    tick, place, pairs[micro], own_in, other_in, probe, full_out, order, goal_now
+                    tick, section, pairs[micro], own_in, other_in, probe, full_out, order, goal_now
                 )
                 kept[micro].append(stores)
             if tick < LAYERS - 1:
@@ -522,7 +524,7 @@
     for tick in range(LAYERS - 1):
         for micro in range(MICRO):
             pairs[micro], low_grads = backward_call(
-                tick, place, pairs[micro], *turned, kept[micro][LAYERS - 2 - tick]
+                tick, section, pairs[micro], *turned, kept[micro][LAYERS - 2 - tick]
             )
             grads[micro].append(low_grads)
             pairs[micro] = routed(pairs[micro], down_from(LAYERS - 1 - tick))
@@ -530,7 +532,7 @@
     for micro in range(MICRO):
         norms = [stores[0] for stores in kept[micro]]
         sums = curvature_call(
-            micro, place, pairs[micro], turned[2], slopes[micro], curvature_order, opening_n, norms, grads[micro], sums
+            micro, section, pairs[micro], turned[2], slopes[micro], curvature_order, opening_n, norms, grads[micro], sums
         )
     away, stay = sums
     other = routed(away, swap_core)

time: 255 us -> 241 us (0.945)
  Pallas kernels: 30.2 us -> 8.95 us
  waiting for transfers between devices: 113 us -> 120 us
    pallas_call x14, Pallas kernels: 7.93 us -> 0.13 us  [backward_call(): pl.pallas_call(functools.partial(backward_kernel, tick), out_shape=[PAIR,...]
    pallas_call x14, Pallas kernels: 7.89 us -> 0.12 us  [forward_call(): pl.pallas_call(functools.partial(forward_kernel, tick), out_shape=[PAIR,...]
    ppermute x42, waiting for transfers between devices: 97.8 us -> 104 us  [routed(): return lax.ppermute(value, NAMES, pairs)]
  transfers between devices with their start and end apart: 43 -> 43, of which waited for: 16 -> 18; matrix products, arithmetic and copies ran while one was open for 1% -> 1% of each run, Pallas kernels for 10% -> 3%
where the time goes in v2:
time: 241 us; the launch traced here: 240 us
  waiting for transfers between devices  120 us (50%)
  starting transfers between devices  85.3 us (35%)
  blocking collectives  19.4 us (8%)
  Pallas kernels  8.95 us (4%)
  other arithmetic  3.51 us (1%)
    ppermute x42, waiting for transfers between devices, routed(): return lax.ppermute(value, NAMES, pairs)  104 us
    ppermute x42, starting transfers between devices, routed(): return lax.ppermute(value, NAMES, pairs)  80.8 us
    all_to_all x1, blocking collectives, shards(): lax.all_to_all(summed.reshape(4, 64, HIDDEN), 'y', 0, 0, tiled=True)  19.4 us
    all_to_all x1, waiting for transfers between devices, shards(): lax.all_to_all(summed.reshape(8, 8, HIDDEN), ('b1', 'b2', 'b4'), 0, 0, ti...  15.5 us
  transfers between devices with their start and end apart: 43, of which 18 were waited for; matrix products, arithmetic and copies ran while one was open for 1% of the time, Pallas kernels for 3%

profile of v2, /device:TPU:8, one launch (start us, length us, event | category | flops | bytes accessed | tf_op | source)
XLA Modules:
  0.0 239.6 jit_solution(5812649614163618590)
XLA Ops:
  0.0 0.8 copy-done.2
  0.8 9.1 %collective-permute-start.6 = (bf16[32,512]{1,0:T(8,128)(2,1)S(1)}, bf16[32,512]{1,0:T(8,128)(2,1)S(1)}, u32[]{:S(2)}, u32[]{:S(2)}) collective-permute-start(bf16[32,512]{1,0:T(8,128)(2,1)S(1)} %settled.1), channel_id=1, source_target_pairs={{0,32},{1,33},{2,34},{3,35},{4,36},{5,37},{6,38},{7,39},{8,40},{9,... | collective-permute-start | bytes 98312 | tf_op jit(solution)/shard_map/ppermute | solution.py:51
  9.9 1.9 collective-permute-start
  11.8 0.8 constant_dynamic-update-slice_fusion.4
  12.6 5.2 %collective-permute-start.7 = (bf16[64,512]{1,0:T(8,128)(2,1)S(1)}, bf16[64,512]{1,0:T(8,128)(2,1)S(1)}, u32[]{:S(2)}, u32[]{:S(2)}) collective-permute-start(bf16[64,512]{1,0:T(8,128)(2,1)S(1)} %pad_maximum_fusion.5), channel_id=1, source_target_pairs={{0,16},{1,17},{2,18},{3,19},{4,20},{5,21},{6,22},{7,23},{8,24},{9,... | collective-permute-start | bytes 196616 | tf_op jit(solution)/shard_map/ppermute | solution.py:51
  17.8 2.4 collective-permute-done
  20.2 0.8 pad_maximum_fusion.4
  20.9 5.2 %collective-permute-start.1 = (bf16[16,2048]{1,0:T(8,128)(2,1)S(1)}, bf16[16,2048]{1,0:T(8,128)(2,1)S(1)}, u32[]{:S(2)}, u32[]{:S(2)}) collective-permute-start(bf16[16,2048]{1,0:T(8,128)(2,1)S(1)} %pad_maximum_fusion.4), channel_id=1, source_target_pairs={{0,16},{1,17},{2,18},{3,19},{4,20},{5,21},{6,22},{7,23},{8,24},{9,... | collective-permute-start | bytes 196616 | tf_op jit(solution)/shard_map/ppermute | solution.py:51
  26.2 3.5 %collective-permute-start.8 = (bf16[128,512]{1,0:T(8,128)(2,1)S(1)}, bf16[128,512]{1,0:T(8,128)(2,1)S(1)}, u32[]{:S(2)}, u32[]{:S(2)}) collective-permute-start(bf16[128,512]{1,0:T(8,128)(2,1)S(1)} %pad_maximum_fusion.3), channel_id=1, source_target_pairs={{0,8},{1,9},{2,10},{3,11},{4,12},{5,13},{6,14},{7,15},{8,0},{9,1},... | collective-permute-start | bytes 393224 | tf_op jit(solution)/shard_map/ppermute | solution.py:51
  29.7 0.8 pad_maximum_fusion.2
  30.5 2.8 %collective-permute-start.2 = (bf16[32,2048]{1,0:T(8,128)(2,1)S(1)}, bf16[32,2048]{1,0:T(8,128)(2,1)S(1)}, u32[]{:S(2)}, u32[]{:S(2)}) collective-permute-start(bf16[32,2048]{1,0:T(8,128)(2,1)S(1)} %pad_maximum_fusion.2), channel_id=1, source_target_pairs={{0,8},{1,9},{2,10},{3,11},{4,12},{5,13},{6,14},{7,15},{8,0},{9,1},... | collective-permute-start | bytes 393224 | tf_op jit(solution)/shard_map/ppermute | solution.py:51
  33.4 3.5 %collective-permute-start.9 = (bf16[256,512]{1,0:T(8,128)(2,1)S(1)}, bf16[256,512]{1,0:T(8,128)(2,1)S(1)}, u32[]{:S(2)}, u32[]{:S(2)}) collective-permute-start(bf16[256,512]{1,0:T(8,128)(2,1)S(1)} %pad_maximum_fusion.1), channel_id=1, source_target_pairs={{0,6},{1,7},{2,4},{3,5},{4,2},{5,3},{6,0},{7,1},{8,14},{9,15},{10,... | collective-permute-start | bytes 786440 | tf_op jit(solution)/shard_map/ppermute | solution.py:51
  37.4 3.3 %collective-permute-start.3 = (bf16[64,2048]{1,0:T(8,128)(2,1)S(1)}, bf16[64,2048]{1,0:T(8,128)(2,1)S(1)}, u32[]{:S(2)}, u32[]{:S(2)}) collective-permute-start(bf16[64,2048]{1,0:T(8,128)(2,1)S(1)} %pad_maximum_fusion), channel_id=1, source_target_pairs={{0,2},{1,3},{2,0},{3,1},{4,6},{5,7},{6,4},{7,5},{8,10},{9,11},{10,... | collective-permute-start | bytes 786440 | tf_op jit(solution)/shard_map/ppermute | solution.py:51
  40.8 0.8 collective-permute-done.9
  41.7 3.6 %collective-permute-start.10 = (bf16[512,512]{1,0:T(8,128)(2,1)S(1)}, bf16[512,512]{1,0:T(8,128)(2,1)S(1)}, u32[]{:S(2)}, u32[]{:S(2)}) collective-permute-start(bf16[512,512]{1,0:T(8,128)(2,1)S(1)} %get-tuple-element.203), channel_id=1, source_target_pairs={{0,2},{1,3},{2,0},{3,1},{4,6},{5,7},{6,4},{7,5},{8,10},{9,11},{10,... | collective-permute-start | bytes 1572872 | tf_op jit(solution)/shard_map/ppermute | solution.py:51
  45.3 3.1 %collective-permute-done.3 = bf16[64,2048]{1,0:T(8,128)(2,1)S(1)} collective-permute-done((bf16[64,2048]{1,0:T(8,128)(2,1)S(1)}, bf16[64,2048]{1,0:T(8,128)(2,1)S(1)}, u32[]{:S(2)}, u32[]{:S(2)}) %collective-permute-start.3) | collective-permute-done | bytes 262176 | tf_op jit(solution)/shard_map/ppermute | solution.py:51
  48.5 3.5 %collective-permute-start.4 = (bf16[128,2048]{1,0:T(8,128)(2,1)S(1)}, bf16[128,2048]{1,0:T(8,128)(2,1)S(1)}, u32[]{:S(2)}, u32[]{:S(2)}) collective-permute-start(bf16[128,2048]{1,0:T(8,128)(2,1)S(1)} %get-tuple-element.205), channel_id=1, source_target_pairs={{0,6},{1,7},{2,4},{3,5},{4,2},{5,3},{6,0},{7,1},{8,14},{9,15},{10,... | collective-permute-start | bytes 1572872 | tf_op jit(solution)/shard_map/ppermute | solution.py:51
  52.0 4.2 %collective-permute-done.10 = bf16[512,512]{1,0:T(8,128)(2,1)S(1)} collective-permute-done((bf16[512,512]{1,0:T(8,128)(2,1)S(1)}, bf16[512,512]{1,0:T(8,128)(2,1)S(1)}, u32[]{:S(2)}, u32[]{:S(2)}) %collective-permute-start.10) | collective-permute-done | bytes 524320 | tf_op jit(solution)/shard_map/ppermute | solution.py:51
  56.2 1.9 collective-permute-start.11
  58.2 1.4 collective-permute-done.4
  59.6 1.9 collective-permute-start.5
  61.5 1.3 opening.1
  63.1 1.1 collective-permute-done.5.other_in.refs_3_
  64.2 1.2 layer_up_0.3
  65.4 2.2 collective-permute-start.27
  67.6 1.2 layer_up_0.2
  68.8 1.3 collective-permute-start.12
  71.5 1.9 collective-permute-done.12.refs_1_
  76.9 9.2 %collective-permute-start.31 = (bf16[2,64,512]{2,1,0:T(8,128)(2,1)S(1)}, bf16[2,64,512]{2,1,0:T(8,128)(2,1)S(1)}, u32[]{:S(2)}, u32[]{:S(2)}) collective-permute-start(bf16[2,64,512]{2,1,0:T(8,128)(2,1)S(1)} %get-tuple-element.159), channel_id=1, source_target_pairs={{0,64},{1,65},{2,66},{3,67},{4,68},{5,69},{6,70},{7,71},{8,72},{9,... | collective-permute-start | bytes 393224 | tf_op jit(solution)/shard_map/ppermute | solution.py:51
  86.1 1.3 collective-permute-start.16
  87.4 1.5 collective-permute-done.31.refs_1_
  88.9 0.8 collective-permute-start.32
  90.3 0.8 collective-permute-start.17
  93.3 2.0 turned_weights.1
  98.3 1.3 collective-permute-start.36
  99.6 1.3 collective-permute-start.22
  100.9 36.0 %collective-permute-done.36.refs_1_ = bf16[2,64,512]{2,1,0:T(8,128)(2,1)S(1)} collective-permute-done((bf16[2,64,512]{2,1,0:T(8,128)(2,1)S(1)}, bf16[2,64,512]{2,1,0:T(8,128)(2,1)S(1)}, u32[]{:S(2)}, u32[]{:S(2)}) %collective-permute-start.36) | collective-permute-done | bytes 131104 | tf_op jit(solution)/shard_map/ppermute | solution.py:51
  141.9 1.3 collective-permute-start.40
  143.2 1.3 collective-permute-start.26
  144.5 45.6 %collective-permute-done.40.refs_1_ = bf16[2,64,512]{2,1,0:T(8,128)(2,1)S(1)} collective-permute-done((bf16[2,64,512]{2,1,0:T(8,128)(2,1)S(1)}, bf16[2,64,512]{2,1,0:T(8,128)(2,1)S(1)}, u32[]{:S(2)}, u32[]{:S(2)}) %collective-permute-start.40) | collective-permute-done | bytes 131104 | tf_op jit(solution)/shard_map/ppermute | solution.py:51
  190.1 1.4 curvature_first.1
  192.2 1.4 curvature_last.1
  193.6 1.9 collective-permute-start.41
  195.5 2.6 %collective-permute-done.41 = bf16[256,2048]{1,0:T(8,128)(2,1)S(1)} collective-permute-done((bf16[256,2048]{1,0:T(8,128)(2,1)S(1)}, bf16[256,2048]{1,0:T(8,128)(2,1)S(1)}, u32[]{:S(2)}, u32[]{:S(2)}) %collective-permute-start.41) | collective-permute-done | bytes 1048608 | tf_op jit(solution)/shard_map/ppermute | solution.py:51
  198.5 19.4 %all_to_all.10 = bf16[4,64,2048]{2,1,0:T(8,128)(2,1)S(1)} all-to-all(bf16[4,64,2048]{2,1,0:T(8,128)(2,1)S(1)} %bitcast.32), channel_id=1, replica_groups=mesh['zh'=2,'x'=4,'b4'=2,'b2'=2,'b1'=2,'y'=4,'c'=2] {'y'}, dimensions={0} | all-to-all | bytes 2097152 | tf_op jit(solution)/shard_map/all_to_all | solution.py:540
  217.9 0.9 reduce_sum.23
  218.8 4.6 %all-to-all-start.1 = ((bf16[8,8,2048]{2,1,0:T(8,128)(2,1)}), bf16[8,8,2048]{2,1,0:T(8,128)(2,1)S(1)}, u32[]{:S(2)}, u32[]{:S(2)}) async-start(bf16[8,8,2048]{2,1,0:T(8,128)(2,1)} %bitcast.10), calls=%async_computation.1 | async-start | bytes 524288 | tf_op jit(solution)/shard_map/all_to_all | solution.py:542
  223.4 15.5 %all-to-all-done.1 = bf16[8,8,2048]{2,1,0:T(8,128)(2,1)S(1)} async-done(((bf16[8,8,2048]{2,1,0:T(8,128)(2,1)}), bf16[8,8,2048]{2,1,0:T(8,128)(2,1)S(1)}, u32[]{:S(2)}, u32[]{:S(2)}) %all-to-all-start.1) | async-done | bytes 262176 | tf_op jit(solution)/shard_map/all_to_all | solution.py:542
  (108 shorter events, 17.9 us)
Async XLA Ops:
  0.0 37.4 %copy-start.3 = (bf16[1,8,2048]{2,1,0:T(8,128)(2,1)S(1)}, bf16[1,8,2048]{2,1,0:T(8,128)(2,1)}, u32[]{:S(2)}) copy-start(bf16[1,8,2048]{2,1,0:T(8,128)(2,1)} %param.7) | copy-start | bytes 98308
  0.0 0.8 copy-start.2
  0.8 11.8 %collective-permute-start.6 = (bf16[32,512]{1,0:T(8,128)(2,1)S(1)}, bf16[32,512]{1,0:T(8,128)(2,1)S(1)}, u32[]{:S(2)}, u32[]{:S(2)}) collective-permute-start(bf16[32,512]{1,0:T(8,128)(2,1)S(1)} %settled.1), channel_id=1, source_target_pairs={{0,32},{1,33},{2,34},{3,35},{4,36},{5,37},{6,38},{7,39},{8,40},{9,... | collective-permute-start | bytes 98312 | tf_op jit(solution)/shard_map/ppermute | solution.py:51
  9.9 10.3 %collective-permute-start = (bf16[8,2048]{1,0:T(8,128)(2,1)}, bf16[8,2048]{1,0:T(8,128)(2,1)S(1)}, u32[]{:S(2)}, u32[]{:S(2)}) collective-permute-start(bf16[8,2048]{1,0:T(8,128)(2,1)} %bitcast.33), channel_id=1, source_target_pairs={{0,32},{1,33},{2,34},{3,35},{4,36},{5,37},{6,38},{7,39},{8,40},{9,... | collective-permute-start | bytes 98312 | tf_op jit(solution)/shard_map/ppermute | solution.py:51
  12.6 13.6 %collective-permute-start.7 = (bf16[64,512]{1,0:T(8,128)(2,1)S(1)}, bf16[64,512]{1,0:T(8,128)(2,1)S(1)}, u32[]{:S(2)}, u32[]{:S(2)}) collective-permute-start(bf16[64,512]{1,0:T(8,128)(2,1)S(1)} %pad_maximum_fusion.5), channel_id=1, source_target_pairs={{0,16},{1,17},{2,18},{3,19},{4,20},{5,21},{6,22},{7,23},{8,24},{9,... | collective-permute-start | bytes 196616 | tf_op jit(solution)/shard_map/ppermute | solution.py:51
  20.9 8.8 %collective-permute-start.1 = (bf16[16,2048]{1,0:T(8,128)(2,1)S(1)}, bf16[16,2048]{1,0:T(8,128)(2,1)S(1)}, u32[]{:S(2)}, u32[]{:S(2)}) collective-permute-start(bf16[16,2048]{1,0:T(8,128)(2,1)S(1)} %pad_maximum_fusion.4), channel_id=1, source_target_pairs={{0,16},{1,17},{2,18},{3,19},{4,20},{5,21},{6,22},{7,23},{8,24},{9,... | collective-permute-start | bytes 196616 | tf_op jit(solution)/shard_map/ppermute | solution.py:51
  26.2 7.2 %collective-permute-start.8 = (bf16[128,512]{1,0:T(8,128)(2,1)S(1)}, bf16[128,512]{1,0:T(8,128)(2,1)S(1)}, u32[]{:S(2)}, u32[]{:S(2)}) collective-permute-start(bf16[128,512]{1,0:T(8,128)(2,1)S(1)} %pad_maximum_fusion.3), channel_id=1, source_target_pairs={{0,8},{1,9},{2,10},{3,11},{4,12},{5,13},{6,14},{7,15},{8,0},{9,1},... | collective-permute-start | bytes 393224 | tf_op jit(solution)/shard_map/ppermute | solution.py:51
  30.5 6.9 %collective-permute-start.2 = (bf16[32,2048]{1,0:T(8,128)(2,1)S(1)}, bf16[32,2048]{1,0:T(8,128)(2,1)S(1)}, u32[]{:S(2)}, u32[]{:S(2)}) collective-permute-start(bf16[32,2048]{1,0:T(8,128)(2,1)S(1)} %pad_maximum_fusion.2), channel_id=1, source_target_pairs={{0,8},{1,9},{2,10},{3,11},{4,12},{5,13},{6,14},{7,15},{8,0},{9,1},... | collective-permute-start | bytes 393224 | tf_op jit(solution)/shard_map/ppermute | solution.py:51
  33.4 8.3 %collective-permute-start.9 = (bf16[256,512]{1,0:T(8,128)(2,1)S(1)}, bf16[256,512]{1,0:T(8,128)(2,1)S(1)}, u32[]{:S(2)}, u32[]{:S(2)}) collective-permute-start(bf16[256,512]{1,0:T(8,128)(2,1)S(1)} %pad_maximum_fusion.1), channel_id=1, source_target_pairs={{0,6},{1,7},{2,4},{3,5},{4,2},{5,3},{6,0},{7,1},{8,14},{9,15},{10,... | collective-permute-start | bytes 786440 | tf_op jit(solution)/shard_map/ppermute | solution.py:51
  37.4 11.0 %collective-permute-start.3 = (bf16[64,2048]{1,0:T(8,128)(2,1)S(1)}, bf16[64,2048]{1,0:T(8,128)(2,1)S(1)}, u32[]{:S(2)}, u32[]{:S(2)}) collective-permute-start(bf16[64,2048]{1,0:T(8,128)(2,1)S(1)} %pad_maximum_fusion), channel_id=1, source_target_pairs={{0,2},{1,3},{2,0},{3,1},{4,6},{5,7},{6,4},{7,5},{8,10},{9,11},{10,... | collective-permute-start | bytes 786440 | tf_op jit(solution)/shard_map/ppermute | solution.py:51
  40.8 20.7 %copy-start = (bf16[1,512,2048]{2,1,0:T(8,128)(2,1)S(1)}, bf16[1,512,2048]{2,1,0:T(8,128)(2,1)}, u32[]{:S(2)}) copy-start(bf16[1,512,2048]{2,1,0:T(8,128)(2,1)} %param.9) | copy-start | bytes 6291460
  40.8 20.7 %copy-start.1 = (bf16[128,512]{1,0:T(8,128)(2,1)S(1)}, bf16[128,512]{1,0:T(8,128)(2,1)}, u32[]{:S(2)}) copy-start(bf16[128,512]{1,0:T(8,128)(2,1)} %inputs.3) | copy-start | bytes 393220
  41.7 14.5 %collective-permute-start.10 = (bf16[512,512]{1,0:T(8,128)(2,1)S(1)}, bf16[512,512]{1,0:T(8,128)(2,1)S(1)}, u32[]{:S(2)}, u32[]{:S(2)}) collective-permute-start(bf16[512,512]{1,0:T(8,128)(2,1)S(1)} %get-tuple-element.203), channel_id=1, source_target_pairs={{0,2},{1,3},{2,0},{3,1},{4,6},{5,7},{6,4},{7,5},{8,10},{9,11},{10,... | collective-permute-start | bytes 1572872 | tf_op jit(solution)/shard_map/ppermute | solution.py:51
  48.5 11.1 %collective-permute-start.4 = (bf16[128,2048]{1,0:T(8,128)(2,1)S(1)}, bf16[128,2048]{1,0:T(8,128)(2,1)S(1)}, u32[]{:S(2)}, u32[]{:S(2)}) collective-permute-start(bf16[128,2048]{1,0:T(8,128)(2,1)S(1)} %get-tuple-element.205), channel_id=1, source_target_pairs={{0,6},{1,7},{2,4},{3,5},{4,2},{5,3},{6,0},{7,1},{8,14},{9,15},{10,... | collective-permute-start | bytes 1572872 | tf_op jit(solution)/shard_map/ppermute | solution.py:51
  56.2 6.6 %collective-permute-start.11 = (bf16[1024,512]{1,0:T(8,128)(2,1)S(1)}, bf16[1024,512]{1,0:T(8,128)(2,1)S(1)}, u32[]{:S(2)}, u32[]{:S(2)}) collective-permute-start(bf16[1024,512]{1,0:T(8,128)(2,1)S(1)} %constant_dynamic-update-slice_fusion.16.refs_6_), channel_id=1, source_target_pairs={{0,1},{1,0},{2,3},{3,2},{4,5},{5,4},{6,7},{7,6},{8,9},{9,8},{10,11... | collective-permute-start | bytes 3145736 | tf_op jit(solution)/shard_map/ppermute | solution.py:51
  59.6 4.6 %collective-permute-start.5 = (bf16[256,2048]{1,0:T(8,128)(2,1)S(1)}, bf16[256,2048]{1,0:T(8,128)(2,1)S(1)}, u32[]{:S(2)}, u32[]{:S(2)}) collective-permute-start(bf16[256,2048]{1,0:T(8,128)(2,1)S(1)} %constant_dynamic-update-slice_fusion.5.own_in.refs_2_), channel_id=1, source_target_pairs={{0,1},{1,0},{2,3},{3,2},{4,5},{5,4},{6,7},{7,6},{8,9},{9,8},{10,11... | collective-permute-start | bytes 3145736 | tf_op jit(solution)/shard_map/ppermute | solution.py:51
  65.4 5.4 %collective-permute-start.27 = (bf16[2,64,512]{2,1,0:T(8,128)(2,1)S(1)}, bf16[2,64,512]{2,1,0:T(8,128)(2,1)S(1)}, u32[]{:S(2)}, u32[]{:S(2)}) collective-permute-start(bf16[2,64,512]{2,1,0:T(8,128)(2,1)S(1)} %get-tuple-element.155), channel_id=1, source_target_pairs={{0,64},{1,65},{2,66},{3,67},{4,68},{5,69},{6,70},{7,71},{8,72},{9,... | collective-permute-start | bytes 393224 | tf_op jit(solution)/shard_map/ppermute | solution.py:51
  68.8 4.6 %collective-permute-start.12 = (bf16[2,64,512]{2,1,0:T(8,128)(2,1)S(1)}, bf16[2,64,512]{2,1,0:T(8,128)(2,1)S(1)}, u32[]{:S(2)}, u32[]{:S(2)}) collective-permute-start(bf16[2,64,512]{2,1,0:T(8,128)(2,1)S(1)} %get-tuple-element.107), channel_id=1, source_target_pairs={{0,64},{1,65},{2,66},{3,67},{4,68},{5,69},{6,70},{7,71},{8,72},{9,... | collective-permute-start | bytes 393224 | tf_op jit(solution)/shard_map/ppermute | solution.py:51
  70.8 3.3 %collective-permute-start.28 = (bf16[2,64,512]{2,1,0:T(8,128)(2,1)S(1)}, bf16[2,64,512]{2,1,0:T(8,128)(2,1)S(1)}, u32[]{:S(2)}, u32[]{:S(2)}) collective-permute-start(bf16[2,64,512]{2,1,0:T(8,128)(2,1)S(1)} %get-tuple-element.156), channel_id=1, source_target_pairs={{64,128},{65,129},{66,130},{67,131},{68,132},{69,133},{70,134},{71... | collective-permute-start | bytes 393224 | tf_op jit(solution)/shard_map/ppermute | solution.py:51
  73.4 1.4 collective-permute-start.13
  74.1 1.4 collective-permute-start.29
  74.8 1.4 collective-permute-start.14
  75.5 1.4 collective-permute-start.30
  76.2 9.9 %collective-permute-start.15 = (bf16[2,64,512]{2,1,0:T(8,128)(2,1)S(1)}, bf16[2,64,512]{2,1,0:T(8,128)(2,1)S(1)}, u32[]{:S(2)}, u32[]{:S(2)}) collective-permute-start(bf16[2,64,512]{2,1,0:T(8,128)(2,1)S(1)} %get-tuple-element.110), channel_id=1, source_target_pairs={{192,312},{193,313},{194,314},{195,315},{196,316},{197,317},{198,3... | collective-permute-start | bytes 393224 | tf_op jit(solution)/shard_map/ppermute | solution.py:51
  76.9 12.0 %collective-permute-start.31 = (bf16[2,64,512]{2,1,0:T(8,128)(2,1)S(1)}, bf16[2,64,512]{2,1,0:T(8,128)(2,1)S(1)}, u32[]{:S(2)}, u32[]{:S(2)}) collective-permute-start(bf16[2,64,512]{2,1,0:T(8,128)(2,1)S(1)} %get-tuple-element.159), channel_id=1, source_target_pairs={{0,64},{1,65},{2,66},{3,67},{4,68},{5,69},{6,70},{7,71},{8,72},{9,... | collective-permute-start | bytes 393224 | tf_op jit(solution)/shard_map/ppermute | solution.py:51
  86.1 4.2 %collective-permute-start.16 = (bf16[2,64,512]{2,1,0:T(8,128)(2,1)S(1)}, bf16[2,64,512]{2,1,0:T(8,128)(2,1)S(1)}, u32[]{:S(2)}, u32[]{:S(2)}) collective-permute-start(bf16[2,64,512]{2,1,0:T(8,128)(2,1)S(1)} %get-tuple-element.111), channel_id=1, source_target_pairs={{0,64},{1,65},{2,66},{3,67},{4,68},{5,69},{6,70},{7,71},{8,72},{9,... | collective-permute-start | bytes 393224 | tf_op jit(solution)/shard_map/ppermute | solution.py:51
  88.9 2.3 copy-start.4
  88.9 2.9 %collective-permute-start.32 = (bf16[2,64,512]{2,1,0:T(8,128)(2,1)S(1)}, bf16[2,64,512]{2,1,0:T(8,128)(2,1)S(1)}, u32[]{:S(2)}, u32[]{:S(2)}) collective-permute-start(bf16[2,64,512]{2,1,0:T(8,128)(2,1)S(1)} %get-tuple-element.160), channel_id=1, source_target_pairs={{64,128},{65,129},{66,130},{67,131},{68,132},{69,133},{70,134},{71... | collective-permute-start | bytes 393224 | tf_op jit(solution)/shard_map/ppermute | solution.py:51
  90.3 2.2 collective-permute-start.17
  91.2 2.1 collective-permute-start.19
  91.9 3.5 %collective-permute-start.33 = (bf16[2,64,512]{2,1,0:T(8,128)(2,1)S(1)}, bf16[2,64,512]{2,1,0:T(8,128)(2,1)S(1)}, u32[]{:S(2)}, u32[]{:S(2)}) collective-permute-start(bf16[2,64,512]{2,1,0:T(8,128)(2,1)S(1)} %get-tuple-element.161), channel_id=1, source_target_pairs={{128,192},{129,193},{130,194},{131,195},{132,196},{133,197},{134,1... | collective-permute-start | bytes 393224 | tf_op jit(solution)/shard_map/ppermute | solution.py:51
  92.6 3.5 %collective-permute-start.18 = (bf16[2,64,512]{2,1,0:T(8,128)(2,1)S(1)}, bf16[2,64,512]{2,1,0:T(8,128)(2,1)S(1)}, u32[]{:S(2)}, u32[]{:S(2)}) collective-permute-start(bf16[2,64,512]{2,1,0:T(8,128)(2,1)S(1)} %get-tuple-element.113), channel_id=1, source_target_pairs={{128,192},{129,193},{130,194},{131,195},{132,196},{133,197},{134,1... | collective-permute-start | bytes 393224 | tf_op jit(solution)/shard_map/ppermute | solution.py:51
  95.4 1.4 collective-permute-start.34
  96.1 1.4 collective-permute-start.20
  96.8 1.4 collective-permute-start.35
  97.5 2.0 collective-permute-start.21
  98.3 38.7 %collective-permute-start.36 = (bf16[2,64,512]{2,1,0:T(8,128)(2,1)S(1)}, bf16[2,64,512]{2,1,0:T(8,128)(2,1)S(1)}, u32[]{:S(2)}, u32[]{:S(2)}) collective-permute-start(bf16[2,64,512]{2,1,0:T(8,128)(2,1)S(1)} %get-tuple-element.174), channel_id=1, source_target_pairs={{64,0},{65,1},{66,2},{67,3},{68,4},{69,5},{70,6},{71,7},{72,8},{73... | collective-permute-start | bytes 393224 | tf_op jit(solution)/shard_map/ppermute | solution.py:51
  99.6 38.8 %collective-permute-start.22 = (bf16[2,64,512]{2,1,0:T(8,128)(2,1)S(1)}, bf16[2,64,512]{2,1,0:T(8,128)(2,1)S(1)}, u32[]{:S(2)}, u32[]{:S(2)}) collective-permute-start(bf16[2,64,512]{2,1,0:T(8,128)(2,1)S(1)} %get-tuple-element.130), channel_id=1, source_target_pairs={{64,0},{65,1},{66,2},{67,3},{68,4},{69,5},{70,6},{71,7},{72,8},{73... | collective-permute-start | bytes 393224 | tf_op jit(solution)/shard_map/ppermute | solution.py:51
  136.9 2.1 collective-permute-start.37
  138.3 1.4 collective-permute-start.23
  139.0 1.4 collective-permute-start.38
  139.7 1.4 collective-permute-start.24
  140.4 1.4 collective-permute-start.39
  141.1 2.0 collective-permute-start.25
  141.9 48.3 %collective-permute-start.40 = (bf16[2,64,512]{2,1,0:T(8,128)(2,1)S(1)}, bf16[2,64,512]{2,1,0:T(8,128)(2,1)S(1)}, u32[]{:S(2)}, u32[]{:S(2)}) collective-permute-start(bf16[2,64,512]{2,1,0:T(8,128)(2,1)S(1)} %get-tuple-element.190), channel_id=1, source_target_pairs={{64,0},{65,1},{66,2},{67,3},{68,4},{69,5},{70,6},{71,7},{72,8},{73... | collective-permute-start | bytes 393224 | tf_op jit(solution)/shard_map/ppermute | solution.py:51
  143.2 49.1 %collective-permute-start.26 = (bf16[2,64,512]{2,1,0:T(8,128)(2,1)S(1)}, bf16[2,64,512]{2,1,0:T(8,128)(2,1)S(1)}, u32[]{:S(2)}, u32[]{:S(2)}) collective-permute-start(bf16[2,64,512]{2,1,0:T(8,128)(2,1)S(1)} %get-tuple-element.145), channel_id=1, source_target_pairs={{64,0},{65,1},{66,2},{67,3},{68,4},{69,5},{70,6},{71,7},{72,8},{73... | collective-permute-start | bytes 393224 | tf_op jit(solution)/shard_map/ppermute | solution.py:51
  193.6 4.6 %collective-permute-start.41 = (bf16[256,2048]{1,0:T(8,128)(2,1)S(1)}, bf16[256,2048]{1,0:T(8,128)(2,1)S(1)}, u32[]{:S(2)}, u32[]{:S(2)}) collective-permute-start(bf16[256,2048]{1,0:T(8,128)(2,1)S(1)} %get-tuple-element.202), channel_id=1, source_target_pairs={{0,1},{1,0},{2,3},{3,2},{4,5},{5,4},{6,7},{7,6},{8,9},{9,8},{10,11... | collective-permute-start | bytes 3145736 | tf_op jit(solution)/shard_map/ppermute | solution.py:51
  218.8 20.1 %all-to-all-start.1 = ((bf16[8,8,2048]{2,1,0:T(8,128)(2,1)}), bf16[8,8,2048]{2,1,0:T(8,128)(2,1)S(1)}, u32[]{:S(2)}, u32[]{:S(2)}) async-start(bf16[8,8,2048]{2,1,0:T(8,128)(2,1)} %bitcast.10), calls=%async_computation.1 | async-start | bytes 524288 | tf_op jit(solution)/shard_map/all_to_all | solution.py:542

commit v3 on v2

--- a/solution.py
+++ b/solution.py
@@ -27,6 +27,7 @@
 UNROLL_DOWN = 2
 UNROLL_LAST = 2
 TURN_TICK = 3
+CROSS_TICK = 4
 TOKENS = 8192
 CHUNK = 1024
 CHUNKS = HIDDEN // CHUNK
@@ -81,24 +82,36 @@
 
 def up_from(section):
     def route(zh, x, b4, b2, b1, y, c):
-        if x != section % 4 or (x == 3 and zh == 1):
-            return None
-        if x == 3:
-            return (1, 0, 1 - b4, 1 - b2, 1 - b1, y, c)
-        return (zh, x + 1, b4, b2, b1, y, c)
+        return (zh, x + 1, b4, b2, b1, y, c) if x == section % 4 else None
 
     return route
 
 
 def down_from(section):
     def route(zh, x, b4, b2, b1, y, c):
-        if x != section % 4 or (x == 0 and zh == 0):
-            return None
-        if x == 0:
-            return (0, 3, 1 - b4, 1 - b2, 1 - b1, y, c)
-        return (zh, x - 1, b4, b2, b1, y, c)
+        return (zh, x - 1, b4, b2, b1, y, c) if x == section % 4 else None
 
     return route
+
+
+def up_across(zh, x, b4, b2, b1, y, c):
+    if (zh, x) != (0, 3):
+        return None
+    return (0, 0, b4, b2, b1, y, 1) if c else (1, 0, 1 - b4, 1 - b2, 1 - b1, y, 0)
+
+
+def up_relayed(zh, x, b4, b2, b1, y, c):
+    return (1, 0, 1 - b4, 1 - b2, 1 - b1, y, 1) if (zh, x, c) == (0, 0, 1) else None
+
+
+def down_across(zh, x, b4, b2, b1, y, c):
+    if (zh, x) != (1, 0):
+        return None
+    return (0, 3, 1 - b4, 1 - b2, 1 - b1, y, 1) if c else (1, 3, b4, b2, b1, y, 0)
+
+
+def down_relayed(zh, x, b4, b2, b1, y, c):
+    return (0, 3, 1 - b4, 1 - b2, 1 - b1, y, 0) if (zh, x, c) == (1, 3, 0) else None
 
 
 def doubled(block, route):
@@ -243,16 +256,16 @@
 
 def forward_kernel(tick, *refs):
     last = tick == LAYERS - 1
-    section, pair, own_in, other_in, probe, w_out, order = refs[:7]
-    refs = refs[7:]
+    section, own_in, other_in, probe, w_out, order = refs[:6]
+    pairs, refs = (refs[6:8], refs[8:]) if tick == CROSS_TICK else (refs[6:7], refs[7:])
     if last:
         goal, refs = refs[0], refs[1:]
     pair_out, norm, stat, slope_out, natural, lhs, acc = refs
 
     @pl.when(section[0] == tick)
     def _():
-        inflow = pair[0].astype(jnp.float32)
-        inflow_t = pair[1].astype(jnp.float32)
+        inflow = sum(pair[0].astype(jnp.float32) for pair in pairs)
+        inflow_t = sum(pair[1].astype(jnp.float32) for pair in pairs)
         centred = inflow - row_mean(inflow)
         rscale = lax.rsqrt(row_mean(centred * centred) + EPSILON)
         normed = centred * rscale
@@ -309,8 +322,8 @@
     )(section, inputs, opening_n, opening_t, order, own_in, other_in, w_out)
 
 
-def forward_call(tick, section, pair, own_in, other_in, probe, w_out, order, goal):
-    operands = [section, pair, own_in, other_in, probe, w_out, order] + ([goal] if tick == LAYERS - 1 else [])
+def forward_call(tick, section, pairs, own_in, other_in, probe, w_out, order, goal):
+    operands = [section, own_in, other_in, probe, w_out, order, *pairs] + ([goal] if tick == LAYERS - 1 else [])
     return pl.pallas_call(
         functools.partial(forward_kernel, tick),
         out_shape=[PAIR, NORM, STAT, SLOPE],
@@ -371,15 +384,23 @@
 
 def backward_kernel(tick, *refs):
     section, pair, w_in_t, probe_t, w_out_t, norm, stat, slope = refs[:8]
-    pair_out, grads, acc, acc_t = refs[8:]
+    refs = refs[8:]
+    if tick == CROSS_TICK:
+        other_pair, pair_out, grads, acc, acc_t, whole = refs
+    else:
+        pair_out, grads, acc, acc_t = refs
 
     @pl.when(section[0] == LAYERS - 1 - tick)
     def _():
+        adjoint = pair
+        if tick == CROSS_TICK:
+            adjoint = whole
+            whole[...] = (pair[...].astype(jnp.float32) + other_pair[...].astype(jnp.float32)).astype(jnp.bfloat16)
         acc[...] = jnp.zeros_like(acc)
         acc_t[...] = jnp.zeros_like(acc_t)
 
         def step(chunk, carry):
-            low_grad, low_grad_t = hidden_grads(pair, w_out_t, slope, chunk)
+            low_grad, low_grad_t = hidden_grads(adjoint, w_out_t, slope, chunk)
             both = jnp.concatenate([low_grad_t, low_grad], axis=0)
             grads[:, columns(chunk)] = both
             acc[...] += jnp.dot(both, w_in_t[columns(chunk), :], preferred_element_type=jnp.float32)
@@ -397,12 +418,13 @@
             - rscale * tangent_dot * through
             - rscale * (normed_t * row_mean(normed * grad_norm) + normed * row_mean(normed_t * grad_norm))
         )
-        pair_out[0] = (pair[0].astype(jnp.float32) + through).astype(jnp.bfloat16)
-        pair_out[1] = (pair[1].astype(jnp.float32) + through_t).astype(jnp.bfloat16)
-
-
-def backward_call(tick, section, pair, w_in_t, probe_t, w_out_t, kept):
-    operands = [section, pair, w_in_t, probe_t, w_out_t, *kept]
+        pair_out[0] = (adjoint[0].astype(jnp.float32) + through).astype(jnp.bfloat16)
+        pair_out[1] = (adjoint[1].astype(jnp.float32) + through_t).astype(jnp.bfloat16)
+
+
+def backward_call(tick, section, pairs, w_in_t, probe_t, w_out_t, kept):
+    operands = [section, pairs[0], w_in_t, probe_t, w_out_t, *kept, *pairs[1:]]
+    whole = [pltpu.VMEM(PAIR.shape, PAIR.dtype)] if tick == CROSS_TICK else []
     return pl.pallas_call(
         functools.partial(backward_kernel, tick),
         out_shape=[PAIR, GRADS],
@@ -411,6 +433,7 @@
         scratch_shapes=[
             pltpu.VMEM((2 * ROWS, FEATURES), jnp.float32),
             pltpu.VMEM((ROWS, FEATURES), jnp.float32),
+            *whole,
         ],
         compiler_params=PARAMS,
         name=f"layer_down_{tick}",
@@ -494,10 +517,10 @@
 def shards(inputs, targets, w_in, w_out, probes):
     place = [jnp.reshape(lax.axis_index(name), (1,)).astype(jnp.int32) for name in (*DP, SECTION)]
     section = place[-1]
-    out_block = settled_call(place, w_out[0])
+    in_block = settled_call(place, w_in[0])
     probe = probes[0]
-    own_in, other_in = gathered(w_in[0], True)
-    full_out = placed_call(place, *gathered(out_block, False))
+    own_in, other_in = gathered(in_block, True)
+    full_out = placed_call(place, *gathered(w_out[0], False))
     order, curvature_order, opening_n, opening_t = opening_call(place, inputs, probe)
     goal = routed(targets, goal_route)
     pairs, slopes, kept, grads = [None] * MICRO, [], [], []
@@ -507,32 +530,36 @@
     for tick in range(LAYERS):
         for micro in range(MICRO):
             if tick == 0:
-                pairs[micro], slope = first_call(
+                pair, slope = first_call(
                     micro, section, inputs, opening_n, opening_t, order, own_in, other_in, full_out
                 )
                 slopes.append(slope)
             else:
                 goal_now = goal[micro * ROWS : (micro + 1) * ROWS]
-                pairs[micro], *stores = forward_call(
+                pair, *stores = forward_call(
                     tick, section, pairs[micro], own_in, other_in, probe, full_out, order, goal_now
                 )
                 kept[micro].append(stores)
             if tick < LAYERS - 1:
-                pairs[micro] = routed(pairs[micro], up_from(tick))
+                pairs[micro] = [routed(pair, up_across if tick + 1 == CROSS_TICK else up_from(tick))]
+            else:
+                pairs[micro] = [pair]
+            if tick + 1 == CROSS_TICK:
+                pairs[micro].append(routed(pairs[micro][0], up_relayed))
         if tick == TURN_TICK:
             turned = turned_call(own_in, other_in, probe, full_out, order, kept[-1][-1][0])
     for tick in range(LAYERS - 1):
         for micro in range(MICRO):
-            pairs[micro], low_grads = backward_call(
-                tick, section, pairs[micro], *turned, kept[micro][LAYERS - 2 - tick]
-            )
+            pair, low_grads = backward_call(tick, section, pairs[micro], *turned, kept[micro][LAYERS - 2 - tick])
             grads[micro].append(low_grads)
-            pairs[micro] = routed(pairs[micro], down_from(LAYERS - 1 - tick))
+            pairs[micro] = [routed(pair, down_across if tick + 1 == CROSS_TICK else down_from(LAYERS - 1 - tick))]
+            if tick + 1 == CROSS_TICK:
+                pairs[micro].append(routed(pairs[micro][0], down_relayed))
     sums = ()
     for micro in range(MICRO):
         norms = [stores[0] for stores in kept[micro]]
         sums = curvature_call(
-            micro, section, pairs[micro], turned[2], slopes[micro], curvature_order, opening_n, norms, grads[micro], sums
+            micro, section, pairs[micro][0], turned[2], slopes[micro], curvature_order, opening_n, norms, grads[micro], sums
         )
     away, stay = sums
     other = routed(away, swap_core)

time: 241 us -> 245 us (1.017)
  starting transfers between devices: 85.3 us -> 89.2 us
    all_to_all x1, starting transfers between devices: 4.58 us -> 7.41 us  [shards(): lax.all_to_all(summed.reshape(8, 8, HIDDEN), ('b1', 'b2', 'b4'), 0, 0, ti...]
    ppermute x42 -> x46, waiting for transfers between devices: 104 us -> 103 us  [routed(): return lax.ppermute(value, NAMES, pairs)]
    ppermute x42 -> x46, starting transfers between devices: 80.8 us -> 81.8 us  [routed(): return lax.ppermute(value, NAMES, pairs)]
  transfers between devices with their start and end apart: 43 -> 47, of which waited for: 18 -> 17; matrix products, arithmetic and copies ran while one was open for 1% -> 1% of each run, Pallas kernels for 3% -> 3%
where the time goes in v3:
time: 245 us; the launch traced here: 243 us
  waiting for transfers between devices  119 us (49%)
  starting transfers between devices  89.2 us (36%)
  blocking collectives  19.5 us (8%)
  Pallas kernels  8.94 us (4%)
  other arithmetic  4.26 us (2%)
    ppermute x46, waiting for transfers between devices, routed(): return lax.ppermute(value, NAMES, pairs)  103 us
    ppermute x46, starting transfers between devices, routed(): return lax.ppermute(value, NAMES, pairs)  81.8 us
    all_to_all x1, blocking collectives, shards(): lax.all_to_all(summed.reshape(4, 64, HIDDEN), 'y', 0, 0, tiled=True)  19.5 us
    all_to_all x1, waiting for transfers between devices, shards(): lax.all_to_all(summed.reshape(8, 8, HIDDEN), ('b1', 'b2', 'b4'), 0, 0, ti...  16.2 us
    all_to_all x1, starting transfers between devices, shards(): lax.all_to_all(summed.reshape(8, 8, HIDDEN), ('b1', 'b2', 'b4'), 0, 0, ti...  7.41 us
  transfers between devices with their start and end apart: 47, of which 17 were waited for; matrix products, arithmetic and copies ran while one was open for 1% of the time, Pallas kernels for 3%

profile of v3, /device:TPU:8, one launch (start us, length us, event | category | flops | bytes accessed | tf_op | source)
XLA Modules:
  0.0 243.3 jit_solution(4296386079781627944)
XLA Ops:
  0.0 9.1 %collective-permute-start.6 = (bf16[32,512]{1,0:T(8,128)(2,1)}, bf16[32,512]{1,0:T(8,128)(2,1)S(1)}, u32[]{:S(2)}, u32[]{:S(2)}) collective-permute-start(bf16[32,512]{1,0:T(8,128)(2,1)} %bitcast.33), channel_id=1, source_target_pairs={{0,32},{1,33},{2,34},{3,35},{4,36},{5,37},{6,38},{7,39},{8,40},{9,... | collective-permute-start | bytes 98312 | tf_op jit(solution)/shard_map/ppermute | solution.py:52
  9.9 1.9 collective-permute-start
  13.3 5.2 %collective-permute-start.7 = (bf16[64,512]{1,0:T(8,128)(2,1)S(1)}, bf16[64,512]{1,0:T(8,128)(2,1)S(1)}, u32[]{:S(2)}, u32[]{:S(2)}) collective-permute-start(bf16[64,512]{1,0:T(8,128)(2,1)S(1)} %pad_maximum_fusion.5), channel_id=1, source_target_pairs={{0,16},{1,17},{2,18},{3,19},{4,20},{5,21},{6,22},{7,23},{8,24},{9,... | collective-permute-start | bytes 196616 | tf_op jit(solution)/shard_map/ppermute | solution.py:52
  18.5 1.5 collective-permute-done
  20.0 5.2 %collective-permute-start.1 = (bf16[16,2048]{1,0:T(8,128)(2,1)S(1)}, bf16[16,2048]{1,0:T(8,128)(2,1)S(1)}, u32[]{:S(2)}, u32[]{:S(2)}) collective-permute-start(bf16[16,2048]{1,0:T(8,128)(2,1)S(1)} %pad_maximum_fusion.4), channel_id=1, source_target_pairs={{0,16},{1,17},{2,18},{3,19},{4,20},{5,21},{6,22},{7,23},{8,24},{9,... | collective-permute-start | bytes 196616 | tf_op jit(solution)/shard_map/ppermute | solution.py:52
  25.2 0.8 pad_maximum_fusion.3
  26.0 3.4 %collective-permute-start.8 = (bf16[128,512]{1,0:T(8,128)(2,1)S(1)}, bf16[128,512]{1,0:T(8,128)(2,1)S(1)}, u32[]{:S(2)}, u32[]{:S(2)}) collective-permute-start(bf16[128,512]{1,0:T(8,128)(2,1)S(1)} %pad_maximum_fusion.3), channel_id=1, source_target_pairs={{0,8},{1,9},{2,10},{3,11},{4,12},{5,13},{6,14},{7,15},{8,0},{9,1},... | collective-permute-start | bytes 393224 | tf_op jit(solution)/shard_map/ppermute | solution.py:52
  29.4 2.4 collective-permute-start.2
  31.9 2.0 collective-permute-done.8
  33.9 0.8 pad_maximum_fusion.1
  34.7 3.5 %collective-permute-start.9 = (bf16[256,512]{1,0:T(8,128)(2,1)S(1)}, bf16[256,512]{1,0:T(8,128)(2,1)S(1)}, u32[]{:S(2)}, u32[]{:S(2)}) collective-permute-start(bf16[256,512]{1,0:T(8,128)(2,1)S(1)} %pad_maximum_fusion.1), channel_id=1, source_target_pairs={{0,6},{1,7},{2,4},{3,5},{4,2},{5,3},{6,0},{7,1},{8,14},{9,15},{10,... | collective-permute-start | bytes 786440 | tf_op jit(solution)/shard_map/ppermute | solution.py:52
  38.3 3.8 %collective-permute-start.3 = (bf16[64,2048]{1,0:T(8,128)(2,1)S(1)}, bf16[64,2048]{1,0:T(8,128)(2,1)S(1)}, u32[]{:S(2)}, u32[]{:S(2)}) collective-permute-start(bf16[64,2048]{1,0:T(8,128)(2,1)S(1)} %pad_maximum_fusion), channel_id=1, source_target_pairs={{0,2},{1,3},{2,0},{3,1},{4,6},{5,7},{6,4},{7,5},{8,10},{9,11},{10,... | collective-permute-start | bytes 786440 | tf_op jit(solution)/shard_map/ppermute | solution.py:52
  42.1 0.9 collective-permute-done.9
  43.0 3.6 %collective-permute-start.10 = (bf16[512,512]{1,0:T(8,128)(2,1)S(1)}, bf16[512,512]{1,0:T(8,128)(2,1)S(1)}, u32[]{:S(2)}, u32[]{:S(2)}) collective-permute-start(bf16[512,512]{1,0:T(8,128)(2,1)S(1)} %get-tuple-element.203), channel_id=1, source_target_pairs={{0,2},{1,3},{2,0},{3,1},{4,6},{5,7},{6,4},{7,5},{8,10},{9,11},{10,... | collective-permute-start | bytes 1572872 | tf_op jit(solution)/shard_map/ppermute | solution.py:52
  46.6 2.8 %collective-permute-done.3 = bf16[64,2048]{1,0:T(8,128)(2,1)S(1)} collective-permute-done((bf16[64,2048]{1,0:T(8,128)(2,1)S(1)}, bf16[64,2048]{1,0:T(8,128)(2,1)S(1)}, u32[]{:S(2)}, u32[]{:S(2)}) %collective-permute-start.3) | collective-permute-done | bytes 262176 | tf_op jit(solution)/shard_map/ppermute | solution.py:52
  49.4 2.1 collective-permute-start.4
  51.5 4.7 %collective-permute-done.10 = bf16[512,512]{1,0:T(8,128)(2,1)S(1)} collective-permute-done((bf16[512,512]{1,0:T(8,128)(2,1)S(1)}, bf16[512,512]{1,0:T(8,128)(2,1)S(1)}, u32[]{:S(2)}, u32[]{:S(2)}) %collective-permute-start.10) | collective-permute-done | bytes 524320 | tf_op jit(solution)/shard_map/ppermute | solution.py:52
  56.3 1.9 collective-permute-start.11
  58.2 2.3 collective-permute-done.4
  60.6 1.9 collective-permute-start.5
  62.5 1.3 opening.1
  64.0 1.1 collective-permute-done.5.other_in.refs_2_
  65.1 1.2 layer_up_0.3
  66.3 2.2 collective-permute-start.29
  68.5 1.2 layer_up_0.2
  69.7 1.3 collective-permute-start.12
  72.4 1.9 collective-permute-done.12.refs_6_
  79.3 9.2 %collective-permute-start.34 = (bf16[2,64,512]{2,1,0:T(8,128)(2,1)S(1)}, bf16[2,64,512]{2,1,0:T(8,128)(2,1)S(1)}, u32[]{:S(2)}, u32[]{:S(2)}) collective-permute-start(bf16[2,64,512]{2,1,0:T(8,128)(2,1)S(1)} %get-tuple-element.159), channel_id=1, source_target_pairs={{0,64},{1,65},{2,66},{3,67},{4,68},{5,69},{6,70},{7,71},{8,72},{9,... | collective-permute-start | bytes 393224 | tf_op jit(solution)/shard_map/ppermute | solution.py:52
  88.5 1.3 collective-permute-start.17
  89.8 1.2 collective-permute-done.34.refs_6_
  91.0 0.8 collective-permute-start.35
  95.1 2.0 turned_weights.1
  100.1 1.3 collective-permute-start.39
  101.4 1.3 collective-permute-start.23
  102.7 29.0 %collective-permute-done.39.refs_1_ = bf16[2,64,512]{2,1,0:T(8,128)(2,1)S(1)} collective-permute-done((bf16[2,64,512]{2,1,0:T(8,128)(2,1)S(1)}, bf16[2,64,512]{2,1,0:T(8,128)(2,1)S(1)}, u32[]{:S(2)}, u32[]{:S(2)}) %collective-permute-start.39) | collective-permute-done | bytes 131104 | tf_op jit(solution)/shard_map/ppermute | solution.py:52
  132.3 4.8 %collective-permute-done.23.refs_1_ = bf16[2,64,512]{2,1,0:T(8,128)(2,1)S(1)} collective-permute-done((bf16[2,64,512]{2,1,0:T(8,128)(2,1)S(1)}, bf16[2,64,512]{2,1,0:T(8,128)(2,1)S(1)}, u32[]{:S(2)}, u32[]{:S(2)}) %collective-permute-start.23) | collective-permute-done | bytes 131104 | tf_op jit(solution)/shard_map/ppermute | solution.py:52
  142.1 1.3 collective-permute-start.44
  143.4 1.3 collective-permute-start.28
  144.7 45.1 %collective-permute-done.44.refs_1_ = bf16[2,64,512]{2,1,0:T(8,128)(2,1)S(1)} collective-permute-done((bf16[2,64,512]{2,1,0:T(8,128)(2,1)S(1)}, bf16[2,64,512]{2,1,0:T(8,128)(2,1)S(1)}, u32[]{:S(2)}, u32[]{:S(2)}) %collective-permute-start.44) | collective-permute-done | bytes 131104 | tf_op jit(solution)/shard_map/ppermute | solution.py:52
  189.8 1.4 curvature_first.1
  191.1 1.3 collective-permute-done.28.refs_1_
  192.4 1.4 curvature_last.1
  193.8 1.9 collective-permute-start.45
  195.7 2.6 %collective-permute-done.45 = bf16[256,2048]{1,0:T(8,128)(2,1)S(1)} collective-permute-done((bf16[256,2048]{1,0:T(8,128)(2,1)S(1)}, bf16[256,2048]{1,0:T(8,128)(2,1)S(1)}, u32[]{:S(2)}, u32[]{:S(2)}) %collective-permute-start.45) | collective-permute-done | bytes 1048608 | tf_op jit(solution)/shard_map/ppermute | solution.py:52
  198.7 19.5 %all_to_all.10 = bf16[4,64,2048]{2,1,0:T(8,128)(2,1)S(1)} all-to-all(bf16[4,64,2048]{2,1,0:T(8,128)(2,1)S(1)} %bitcast.32), channel_id=1, replica_groups=mesh['zh'=2,'x'=4,'b4'=2,'b2'=2,'b1'=2,'y'=4,'c'=2] {'y'}, dimensions={0} | all-to-all | bytes 2097152 | tf_op jit(solution)/shard_map/all_to_all | solution.py:567
  218.2 0.9 reduce_sum.23
  219.1 7.4 %all-to-all-start.1 = ((bf16[8,8,2048]{2,1,0:T(8,128)(2,1)}), bf16[8,8,2048]{2,1,0:T(8,128)(2,1)S(1)}, u32[]{:S(2)}, u32[]{:S(2)}) async-start(bf16[8,8,2048]{2,1,0:T(8,128)(2,1)} %bitcast.10), calls=%async_computation.1 | async-start | bytes 524288 | tf_op jit(solution)/shard_map/all_to_all | solution.py:569
  226.5 16.2 %all-to-all-done.1 = bf16[8,8,2048]{2,1,0:T(8,128)(2,1)S(1)} async-done(((bf16[8,8,2048]{2,1,0:T(8,128)(2,1)}), bf16[8,8,2048]{2,1,0:T(8,128)(2,1)S(1)}, u32[]{:S(2)}, u32[]{:S(2)}) %all-to-all-start.1) | async-done | bytes 262176 | tf_op jit(solution)/shard_map/all_to_all | solution.py:569
  (114 shorter events, 21.5 us)
Async XLA Ops:
  0.0 12.6 %collective-permute-start.6 = (bf16[32,512]{1,0:T(8,128)(2,1)}, bf16[32,512]{1,0:T(8,128)(2,1)S(1)}, u32[]{:S(2)}, u32[]{:S(2)}) collective-permute-start(bf16[32,512]{1,0:T(8,128)(2,1)} %bitcast.33), channel_id=1, source_target_pairs={{0,32},{1,33},{2,34},{3,35},{4,36},{5,37},{6,38},{7,39},{8,40},{9,... | collective-permute-start | bytes 98312 | tf_op jit(solution)/shard_map/ppermute | solution.py:52
  9.9 10.1 %collective-permute-start = (bf16[8,2048]{1,0:T(8,128)(2,1)S(1)}, bf16[8,2048]{1,0:T(8,128)(2,1)S(1)}, u32[]{:S(2)}, u32[]{:S(2)}) collective-permute-start(bf16[8,2048]{1,0:T(8,128)(2,1)S(1)} %settled.1), channel_id=1, source_target_pairs={{0,32},{1,33},{2,34},{3,35},{4,36},{5,37},{6,38},{7,39},{8,40},{9,... | collective-permute-start | bytes 98312 | tf_op jit(solution)/shard_map/ppermute | solution.py:52
  13.3 11.8 %collective-permute-start.7 = (bf16[64,512]{1,0:T(8,128)(2,1)S(1)}, bf16[64,512]{1,0:T(8,128)(2,1)S(1)}, u32[]{:S(2)}, u32[]{:S(2)}) collective-permute-start(bf16[64,512]{1,0:T(8,128)(2,1)S(1)} %pad_maximum_fusion.5), channel_id=1, source_target_pairs={{0,16},{1,17},{2,18},{3,19},{4,20},{5,21},{6,22},{7,23},{8,24},{9,... | collective-permute-start | bytes 196616 | tf_op jit(solution)/shard_map/ppermute | solution.py:52
  20.0 9.4 %collective-permute-start.1 = (bf16[16,2048]{1,0:T(8,128)(2,1)S(1)}, bf16[16,2048]{1,0:T(8,128)(2,1)S(1)}, u32[]{:S(2)}, u32[]{:S(2)}) collective-permute-start(bf16[16,2048]{1,0:T(8,128)(2,1)S(1)} %pad_maximum_fusion.4), channel_id=1, source_target_pairs={{0,16},{1,17},{2,18},{3,19},{4,20},{5,21},{6,22},{7,23},{8,24},{9,... | collective-permute-start | bytes 196616 | tf_op jit(solution)/shard_map/ppermute | solution.py:52
  26.0 8.0 %collective-permute-start.8 = (bf16[128,512]{1,0:T(8,128)(2,1)S(1)}, bf16[128,512]{1,0:T(8,128)(2,1)S(1)}, u32[]{:S(2)}, u32[]{:S(2)}) collective-permute-start(bf16[128,512]{1,0:T(8,128)(2,1)S(1)} %pad_maximum_fusion.3), channel_id=1, source_target_pairs={{0,8},{1,9},{2,10},{3,11},{4,12},{5,13},{6,14},{7,15},{8,0},{9,1},... | collective-permute-start | bytes 393224 | tf_op jit(solution)/shard_map/ppermute | solution.py:52
  29.4 8.8 %collective-permute-start.2 = (bf16[32,2048]{1,0:T(8,128)(2,1)S(1)}, bf16[32,2048]{1,0:T(8,128)(2,1)S(1)}, u32[]{:S(2)}, u32[]{:S(2)}) collective-permute-start(bf16[32,2048]{1,0:T(8,128)(2,1)S(1)} %pad_maximum_fusion.2), channel_id=1, source_target_pairs={{0,8},{1,9},{2,10},{3,11},{4,12},{5,13},{6,14},{7,15},{8,0},{9,1},... | collective-permute-start | bytes 393224 | tf_op jit(solution)/shard_map/ppermute | solution.py:52
  34.7 8.3 %collective-permute-start.9 = (bf16[256,512]{1,0:T(8,128)(2,1)S(1)}, bf16[256,512]{1,0:T(8,128)(2,1)S(1)}, u32[]{:S(2)}, u32[]{:S(2)}) collective-permute-start(bf16[256,512]{1,0:T(8,128)(2,1)S(1)} %pad_maximum_fusion.1), channel_id=1, source_target_pairs={{0,6},{1,7},{2,4},{3,5},{4,2},{5,3},{6,0},{7,1},{8,14},{9,15},{10,... | collective-permute-start | bytes 786440 | tf_op jit(solution)/shard_map/ppermute | solution.py:52
  38.3 11.1 %collective-permute-start.3 = (bf16[64,2048]{1,0:T(8,128)(2,1)S(1)}, bf16[64,2048]{1,0:T(8,128)(2,1)S(1)}, u32[]{:S(2)}, u32[]{:S(2)}) collective-permute-start(bf16[64,2048]{1,0:T(8,128)(2,1)S(1)} %pad_maximum_fusion), channel_id=1, source_target_pairs={{0,2},{1,3},{2,0},{3,1},{4,6},{5,7},{6,4},{7,5},{8,10},{9,11},{10,... | collective-permute-start | bytes 786440 | tf_op jit(solution)/shard_map/ppermute | solution.py:52
  42.1 20.4 %copy-start = (bf16[1,512,2048]{2,1,0:T(8,128)(2,1)S(1)}, bf16[1,512,2048]{2,1,0:T(8,128)(2,1)}, u32[]{:S(2)}) copy-start(bf16[1,512,2048]{2,1,0:T(8,128)(2,1)} %param.9) | copy-start | bytes 6291460
  43.0 13.2 %collective-permute-start.10 = (bf16[512,512]{1,0:T(8,128)(2,1)S(1)}, bf16[512,512]{1,0:T(8,128)(2,1)S(1)}, u32[]{:S(2)}, u32[]{:S(2)}) collective-permute-start(bf16[512,512]{1,0:T(8,128)(2,1)S(1)} %get-tuple-element.203), channel_id=1, source_target_pairs={{0,2},{1,3},{2,0},{3,1},{4,6},{5,7},{6,4},{7,5},{8,10},{9,11},{10,... | collective-permute-start | bytes 1572872 | tf_op jit(solution)/shard_map/ppermute | solution.py:52
  49.4 11.1 %collective-permute-start.4 = (bf16[128,2048]{1,0:T(8,128)(2,1)S(1)}, bf16[128,2048]{1,0:T(8,128)(2,1)S(1)}, u32[]{:S(2)}, u32[]{:S(2)}) collective-permute-start(bf16[128,2048]{1,0:T(8,128)(2,1)S(1)} %get-tuple-element.205), channel_id=1, source_target_pairs={{0,6},{1,7},{2,4},{3,5},{4,2},{5,3},{6,0},{7,1},{8,14},{9,15},{10,... | collective-permute-start | bytes 1572872 | tf_op jit(solution)/shard_map/ppermute | solution.py:52
  56.3 7.5 %collective-permute-start.11 = (bf16[1024,512]{1,0:T(8,128)(2,1)S(1)}, bf16[1024,512]{1,0:T(8,128)(2,1)S(1)}, u32[]{:S(2)}, u32[]{:S(2)}) collective-permute-start(bf16[1024,512]{1,0:T(8,128)(2,1)S(1)} %constant_dynamic-update-slice_fusion.16.refs_6_), channel_id=1, source_target_pairs={{0,1},{1,0},{2,3},{3,2},{4,5},{5,4},{6,7},{7,6},{8,9},{9,8},{10,11... | collective-permute-start | bytes 3145736 | tf_op jit(solution)/shard_map/ppermute | solution.py:52
  60.6 4.6 %collective-permute-start.5 = (bf16[256,2048]{1,0:T(8,128)(2,1)S(1)}, bf16[256,2048]{1,0:T(8,128)(2,1)S(1)}, u32[]{:S(2)}, u32[]{:S(2)}) collective-permute-start(bf16[256,2048]{1,0:T(8,128)(2,1)S(1)} %constant_dynamic-update-slice_fusion.5.own_in.refs_1_), channel_id=1, source_target_pairs={{0,1},{1,0},{2,3},{3,2},{4,5},{5,4},{6,7},{7,6},{8,9},{9,8},{10,11... | collective-permute-start | bytes 3145736 | tf_op jit(solution)/shard_map/ppermute | solution.py:52
  66.3 5.4 %collective-permute-start.29 = (bf16[2,64,512]{2,1,0:T(8,128)(2,1)S(1)}, bf16[2,64,512]{2,1,0:T(8,128)(2,1)S(1)}, u32[]{:S(2)}, u32[]{:S(2)}) collective-permute-start(bf16[2,64,512]{2,1,0:T(8,128)(2,1)S(1)} %get-tuple-element.155), channel_id=1, source_target_pairs={{0,64},{1,65},{2,66},{3,67},{4,68},{5,69},{6,70},{7,71},{8,72},{9,... | collective-permute-start | bytes 393224 | tf_op jit(solution)/shard_map/ppermute | solution.py:52
  69.7 4.6 %collective-permute-start.12 = (bf16[2,64,512]{2,1,0:T(8,128)(2,1)S(1)}, bf16[2,64,512]{2,1,0:T(8,128)(2,1)S(1)}, u32[]{:S(2)}, u32[]{:S(2)}) collective-permute-start(bf16[2,64,512]{2,1,0:T(8,128)(2,1)S(1)} %get-tuple-element.107), channel_id=1, source_target_pairs={{0,64},{1,65},{2,66},{3,67},{4,68},{5,69},{6,70},{7,71},{8,72},{9,... | collective-permute-start | bytes 393224 | tf_op jit(solution)/shard_map/ppermute | solution.py:52
  71.8 3.3 %collective-permute-start.30 = (bf16[2,64,512]{2,1,0:T(8,128)(2,1)S(1)}, bf16[2,64,512]{2,1,0:T(8,128)(2,1)S(1)}, u32[]{:S(2)}, u32[]{:S(2)}) collective-permute-start(bf16[2,64,512]{2,1,0:T(8,128)(2,1)S(1)} %get-tuple-element.156), channel_id=1, source_target_pairs={{64,128},{65,129},{66,130},{67,131},{68,132},{69,133},{70,134},{71... | collective-permute-start | bytes 393224 | tf_op jit(solution)/shard_map/ppermute | solution.py:52
  74.4 1.4 collective-permute-start.13
  75.1 1.4 collective-permute-start.31
  75.8 1.4 collective-permute-start.14
  76.5 1.4 collective-permute-start.32
  77.2 1.4 collective-permute-start.15
  77.9 1.4 collective-permute-start.33
  78.6 9.9 %collective-permute-start.16 = (bf16[2,64,512]{2,1,0:T(8,128)(2,1)S(1)}, bf16[2,64,512]{2,1,0:T(8,128)(2,1)S(1)}, u32[]{:S(2)}, u32[]{:S(2)}) collective-permute-start(bf16[2,64,512]{2,1,0:T(8,128)(2,1)S(1)} %collective-permute-done.15.refs_6_), channel_id=1, source_target_pairs={{1,313},{3,315},{5,317},{7,319},{9,305},{11,307},{13,309},{15,311}... | collective-permute-start | bytes 393224 | tf_op jit(solution)/shard_map/ppermute | solution.py:52
  79.3 11.7 %collective-permute-start.34 = (bf16[2,64,512]{2,1,0:T(8,128)(2,1)S(1)}, bf16[2,64,512]{2,1,0:T(8,128)(2,1)S(1)}, u32[]{:S(2)}, u32[]{:S(2)}) collective-permute-start(bf16[2,64,512]{2,1,0:T(8,128)(2,1)S(1)} %get-tuple-element.159), channel_id=1, source_target_pairs={{0,64},{1,65},{2,66},{3,67},{4,68},{5,69},{6,70},{7,71},{8,72},{9,... | collective-permute-start | bytes 393224 | tf_op jit(solution)/shard_map/ppermute | solution.py:52
  88.5 3.8 %collective-permute-start.17 = (bf16[2,64,512]{2,1,0:T(8,128)(2,1)S(1)}, bf16[2,64,512]{2,1,0:T(8,128)(2,1)S(1)}, u32[]{:S(2)}, u32[]{:S(2)}) collective-permute-start(bf16[2,64,512]{2,1,0:T(8,128)(2,1)S(1)} %get-tuple-element.111), channel_id=1, source_target_pairs={{0,64},{1,65},{2,66},{3,67},{4,68},{5,69},{6,70},{7,71},{8,72},{9,... | collective-permute-start | bytes 393224 | tf_op jit(solution)/shard_map/ppermute | solution.py:52
  91.0 2.7 %collective-permute-start.35 = (bf16[2,64,512]{2,1,0:T(8,128)(2,1)S(1)}, bf16[2,64,512]{2,1,0:T(8,128)(2,1)S(1)}, u32[]{:S(2)}, u32[]{:S(2)}) collective-permute-start(bf16[2,64,512]{2,1,0:T(8,128)(2,1)S(1)} %get-tuple-element.160), channel_id=1, source_target_pairs={{64,128},{65,129},{66,130},{67,131},{68,132},{69,133},{70,134},{71... | collective-permute-start | bytes 393224 | tf_op jit(solution)/shard_map/ppermute | solution.py:52
  92.3 2.1 collective-permute-start.18
  93.0 2.1 collective-permute-start.20
  93.7 3.5 %collective-permute-start.36 = (bf16[2,64,512]{2,1,0:T(8,128)(2,1)S(1)}, bf16[2,64,512]{2,1,0:T(8,128)(2,1)S(1)}, u32[]{:S(2)}, u32[]{:S(2)}) collective-permute-start(bf16[2,64,512]{2,1,0:T(8,128)(2,1)S(1)} %get-tuple-element.161), channel_id=1, source_target_pairs={{128,192},{129,193},{130,194},{131,195},{132,196},{133,197},{134,1... | collective-permute-start | bytes 393224 | tf_op jit(solution)/shard_map/ppermute | solution.py:52
  94.4 3.5 %collective-permute-start.19 = (bf16[2,64,512]{2,1,0:T(8,128)(2,1)S(1)}, bf16[2,64,512]{2,1,0:T(8,128)(2,1)S(1)}, u32[]{:S(2)}, u32[]{:S(2)}) collective-permute-start(bf16[2,64,512]{2,1,0:T(8,128)(2,1)S(1)} %get-tuple-element.113), channel_id=1, source_target_pairs={{128,192},{129,193},{130,194},{131,195},{132,196},{133,197},{134,1... | collective-permute-start | bytes 393224 | tf_op jit(solution)/shard_map/ppermute | solution.py:52
  97.2 1.4 collective-permute-start.37
  97.9 1.4 collective-permute-start.21
  98.6 1.4 collective-permute-start.38
  99.4 2.0 collective-permute-start.22
  100.1 31.6 %collective-permute-start.39 = (bf16[2,64,512]{2,1,0:T(8,128)(2,1)S(1)}, bf16[2,64,512]{2,1,0:T(8,128)(2,1)S(1)}, u32[]{:S(2)}, u32[]{:S(2)}) collective-permute-start(bf16[2,64,512]{2,1,0:T(8,128)(2,1)S(1)} %get-tuple-element.174), channel_id=1, source_target_pairs={{64,0},{65,1},{66,2},{67,3},{68,4},{69,5},{70,6},{71,7},{72,8},{73... | collective-permute-start | bytes 393224 | tf_op jit(solution)/shard_map/ppermute | solution.py:52
  101.4 35.8 %collective-permute-start.23 = (bf16[2,64,512]{2,1,0:T(8,128)(2,1)S(1)}, bf16[2,64,512]{2,1,0:T(8,128)(2,1)S(1)}, u32[]{:S(2)}, u32[]{:S(2)}) collective-permute-start(bf16[2,64,512]{2,1,0:T(8,128)(2,1)S(1)} %get-tuple-element.130), channel_id=1, source_target_pairs={{64,0},{65,1},{66,2},{67,3},{68,4},{69,5},{70,6},{71,7},{72,8},{73... | collective-permute-start | bytes 393224 | tf_op jit(solution)/shard_map/ppermute | solution.py:52
  131.7 6.2 %collective-permute-start.40 = (bf16[2,64,512]{2,1,0:T(8,128)(2,1)S(1)}, bf16[2,64,512]{2,1,0:T(8,128)(2,1)S(1)}, u32[]{:S(2)}, u32[]{:S(2)}) collective-permute-start(bf16[2,64,512]{2,1,0:T(8,128)(2,1)S(1)} %get-tuple-element.178), channel_id=1, source_target_pairs={{256,448},{257,249},{258,450},{259,251},{260,452},{261,253},{262,4... | collective-permute-start | bytes 393224 | tf_op jit(solution)/shard_map/ppermute | solution.py:52
  137.2 1.4 collective-permute-start.24
  137.8 1.4 collective-permute-start.41
  138.5 1.4 collective-permute-start.25
  139.2 1.4 collective-permute-start.42
  139.9 1.4 collective-permute-start.26
  140.7 1.4 collective-permute-start.43
  141.4 2.0 collective-permute-start.27
  142.1 47.7 %collective-permute-start.44 = (bf16[2,64,512]{2,1,0:T(8,128)(2,1)S(1)}, bf16[2,64,512]{2,1,0:T(8,128)(2,1)S(1)}, u32[]{:S(2)}, u32[]{:S(2)}) collective-permute-start(bf16[2,64,512]{2,1,0:T(8,128)(2,1)S(1)} %get-tuple-element.190), channel_id=1, source_target_pairs={{64,0},{65,1},{66,2},{67,3},{68,4},{69,5},{70,6},{71,7},{72,8},{73... | collective-permute-start | bytes 393224 | tf_op jit(solution)/shard_map/ppermute | solution.py:52
  143.4 49.0 %collective-permute-start.28 = (bf16[2,64,512]{2,1,0:T(8,128)(2,1)S(1)}, bf16[2,64,512]{2,1,0:T(8,128)(2,1)S(1)}, u32[]{:S(2)}, u32[]{:S(2)}) collective-permute-start(bf16[2,64,512]{2,1,0:T(8,128)(2,1)S(1)} %get-tuple-element.145), channel_id=1, source_target_pairs={{64,0},{65,1},{66,2},{67,3},{68,4},{69,5},{70,6},{71,7},{72,8},{73... | collective-permute-start | bytes 393224 | tf_op jit(solution)/shard_map/ppermute | solution.py:52
  193.8 4.6 %collective-permute-start.45 = (bf16[256,2048]{1,0:T(8,128)(2,1)S(1)}, bf16[256,2048]{1,0:T(8,128)(2,1)S(1)}, u32[]{:S(2)}, u32[]{:S(2)}) collective-permute-start(bf16[256,2048]{1,0:T(8,128)(2,1)S(1)} %get-tuple-element.202), channel_id=1, source_target_pairs={{0,1},{1,0},{2,3},{3,2},{4,5},{5,4},{6,7},{7,6},{8,9},{9,8},{10,11... | collective-permute-start | bytes 3145736 | tf_op jit(solution)/shard_map/ppermute | solution.py:52
  219.1 23.6 %all-to-all-start.1 = ((bf16[8,8,2048]{2,1,0:T(8,128)(2,1)}), bf16[8,8,2048]{2,1,0:T(8,128)(2,1)S(1)}, u32[]{:S(2)}, u32[]{:S(2)}) async-start(bf16[8,8,2048]{2,1,0:T(8,128)(2,1)} %bitcast.10), calls=%async_computation.1 | async-start | bytes 524288 | tf_op jit(solution)/shard_map/all_to_all | solution.py:569
  (3 other events, 23.2 us)

commit v4 on v3

--- a/solution.py
+++ b/solution.py
@@ -107,11 +107,11 @@
 def down_across(zh, x, b4, b2, b1, y, c):
     if (zh, x) != (1, 0):
         return None
-    return (0, 3, 1 - b4, 1 - b2, 1 - b1, y, 1) if c else (1, 3, b4, b2, b1, y, 0)
+    return (1, 3, b4, b2, b1, y, 1) if c else (0, 3, 1 - b4, 1 - b2, 1 - b1, y, 0)
 
 
 def down_relayed(zh, x, b4, b2, b1, y, c):
-    return (0, 3, 1 - b4, 1 - b2, 1 - b1, y, 0) if (zh, x, c) == (1, 3, 0) else None
+    return (0, 3, 1 - b4, 1 - b2, 1 - b1, y, 1) if (zh, x, c) == (1, 3, 1) else None
 
 
 def doubled(block, route):
@@ -517,10 +517,10 @@
 def shards(inputs, targets, w_in, w_out, probes):
     place = [jnp.reshape(lax.axis_index(name), (1,)).astype(jnp.int32) for name in (*DP, SECTION)]
     section = place[-1]
-    in_block = settled_call(place, w_in[0])
+    out_block = settled_call(place, w_out[0])
     probe = probes[0]
-    own_in, other_in = gathered(in_block, True)
-    full_out = placed_call(place, *gathered(w_out[0], False))
+    own_in, other_in = gathered(w_in[0], True)
+    full_out = placed_call(place, *gathered(out_block, False))
     order, curvature_order, opening_n, opening_t = opening_call(place, inputs, probe)
     goal = routed(targets, goal_route)
     pairs, slopes, kept, grads = [None] * MICRO, [], [], []

time: 245 us -> 239 us (0.976)
  waiting for transfers between devices: 119 us -> 114 us
    ppermute x46, waiting for transfers between devices: 103 us -> 98.7 us  [routed(): return lax.ppermute(value, NAMES, pairs)]
  transfers between devices with their start and end apart: 47 -> 47, of which waited for: 17 -> 18; matrix products, arithmetic and copies ran while one was open for 1% -> 1% of each run, Pallas kernels for 3% -> 3%
where the time goes in v4:
time: 239 us; the launch traced here: 238 us
  waiting for transfers between devices  114 us (48%)
  starting transfers between devices  89.1 us (37%)
  blocking collectives  19 us (8%)
  Pallas kernels  8.94 us (4%)
  other arithmetic  3.51 us (1%)
    ppermute x46, waiting for transfers between devices, routed(): return lax.ppermute(value, NAMES, pairs)  98.7 us
    ppermute x46, starting transfers between devices, routed(): return lax.ppermute(value, NAMES, pairs)  83.3 us
    all_to_all x1, blocking collectives, shards(): lax.all_to_all(summed.reshape(4, 64, HIDDEN), 'y', 0, 0, tiled=True)  19 us
    all_to_all x1, waiting for transfers between devices, shards(): lax.all_to_all(summed.reshape(8, 8, HIDDEN), ('b1', 'b2', 'b4'), 0, 0, ti...  15.5 us
    all_to_all x1, starting transfers between devices, shards(): lax.all_to_all(summed.reshape(8, 8, HIDDEN), ('b1', 'b2', 'b4'), 0, 0, ti...  5.8 us
  transfers between devices with their start and end apart: 47, of which 18 were waited for; matrix products, arithmetic and copies ran while one was open for 1% of the time, Pallas kernels for 3%

profile of v4, /device:TPU:8, one launch (start us, length us, event | category | flops | bytes accessed | tf_op | source)
XLA Modules:
  0.0 237.6 jit_solution(12148644842983010918)
XLA Ops:
  0.0 0.8 copy-done.2
  0.8 9.1 %collective-permute-start.6 = (bf16[32,512]{1,0:T(8,128)(2,1)S(1)}, bf16[32,512]{1,0:T(8,128)(2,1)S(1)}, u32[]{:S(2)}, u32[]{:S(2)}) collective-permute-start(bf16[32,512]{1,0:T(8,128)(2,1)S(1)} %settled.1), channel_id=1, source_target_pairs={{0,32},{1,33},{2,34},{3,35},{4,36},{5,37},{6,38},{7,39},{8,40},{9,... | collective-permute-start | bytes 98312 | tf_op jit(solution)/shard_map/ppermute | solution.py:52
  9.9 1.9 collective-permute-start
  11.8 0.8 constant_dynamic-update-slice_fusion.4
  12.6 5.2 %collective-permute-start.7 = (bf16[64,512]{1,0:T(8,128)(2,1)S(1)}, bf16[64,512]{1,0:T(8,128)(2,1)S(1)}, u32[]{:S(2)}, u32[]{:S(2)}) collective-permute-start(bf16[64,512]{1,0:T(8,128)(2,1)S(1)} %pad_maximum_fusion.5), channel_id=1, source_target_pairs={{0,16},{1,17},{2,18},{3,19},{4,20},{5,21},{6,22},{7,23},{8,24},{9,... | collective-permute-start | bytes 196616 | tf_op jit(solution)/shard_map/ppermute | solution.py:52
  17.8 2.4 %collective-permute-done = bf16[8,2048]{1,0:T(8,128)(2,1)S(1)} collective-permute-done((bf16[8,2048]{1,0:T(8,128)(2,1)}, bf16[8,2048]{1,0:T(8,128)(2,1)S(1)}, u32[]{:S(2)}, u32[]{:S(2)}) %collective-permute-start) | collective-permute-done | bytes 32800 | tf_op jit(solution)/shard_map/ppermute | solution.py:52
  20.9 5.2 %collective-permute-start.1 = (bf16[16,2048]{1,0:T(8,128)(2,1)S(1)}, bf16[16,2048]{1,0:T(8,128)(2,1)S(1)}, u32[]{:S(2)}, u32[]{:S(2)}) collective-permute-start(bf16[16,2048]{1,0:T(8,128)(2,1)S(1)} %pad_maximum_fusion.4), channel_id=1, source_target_pairs={{0,16},{1,17},{2,18},{3,19},{4,20},{5,21},{6,22},{7,23},{8,24},{9,... | collective-permute-start | bytes 196616 | tf_op jit(solution)/shard_map/ppermute | solution.py:52
  26.2 3.5 %collective-permute-start.8 = (bf16[128,512]{1,0:T(8,128)(2,1)S(1)}, bf16[128,512]{1,0:T(8,128)(2,1)S(1)}, u32[]{:S(2)}, u32[]{:S(2)}) collective-permute-start(bf16[128,512]{1,0:T(8,128)(2,1)S(1)} %pad_maximum_fusion.3), channel_id=1, source_target_pairs={{0,8},{1,9},{2,10},{3,11},{4,12},{5,13},{6,14},{7,15},{8,0},{9,1},... | collective-permute-start | bytes 393224 | tf_op jit(solution)/shard_map/ppermute | solution.py:52
  29.7 0.8 pad_maximum_fusion.2
  30.5 2.8 %collective-permute-start.2 = (bf16[32,2048]{1,0:T(8,128)(2,1)S(1)}, bf16[32,2048]{1,0:T(8,128)(2,1)S(1)}, u32[]{:S(2)}, u32[]{:S(2)}) collective-permute-start(bf16[32,2048]{1,0:T(8,128)(2,1)S(1)} %pad_maximum_fusion.2), channel_id=1, source_target_pairs={{0,8},{1,9},{2,10},{3,11},{4,12},{5,13},{6,14},{7,15},{8,0},{9,1},... | collective-permute-start | bytes 393224 | tf_op jit(solution)/shard_map/ppermute | solution.py:52
  33.4 3.5 %collective-permute-start.9 = (bf16[256,512]{1,0:T(8,128)(2,1)S(1)}, bf16[256,512]{1,0:T(8,128)(2,1)S(1)}, u32[]{:S(2)}, u32[]{:S(2)}) collective-permute-start(bf16[256,512]{1,0:T(8,128)(2,1)S(1)} %pad_maximum_fusion.1), channel_id=1, source_target_pairs={{0,6},{1,7},{2,4},{3,5},{4,2},{5,3},{6,0},{7,1},{8,14},{9,15},{10,... | collective-permute-start | bytes 786440 | tf_op jit(solution)/shard_map/ppermute | solution.py:52
  37.4 3.3 %collective-permute-start.3 = (bf16[64,2048]{1,0:T(8,128)(2,1)S(1)}, bf16[64,2048]{1,0:T(8,128)(2,1)S(1)}, u32[]{:S(2)}, u32[]{:S(2)}) collective-permute-start(bf16[64,2048]{1,0:T(8,128)(2,1)S(1)} %pad_maximum_fusion), channel_id=1, source_target_pairs={{0,2},{1,3},{2,0},{3,1},{4,6},{5,7},{6,4},{7,5},{8,10},{9,11},{10,... | collective-permute-start | bytes 786440 | tf_op jit(solution)/shard_map/ppermute | solution.py:52
  40.8 0.8 collective-permute-done.9
  41.7 3.6 %collective-permute-start.10 = (bf16[512,512]{1,0:T(8,128)(2,1)S(1)}, bf16[512,512]{1,0:T(8,128)(2,1)S(1)}, u32[]{:S(2)}, u32[]{:S(2)}) collective-permute-start(bf16[512,512]{1,0:T(8,128)(2,1)S(1)} %get-tuple-element.203), channel_id=1, source_target_pairs={{0,2},{1,3},{2,0},{3,1},{4,6},{5,7},{6,4},{7,5},{8,10},{9,11},{10,... | collective-permute-start | bytes 1572872 | tf_op jit(solution)/shard_map/ppermute | solution.py:52
  45.3 3.1 %collective-permute-done.3 = bf16[64,2048]{1,0:T(8,128)(2,1)S(1)} collective-permute-done((bf16[64,2048]{1,0:T(8,128)(2,1)S(1)}, bf16[64,2048]{1,0:T(8,128)(2,1)S(1)}, u32[]{:S(2)}, u32[]{:S(2)}) %collective-permute-start.3) | collective-permute-done | bytes 262176 | tf_op jit(solution)/shard_map/ppermute | solution.py:52
  48.5 3.5 %collective-permute-start.4 = (bf16[128,2048]{1,0:T(8,128)(2,1)S(1)}, bf16[128,2048]{1,0:T(8,128)(2,1)S(1)}, u32[]{:S(2)}, u32[]{:S(2)}) collective-permute-start(bf16[128,2048]{1,0:T(8,128)(2,1)S(1)} %get-tuple-element.205), channel_id=1, source_target_pairs={{0,6},{1,7},{2,4},{3,5},{4,2},{5,3},{6,0},{7,1},{8,14},{9,15},{10,... | collective-permute-start | bytes 1572872 | tf_op jit(solution)/shard_map/ppermute | solution.py:52
  52.0 4.2 %collective-permute-done.10 = bf16[512,512]{1,0:T(8,128)(2,1)S(1)} collective-permute-done((bf16[512,512]{1,0:T(8,128)(2,1)S(1)}, bf16[512,512]{1,0:T(8,128)(2,1)S(1)}, u32[]{:S(2)}, u32[]{:S(2)}) %collective-permute-start.10) | collective-permute-done | bytes 524320 | tf_op jit(solution)/shard_map/ppermute | solution.py:52
  56.2 1.9 collective-permute-start.11
  58.2 1.4 collective-permute-done.4
  59.6 1.9 collective-permute-start.5
  61.6 1.3 opening.1
  63.1 1.1 collective-permute-done.5.other_in.refs_2_
  64.2 1.2 layer_up_0.3
  65.4 2.2 collective-permute-start.29
  67.6 1.2 layer_up_0.2
  68.8 1.3 collective-permute-start.12
  71.5 1.9 collective-permute-done.12.refs_6_
  78.3 9.2 %collective-permute-start.34 = (bf16[2,64,512]{2,1,0:T(8,128)(2,1)S(1)}, bf16[2,64,512]{2,1,0:T(8,128)(2,1)S(1)}, u32[]{:S(2)}, u32[]{:S(2)}) collective-permute-start(bf16[2,64,512]{2,1,0:T(8,128)(2,1)S(1)} %get-tuple-element.159), channel_id=1, source_target_pairs={{0,64},{1,65},{2,66},{3,67},{4,68},{5,69},{6,70},{7,71},{8,72},{9,... | collective-permute-start | bytes 393224 | tf_op jit(solution)/shard_map/ppermute | solution.py:52
  87.5 1.3 collective-permute-start.17
  88.8 1.2 collective-permute-done.34.refs_6_
  90.0 0.8 collective-permute-start.35
  94.2 2.0 turned_weights.1
  99.1 1.3 collective-permute-start.39
  100.4 1.3 collective-permute-start.23
  101.7 29.3 %collective-permute-done.39.refs_1_ = bf16[2,64,512]{2,1,0:T(8,128)(2,1)S(1)} collective-permute-done((bf16[2,64,512]{2,1,0:T(8,128)(2,1)S(1)}, bf16[2,64,512]{2,1,0:T(8,128)(2,1)S(1)}, u32[]{:S(2)}, u32[]{:S(2)}) %collective-permute-start.39) | collective-permute-done | bytes 131104 | tf_op jit(solution)/shard_map/ppermute | solution.py:52
  131.7 4.7 %collective-permute-done.23.refs_1_ = bf16[2,64,512]{2,1,0:T(8,128)(2,1)S(1)} collective-permute-done((bf16[2,64,512]{2,1,0:T(8,128)(2,1)S(1)}, bf16[2,64,512]{2,1,0:T(8,128)(2,1)S(1)}, u32[]{:S(2)}, u32[]{:S(2)}) %collective-permute-start.23) | collective-permute-done | bytes 131104 | tf_op jit(solution)/shard_map/ppermute | solution.py:52
  141.3 1.3 collective-permute-start.44
  142.6 1.3 collective-permute-start.28
  143.9 42.7 %collective-permute-done.44.refs_1_ = bf16[2,64,512]{2,1,0:T(8,128)(2,1)S(1)} collective-permute-done((bf16[2,64,512]{2,1,0:T(8,128)(2,1)S(1)}, bf16[2,64,512]{2,1,0:T(8,128)(2,1)S(1)}, u32[]{:S(2)}, u32[]{:S(2)}) %collective-permute-start.44) | collective-permute-done | bytes 131104 | tf_op jit(solution)/shard_map/ppermute | solution.py:52
  186.7 1.4 curvature_first.1
  188.0 1.3 collective-permute-done.28.refs_1_
  189.3 1.4 curvature_last.1
  190.7 1.9 collective-permute-start.45
  192.6 2.6 %collective-permute-done.45 = bf16[256,2048]{1,0:T(8,128)(2,1)S(1)} collective-permute-done((bf16[256,2048]{1,0:T(8,128)(2,1)S(1)}, bf16[256,2048]{1,0:T(8,128)(2,1)S(1)}, u32[]{:S(2)}, u32[]{:S(2)}) %collective-permute-start.45) | collective-permute-done | bytes 1048608 | tf_op jit(solution)/shard_map/ppermute | solution.py:52
  195.6 19.0 %all_to_all.10 = bf16[4,64,2048]{2,1,0:T(8,128)(2,1)S(1)} all-to-all(bf16[4,64,2048]{2,1,0:T(8,128)(2,1)S(1)} %bitcast.32), channel_id=1, replica_groups=mesh['zh'=2,'x'=4,'b4'=2,'b2'=2,'b1'=2,'y'=4,'c'=2] {'y'}, dimensions={0} | all-to-all | bytes 2097152 | tf_op jit(solution)/shard_map/all_to_all | solution.py:567
  214.6 0.9 reduce_sum.23
  215.5 5.8 %all-to-all-start.1 = ((bf16[8,8,2048]{2,1,0:T(8,128)(2,1)}), bf16[8,8,2048]{2,1,0:T(8,128)(2,1)S(1)}, u32[]{:S(2)}, u32[]{:S(2)}) async-start(bf16[8,8,2048]{2,1,0:T(8,128)(2,1)} %bitcast.10), calls=%async_computation.1 | async-start | bytes 524288 | tf_op jit(solution)/shard_map/all_to_all | solution.py:569
  221.3 15.5 %all-to-all-done.1 = bf16[8,8,2048]{2,1,0:T(8,128)(2,1)S(1)} async-done(((bf16[8,8,2048]{2,1,0:T(8,128)(2,1)}), bf16[8,8,2048]{2,1,0:T(8,128)(2,1)S(1)}, u32[]{:S(2)}, u32[]{:S(2)}) %all-to-all-start.1) | async-done | bytes 262176 | tf_op jit(solution)/shard_map/all_to_all | solution.py:569
  (116 shorter events, 20.5 us)
Async XLA Ops:
  0.0 37.4 %copy-start.3 = (bf16[1,8,2048]{2,1,0:T(8,128)(2,1)S(1)}, bf16[1,8,2048]{2,1,0:T(8,128)(2,1)}, u32[]{:S(2)}) copy-start(bf16[1,8,2048]{2,1,0:T(8,128)(2,1)} %param.7) | copy-start | bytes 98308
  0.8 11.8 %collective-permute-start.6 = (bf16[32,512]{1,0:T(8,128)(2,1)S(1)}, bf16[32,512]{1,0:T(8,128)(2,1)S(1)}, u32[]{:S(2)}, u32[]{:S(2)}) collective-permute-start(bf16[32,512]{1,0:T(8,128)(2,1)S(1)} %settled.1), channel_id=1, source_target_pairs={{0,32},{1,33},{2,34},{3,35},{4,36},{5,37},{6,38},{7,39},{8,40},{9,... | collective-permute-start | bytes 98312 | tf_op jit(solution)/shard_map/ppermute | solution.py:52
  9.9 10.3 %collective-permute-start = (bf16[8,2048]{1,0:T(8,128)(2,1)}, bf16[8,2048]{1,0:T(8,128)(2,1)S(1)}, u32[]{:S(2)}, u32[]{:S(2)}) collective-permute-start(bf16[8,2048]{1,0:T(8,128)(2,1)} %bitcast.33), channel_id=1, source_target_pairs={{0,32},{1,33},{2,34},{3,35},{4,36},{5,37},{6,38},{7,39},{8,40},{9,... | collective-permute-start | bytes 98312 | tf_op jit(solution)/shard_map/ppermute | solution.py:52
  12.6 13.6 %collective-permute-start.7 = (bf16[64,512]{1,0:T(8,128)(2,1)S(1)}, bf16[64,512]{1,0:T(8,128)(2,1)S(1)}, u32[]{:S(2)}, u32[]{:S(2)}) collective-permute-start(bf16[64,512]{1,0:T(8,128)(2,1)S(1)} %pad_maximum_fusion.5), channel_id=1, source_target_pairs={{0,16},{1,17},{2,18},{3,19},{4,20},{5,21},{6,22},{7,23},{8,24},{9,... | collective-permute-start | bytes 196616 | tf_op jit(solution)/shard_map/ppermute | solution.py:52
  20.9 8.8 %collective-permute-start.1 = (bf16[16,2048]{1,0:T(8,128)(2,1)S(1)}, bf16[16,2048]{1,0:T(8,128)(2,1)S(1)}, u32[]{:S(2)}, u32[]{:S(2)}) collective-permute-start(bf16[16,2048]{1,0:T(8,128)(2,1)S(1)} %pad_maximum_fusion.4), channel_id=1, source_target_pairs={{0,16},{1,17},{2,18},{3,19},{4,20},{5,21},{6,22},{7,23},{8,24},{9,... | collective-permute-start | bytes 196616 | tf_op jit(solution)/shard_map/ppermute | solution.py:52
  26.2 7.2 %collective-permute-start.8 = (bf16[128,512]{1,0:T(8,128)(2,1)S(1)}, bf16[128,512]{1,0:T(8,128)(2,1)S(1)}, u32[]{:S(2)}, u32[]{:S(2)}) collective-permute-start(bf16[128,512]{1,0:T(8,128)(2,1)S(1)} %pad_maximum_fusion.3), channel_id=1, source_target_pairs={{0,8},{1,9},{2,10},{3,11},{4,12},{5,13},{6,14},{7,15},{8,0},{9,1},... | collective-permute-start | bytes 393224 | tf_op jit(solution)/shard_map/ppermute | solution.py:52
  30.5 6.9 %collective-permute-start.2 = (bf16[32,2048]{1,0:T(8,128)(2,1)S(1)}, bf16[32,2048]{1,0:T(8,128)(2,1)S(1)}, u32[]{:S(2)}, u32[]{:S(2)}) collective-permute-start(bf16[32,2048]{1,0:T(8,128)(2,1)S(1)} %pad_maximum_fusion.2), channel_id=1, source_target_pairs={{0,8},{1,9},{2,10},{3,11},{4,12},{5,13},{6,14},{7,15},{8,0},{9,1},... | collective-permute-start | bytes 393224 | tf_op jit(solution)/shard_map/ppermute | solution.py:52
  33.4 8.3 %collective-permute-start.9 = (bf16[256,512]{1,0:T(8,128)(2,1)S(1)}, bf16[256,512]{1,0:T(8,128)(2,1)S(1)}, u32[]{:S(2)}, u32[]{:S(2)}) collective-permute-start(bf16[256,512]{1,0:T(8,128)(2,1)S(1)} %pad_maximum_fusion.1), channel_id=1, source_target_pairs={{0,6},{1,7},{2,4},{3,5},{4,2},{5,3},{6,0},{7,1},{8,14},{9,15},{10,... | collective-permute-start | bytes 786440 | tf_op jit(solution)/shard_map/ppermute | solution.py:52
  37.4 11.0 %collective-permute-start.3 = (bf16[64,2048]{1,0:T(8,128)(2,1)S(1)}, bf16[64,2048]{1,0:T(8,128)(2,1)S(1)}, u32[]{:S(2)}, u32[]{:S(2)}) collective-permute-start(bf16[64,2048]{1,0:T(8,128)(2,1)S(1)} %pad_maximum_fusion), channel_id=1, source_target_pairs={{0,2},{1,3},{2,0},{3,1},{4,6},{5,7},{6,4},{7,5},{8,10},{9,11},{10,... | collective-permute-start | bytes 786440 | tf_op jit(solution)/shard_map/ppermute | solution.py:52
  41.7 14.5 %collective-permute-start.10 = (bf16[512,512]{1,0:T(8,128)(2,1)S(1)}, bf16[512,512]{1,0:T(8,128)(2,1)S(1)}, u32[]{:S(2)}, u32[]{:S(2)}) collective-permute-start(bf16[512,512]{1,0:T(8,128)(2,1)S(1)} %get-tuple-element.203), channel_id=1, source_target_pairs={{0,2},{1,3},{2,0},{3,1},{4,6},{5,7},{6,4},{7,5},{8,10},{9,11},{10,... | collective-permute-start | bytes 1572872 | tf_op jit(solution)/shard_map/ppermute | solution.py:52
  48.5 11.1 %collective-permute-start.4 = (bf16[128,2048]{1,0:T(8,128)(2,1)S(1)}, bf16[128,2048]{1,0:T(8,128)(2,1)S(1)}, u32[]{:S(2)}, u32[]{:S(2)}) collective-permute-start(bf16[128,2048]{1,0:T(8,128)(2,1)S(1)} %get-tuple-element.205), channel_id=1, source_target_pairs={{0,6},{1,7},{2,4},{3,5},{4,2},{5,3},{6,0},{7,1},{8,14},{9,15},{10,... | collective-permute-start | bytes 1572872 | tf_op jit(solution)/shard_map/ppermute | solution.py:52
  56.2 6.6 %collective-permute-start.11 = (bf16[1024,512]{1,0:T(8,128)(2,1)S(1)}, bf16[1024,512]{1,0:T(8,128)(2,1)S(1)}, u32[]{:S(2)}, u32[]{:S(2)}) collective-permute-start(bf16[1024,512]{1,0:T(8,128)(2,1)S(1)} %constant_dynamic-update-slice_fusion.16.refs_6_), channel_id=1, source_target_pairs={{0,1},{1,0},{2,3},{3,2},{4,5},{5,4},{6,7},{7,6},{8,9},{9,8},{10,11... | collective-permute-start | bytes 3145736 | tf_op jit(solution)/shard_map/ppermute | solution.py:52
  59.6 4.6 %collective-permute-start.5 = (bf16[256,2048]{1,0:T(8,128)(2,1)S(1)}, bf16[256,2048]{1,0:T(8,128)(2,1)S(1)}, u32[]{:S(2)}, u32[]{:S(2)}) collective-permute-start(bf16[256,2048]{1,0:T(8,128)(2,1)S(1)} %constant_dynamic-update-slice_fusion.5.own_in.refs_1_), channel_id=1, source_target_pairs={{0,1},{1,0},{2,3},{3,2},{4,5},{5,4},{6,7},{7,6},{8,9},{9,8},{10,11... | collective-permute-start | bytes 3145736 | tf_op jit(solution)/shard_map/ppermute | solution.py:52
  65.4 5.4 %collective-permute-start.29 = (bf16[2,64,512]{2,1,0:T(8,128)(2,1)S(1)}, bf16[2,64,512]{2,1,0:T(8,128)(2,1)S(1)}, u32[]{:S(2)}, u32[]{:S(2)}) collective-permute-start(bf16[2,64,512]{2,1,0:T(8,128)(2,1)S(1)} %get-tuple-element.155), channel_id=1, source_target_pairs={{0,64},{1,65},{2,66},{3,67},{4,68},{5,69},{6,70},{7,71},{8,72},{9,... | collective-permute-start | bytes 393224 | tf_op jit(solution)/shard_map/ppermute | solution.py:52
  68.8 4.6 %collective-permute-start.12 = (bf16[2,64,512]{2,1,0:T(8,128)(2,1)S(1)}, bf16[2,64,512]{2,1,0:T(8,128)(2,1)S(1)}, u32[]{:S(2)}, u32[]{:S(2)}) collective-permute-start(bf16[2,64,512]{2,1,0:T(8,128)(2,1)S(1)} %get-tuple-element.107), channel_id=1, source_target_pairs={{0,64},{1,65},{2,66},{3,67},{4,68},{5,69},{6,70},{7,71},{8,72},{9,... | collective-permute-start | bytes 393224 | tf_op jit(solution)/shard_map/ppermute | solution.py:52
  70.8 3.3 %collective-permute-start.30 = (bf16[2,64,512]{2,1,0:T(8,128)(2,1)S(1)}, bf16[2,64,512]{2,1,0:T(8,128)(2,1)S(1)}, u32[]{:S(2)}, u32[]{:S(2)}) collective-permute-start(bf16[2,64,512]{2,1,0:T(8,128)(2,1)S(1)} %get-tuple-element.156), channel_id=1, source_target_pairs={{64,128},{65,129},{66,130},{67,131},{68,132},{69,133},{70,134},{71... | collective-permute-start | bytes 393224 | tf_op jit(solution)/shard_map/ppermute | solution.py:52
  73.4 1.4 collective-permute-start.13
  74.1 1.4 collective-permute-start.31
  74.8 1.4 collective-permute-start.14
  75.5 1.4 collective-permute-start.32
  76.2 1.4 collective-permute-start.15
  76.9 1.4 collective-permute-start.33
  77.6 9.9 %collective-permute-start.16 = (bf16[2,64,512]{2,1,0:T(8,128)(2,1)S(1)}, bf16[2,64,512]{2,1,0:T(8,128)(2,1)S(1)}, u32[]{:S(2)}, u32[]{:S(2)}) collective-permute-start(bf16[2,64,512]{2,1,0:T(8,128)(2,1)S(1)} %collective-permute-done.15.refs_6_), channel_id=1, source_target_pairs={{1,313},{3,315},{5,317},{7,319},{9,305},{11,307},{13,309},{15,311}... | collective-permute-start | bytes 393224 | tf_op jit(solution)/shard_map/ppermute | solution.py:52
  78.3 11.7 %collective-permute-start.34 = (bf16[2,64,512]{2,1,0:T(8,128)(2,1)S(1)}, bf16[2,64,512]{2,1,0:T(8,128)(2,1)S(1)}, u32[]{:S(2)}, u32[]{:S(2)}) collective-permute-start(bf16[2,64,512]{2,1,0:T(8,128)(2,1)S(1)} %get-tuple-element.159), channel_id=1, source_target_pairs={{0,64},{1,65},{2,66},{3,67},{4,68},{5,69},{6,70},{7,71},{8,72},{9,... | collective-permute-start | bytes 393224 | tf_op jit(solution)/shard_map/ppermute | solution.py:52
  87.5 3.8 %collective-permute-start.17 = (bf16[2,64,512]{2,1,0:T(8,128)(2,1)S(1)}, bf16[2,64,512]{2,1,0:T(8,128)(2,1)S(1)}, u32[]{:S(2)}, u32[]{:S(2)}) collective-permute-start(bf16[2,64,512]{2,1,0:T(8,128)(2,1)S(1)} %get-tuple-element.111), channel_id=1, source_target_pairs={{0,64},{1,65},{2,66},{3,67},{4,68},{5,69},{6,70},{7,71},{8,72},{9,... | collective-permute-start | bytes 393224 | tf_op jit(solution)/shard_map/ppermute | solution.py:52
  90.0 2.7 %collective-permute-start.35 = (bf16[2,64,512]{2,1,0:T(8,128)(2,1)S(1)}, bf16[2,64,512]{2,1,0:T(8,128)(2,1)S(1)}, u32[]{:S(2)}, u32[]{:S(2)}) collective-permute-start(bf16[2,64,512]{2,1,0:T(8,128)(2,1)S(1)} %get-tuple-element.160), channel_id=1, source_target_pairs={{64,128},{65,129},{66,130},{67,131},{68,132},{69,133},{70,134},{71... | collective-permute-start | bytes 393224 | tf_op jit(solution)/shard_map/ppermute | solution.py:52
  91.4 2.1 collective-permute-start.18
  92.0 2.1 collective-permute-start.20
  92.7 3.5 %collective-permute-start.36 = (bf16[2,64,512]{2,1,0:T(8,128)(2,1)S(1)}, bf16[2,64,512]{2,1,0:T(8,128)(2,1)S(1)}, u32[]{:S(2)}, u32[]{:S(2)}) collective-permute-start(bf16[2,64,512]{2,1,0:T(8,128)(2,1)S(1)} %get-tuple-element.161), channel_id=1, source_target_pairs={{128,192},{129,193},{130,194},{131,195},{132,196},{133,197},{134,1... | collective-permute-start | bytes 393224 | tf_op jit(solution)/shard_map/ppermute | solution.py:52
  93.5 3.5 %collective-permute-start.19 = (bf16[2,64,512]{2,1,0:T(8,128)(2,1)S(1)}, bf16[2,64,512]{2,1,0:T(8,128)(2,1)S(1)}, u32[]{:S(2)}, u32[]{:S(2)}) collective-permute-start(bf16[2,64,512]{2,1,0:T(8,128)(2,1)S(1)} %get-tuple-element.113), channel_id=1, source_target_pairs={{128,192},{129,193},{130,194},{131,195},{132,196},{133,197},{134,1... | collective-permute-start | bytes 393224 | tf_op jit(solution)/shard_map/ppermute | solution.py:52
  96.3 1.4 collective-permute-start.37
  97.0 1.4 collective-permute-start.21
  97.7 1.4 collective-permute-start.38
  98.4 2.0 collective-permute-start.22
  99.1 31.9 %collective-permute-start.39 = (bf16[2,64,512]{2,1,0:T(8,128)(2,1)S(1)}, bf16[2,64,512]{2,1,0:T(8,128)(2,1)S(1)}, u32[]{:S(2)}, u32[]{:S(2)}) collective-permute-start(bf16[2,64,512]{2,1,0:T(8,128)(2,1)S(1)} %get-tuple-element.174), channel_id=1, source_target_pairs={{64,0},{65,1},{66,2},{67,3},{68,4},{69,5},{70,6},{71,7},{72,8},{73... | collective-permute-start | bytes 393224 | tf_op jit(solution)/shard_map/ppermute | solution.py:52
  100.4 36.0 %collective-permute-start.23 = (bf16[2,64,512]{2,1,0:T(8,128)(2,1)S(1)}, bf16[2,64,512]{2,1,0:T(8,128)(2,1)S(1)}, u32[]{:S(2)}, u32[]{:S(2)}) collective-permute-start(bf16[2,64,512]{2,1,0:T(8,128)(2,1)S(1)} %get-tuple-element.130), channel_id=1, source_target_pairs={{64,0},{65,1},{66,2},{67,3},{68,4},{69,5},{70,6},{71,7},{72,8},{73... | collective-permute-start | bytes 393224 | tf_op jit(solution)/shard_map/ppermute | solution.py:52
  131.0 6.0 %collective-permute-start.40 = (bf16[2,64,512]{2,1,0:T(8,128)(2,1)S(1)}, bf16[2,64,512]{2,1,0:T(8,128)(2,1)S(1)}, u32[]{:S(2)}, u32[]{:S(2)}) collective-permute-start(bf16[2,64,512]{2,1,0:T(8,128)(2,1)S(1)} %get-tuple-element.178), channel_id=1, source_target_pairs={{256,248},{257,449},{258,250},{259,451},{260,252},{261,453},{262,2... | collective-permute-start | bytes 393224 | tf_op jit(solution)/shard_map/ppermute | solution.py:52
  136.4 1.4 collective-permute-start.24
  137.1 1.4 collective-permute-start.41
  137.8 1.4 collective-permute-start.25
  138.5 1.4 collective-permute-start.42
  139.2 1.4 collective-permute-start.26
  139.9 1.4 collective-permute-start.43
  140.6 2.0 collective-permute-start.27
  141.3 45.4 %collective-permute-start.44 = (bf16[2,64,512]{2,1,0:T(8,128)(2,1)S(1)}, bf16[2,64,512]{2,1,0:T(8,128)(2,1)S(1)}, u32[]{:S(2)}, u32[]{:S(2)}) collective-permute-start(bf16[2,64,512]{2,1,0:T(8,128)(2,1)S(1)} %get-tuple-element.190), channel_id=1, source_target_pairs={{64,0},{65,1},{66,2},{67,3},{68,4},{69,5},{70,6},{71,7},{72,8},{73... | collective-permute-start | bytes 393224 | tf_op jit(solution)/shard_map/ppermute | solution.py:52
  142.6 46.7 %collective-permute-start.28 = (bf16[2,64,512]{2,1,0:T(8,128)(2,1)S(1)}, bf16[2,64,512]{2,1,0:T(8,128)(2,1)S(1)}, u32[]{:S(2)}, u32[]{:S(2)}) collective-permute-start(bf16[2,64,512]{2,1,0:T(8,128)(2,1)S(1)} %get-tuple-element.145), channel_id=1, source_target_pairs={{64,0},{65,1},{66,2},{67,3},{68,4},{69,5},{70,6},{71,7},{72,8},{73... | collective-permute-start | bytes 393224 | tf_op jit(solution)/shard_map/ppermute | solution.py:52
  190.7 4.6 %collective-permute-start.45 = (bf16[256,2048]{1,0:T(8,128)(2,1)S(1)}, bf16[256,2048]{1,0:T(8,128)(2,1)S(1)}, u32[]{:S(2)}, u32[]{:S(2)}) collective-permute-start(bf16[256,2048]{1,0:T(8,128)(2,1)S(1)} %get-tuple-element.202), channel_id=1, source_target_pairs={{0,1},{1,0},{2,3},{3,2},{4,5},{5,4},{6,7},{7,6},{8,9},{9,8},{10,11... | collective-permute-start | bytes 3145736 | tf_op jit(solution)/shard_map/ppermute | solution.py:52
  215.5 21.3 %all-to-all-start.1 = ((bf16[8,8,2048]{2,1,0:T(8,128)(2,1)}), bf16[8,8,2048]{2,1,0:T(8,128)(2,1)S(1)}, u32[]{:S(2)}, u32[]{:S(2)}) async-start(bf16[8,8,2048]{2,1,0:T(8,128)(2,1)} %bitcast.10), calls=%async_computation.1 | async-start | bytes 524288 | tf_op jit(solution)/shard_map/all_to_all | solution.py:569
  (4 other events, 44.3 us)

commit v5 on v4

--- a/solution.py
+++ b/solution.py
@@ -82,14 +82,14 @@
 
 def up_from(section):
     def route(zh, x, b4, b2, b1, y, c):
-        return (zh, x + 1, b4, b2, b1, y, c) if x == section % 4 else None
+        return (zh, x + 1, b4, b2, b1, y, 1 - c) if x == section % 4 else None
 
     return route
 
 
 def down_from(section):
     def route(zh, x, b4, b2, b1, y, c):
-        return (zh, x - 1, b4, b2, b1, y, c) if x == section % 4 else None
+        return (zh, x - 1, b4, b2, b1, y, 1 - c) if x == section % 4 else None
 
     return route
 

time: 239 us -> 243 us (1.017)
  waiting for transfers between devices: 114 us -> 119 us
    ppermute x46, waiting for transfers between devices: 98.7 us -> 104 us  [routed(): return lax.ppermute(value, NAMES, pairs)]
where the time goes in v5:
time: 243 us; the launch traced here: 242 us
  waiting for transfers between devices  119 us (49%)
  starting transfers between devices  88.8 us (37%)
  blocking collectives  18.7 us (8%)
  Pallas kernels  8.94 us (4%)
  other arithmetic  3.51 us (1%)
    ppermute x46, waiting for transfers between devices, routed(): return lax.ppermute(value, NAMES, pairs)  104 us
    ppermute x46, starting transfers between devices, routed(): return lax.ppermute(value, NAMES, pairs)  83.6 us
    all_to_all x1, blocking collectives, shards(): lax.all_to_all(summed.reshape(4, 64, HIDDEN), 'y', 0, 0, tiled=True)  18.7 us
    all_to_all x1, waiting for transfers between devices, shards(): lax.all_to_all(summed.reshape(8, 8, HIDDEN), ('b1', 'b2', 'b4'), 0, 0, ti...  15.5 us
    all_to_all x1, starting transfers between devices, shards(): lax.all_to_all(summed.reshape(8, 8, HIDDEN), ('b1', 'b2', 'b4'), 0, 0, ti...  5.23 us
  transfers between devices with their start and end apart: 47, of which 18 were waited for; matrix products, arithmetic and copies ran while one was open for 1% of the time, Pallas kernels for 3%

profile of v5, /device:TPU:8, one launch (start us, length us, event | category | flops | bytes accessed | tf_op | source)
XLA Modules:
  0.0 242.1 jit_solution(8310847662442463279)
XLA Ops:
  0.0 0.8 copy-done.2
  0.8 9.1 %collective-permute-start.6 = (bf16[32,512]{1,0:T(8,128)(2,1)S(1)}, bf16[32,512]{1,0:T(8,128)(2,1)S(1)}, u32[]{:S(2)}, u32[]{:S(2)}) collective-permute-start(bf16[32,512]{1,0:T(8,128)(2,1)S(1)} %settled.1), channel_id=1, source_target_pairs={{0,32},{1,33},{2,34},{3,35},{4,36},{5,37},{6,38},{7,39},{8,40},{9,... | collective-permute-start | bytes 98312 | tf_op jit(solution)/shard_map/ppermute | solution.py:52
  9.9 1.9 collective-permute-start
  11.8 0.8 constant_dynamic-update-slice_fusion.4
  12.6 5.2 %collective-permute-start.7 = (bf16[64,512]{1,0:T(8,128)(2,1)S(1)}, bf16[64,512]{1,0:T(8,128)(2,1)S(1)}, u32[]{:S(2)}, u32[]{:S(2)}) collective-permute-start(bf16[64,512]{1,0:T(8,128)(2,1)S(1)} %pad_maximum_fusion.5), channel_id=1, source_target_pairs={{0,16},{1,17},{2,18},{3,19},{4,20},{5,21},{6,22},{7,23},{8,24},{9,... | collective-permute-start | bytes 196616 | tf_op jit(solution)/shard_map/ppermute | solution.py:52
  17.8 2.4 collective-permute-done
  20.9 5.2 %collective-permute-start.1 = (bf16[16,2048]{1,0:T(8,128)(2,1)S(1)}, bf16[16,2048]{1,0:T(8,128)(2,1)S(1)}, u32[]{:S(2)}, u32[]{:S(2)}) collective-permute-start(bf16[16,2048]{1,0:T(8,128)(2,1)S(1)} %pad_maximum_fusion.4), channel_id=1, source_target_pairs={{0,16},{1,17},{2,18},{3,19},{4,20},{5,21},{6,22},{7,23},{8,24},{9,... | collective-permute-start | bytes 196616 | tf_op jit(solution)/shard_map/ppermute | solution.py:52
  26.2 3.5 %collective-permute-start.8 = (bf16[128,512]{1,0:T(8,128)(2,1)S(1)}, bf16[128,512]{1,0:T(8,128)(2,1)S(1)}, u32[]{:S(2)}, u32[]{:S(2)}) collective-permute-start(bf16[128,512]{1,0:T(8,128)(2,1)S(1)} %pad_maximum_fusion.3), channel_id=1, source_target_pairs={{0,8},{1,9},{2,10},{3,11},{4,12},{5,13},{6,14},{7,15},{8,0},{9,1},... | collective-permute-start | bytes 393224 | tf_op jit(solution)/shard_map/ppermute | solution.py:52
  29.7 0.8 pad_maximum_fusion.2
  30.5 2.8 %collective-permute-start.2 = (bf16[32,2048]{1,0:T(8,128)(2,1)S(1)}, bf16[32,2048]{1,0:T(8,128)(2,1)S(1)}, u32[]{:S(2)}, u32[]{:S(2)}) collective-permute-start(bf16[32,2048]{1,0:T(8,128)(2,1)S(1)} %pad_maximum_fusion.2), channel_id=1, source_target_pairs={{0,8},{1,9},{2,10},{3,11},{4,12},{5,13},{6,14},{7,15},{8,0},{9,1},... | collective-permute-start | bytes 393224 | tf_op jit(solution)/shard_map/ppermute | solution.py:52
  33.4 3.5 %collective-permute-start.9 = (bf16[256,512]{1,0:T(8,128)(2,1)S(1)}, bf16[256,512]{1,0:T(8,128)(2,1)S(1)}, u32[]{:S(2)}, u32[]{:S(2)}) collective-permute-start(bf16[256,512]{1,0:T(8,128)(2,1)S(1)} %pad_maximum_fusion.1), channel_id=1, source_target_pairs={{0,6},{1,7},{2,4},{3,5},{4,2},{5,3},{6,0},{7,1},{8,14},{9,15},{10,... | collective-permute-start | bytes 786440 | tf_op jit(solution)/shard_map/ppermute | solution.py:52
  37.4 3.3 %collective-permute-start.3 = (bf16[64,2048]{1,0:T(8,128)(2,1)S(1)}, bf16[64,2048]{1,0:T(8,128)(2,1)S(1)}, u32[]{:S(2)}, u32[]{:S(2)}) collective-permute-start(bf16[64,2048]{1,0:T(8,128)(2,1)S(1)} %pad_maximum_fusion), channel_id=1, source_target_pairs={{0,2},{1,3},{2,0},{3,1},{4,6},{5,7},{6,4},{7,5},{8,10},{9,11},{10,... | collective-permute-start | bytes 786440 | tf_op jit(solution)/shard_map/ppermute | solution.py:52
  40.8 0.8 collective-permute-done.9
  41.7 3.6 %collective-permute-start.10 = (bf16[512,512]{1,0:T(8,128)(2,1)S(1)}, bf16[512,512]{1,0:T(8,128)(2,1)S(1)}, u32[]{:S(2)}, u32[]{:S(2)}) collective-permute-start(bf16[512,512]{1,0:T(8,128)(2,1)S(1)} %get-tuple-element.203), channel_id=1, source_target_pairs={{0,2},{1,3},{2,0},{3,1},{4,6},{5,7},{6,4},{7,5},{8,10},{9,11},{10,... | collective-permute-start | bytes 1572872 | tf_op jit(solution)/shard_map/ppermute | solution.py:52
  45.3 3.1 %collective-permute-done.3 = bf16[64,2048]{1,0:T(8,128)(2,1)S(1)} collective-permute-done((bf16[64,2048]{1,0:T(8,128)(2,1)S(1)}, bf16[64,2048]{1,0:T(8,128)(2,1)S(1)}, u32[]{:S(2)}, u32[]{:S(2)}) %collective-permute-start.3) | collective-permute-done | bytes 262176 | tf_op jit(solution)/shard_map/ppermute | solution.py:52
  48.5 3.5 %collective-permute-start.4 = (bf16[128,2048]{1,0:T(8,128)(2,1)S(1)}, bf16[128,2048]{1,0:T(8,128)(2,1)S(1)}, u32[]{:S(2)}, u32[]{:S(2)}) collective-permute-start(bf16[128,2048]{1,0:T(8,128)(2,1)S(1)} %get-tuple-element.205), channel_id=1, source_target_pairs={{0,6},{1,7},{2,4},{3,5},{4,2},{5,3},{6,0},{7,1},{8,14},{9,15},{10,... | collective-permute-start | bytes 1572872 | tf_op jit(solution)/shard_map/ppermute | solution.py:52
  52.0 4.2 %collective-permute-done.10 = bf16[512,512]{1,0:T(8,128)(2,1)S(1)} collective-permute-done((bf16[512,512]{1,0:T(8,128)(2,1)S(1)}, bf16[512,512]{1,0:T(8,128)(2,1)S(1)}, u32[]{:S(2)}, u32[]{:S(2)}) %collective-permute-start.10) | collective-permute-done | bytes 524320 | tf_op jit(solution)/shard_map/ppermute | solution.py:52
  56.2 1.9 collective-permute-start.11
  58.2 1.4 collective-permute-done.4
  59.6 1.9 collective-permute-start.5
  61.6 1.3 opening.1
  63.1 1.1 collective-permute-done.5.other_in.refs_2_
  64.2 1.2 layer_up_0.3
  65.4 1.9 collective-permute-start.29
  67.3 1.2 layer_up_0.2
  68.5 1.3 collective-permute-start.12
  69.8 1.2 collective-permute-done.29.refs_6_
  71.7 1.9 collective-permute-done.12.refs_6_
  78.6 9.7 %collective-permute-start.34 = (bf16[2,64,512]{2,1,0:T(8,128)(2,1)S(1)}, bf16[2,64,512]{2,1,0:T(8,128)(2,1)S(1)}, u32[]{:S(2)}, u32[]{:S(2)}) collective-permute-start(bf16[2,64,512]{2,1,0:T(8,128)(2,1)S(1)} %get-tuple-element.159), channel_id=1, source_target_pairs={{0,65},{1,64},{2,67},{3,66},{4,69},{5,68},{6,71},{7,70},{8,73},{9,... | collective-permute-start | bytes 393224 | tf_op jit(solution)/shard_map/ppermute | solution.py:52
  88.3 1.3 collective-permute-start.17
  89.6 1.2 collective-permute-done.34.refs_6_
  90.7 0.8 collective-permute-start.35
  94.9 2.0 turned_weights.1
  99.8 1.3 collective-permute-start.39
  101.2 1.3 collective-permute-start.23
  102.5 20.3 %collective-permute-done.39.refs_1_ = bf16[2,64,512]{2,1,0:T(8,128)(2,1)S(1)} collective-permute-done((bf16[2,64,512]{2,1,0:T(8,128)(2,1)S(1)}, bf16[2,64,512]{2,1,0:T(8,128)(2,1)S(1)}, u32[]{:S(2)}, u32[]{:S(2)}) %collective-permute-start.39) | collective-permute-done | bytes 131104 | tf_op jit(solution)/shard_map/ppermute | solution.py:52
  129.1 1.3 collective-permute-start.44
  130.4 1.3 collective-permute-start.28
  131.7 60.2 %collective-permute-done.44.refs_1_ = bf16[2,64,512]{2,1,0:T(8,128)(2,1)S(1)} collective-permute-done((bf16[2,64,512]{2,1,0:T(8,128)(2,1)S(1)}, bf16[2,64,512]{2,1,0:T(8,128)(2,1)S(1)}, u32[]{:S(2)}, u32[]{:S(2)}) %collective-permute-start.44) | collective-permute-done | bytes 131104 | tf_op jit(solution)/shard_map/ppermute | solution.py:52
  191.9 1.4 curvature_first.1
  193.3 1.5 collective-permute-done.28.refs_1_
  194.8 1.4 curvature_last.1
  196.1 2.0 collective-permute-start.45
  198.2 2.5 %collective-permute-done.45 = bf16[256,2048]{1,0:T(8,128)(2,1)S(1)} collective-permute-done((bf16[256,2048]{1,0:T(8,128)(2,1)S(1)}, bf16[256,2048]{1,0:T(8,128)(2,1)S(1)}, u32[]{:S(2)}, u32[]{:S(2)}) %collective-permute-start.45) | collective-permute-done | bytes 1048608 | tf_op jit(solution)/shard_map/ppermute | solution.py:52
  201.0 18.7 %all_to_all.10 = bf16[4,64,2048]{2,1,0:T(8,128)(2,1)S(1)} all-to-all(bf16[4,64,2048]{2,1,0:T(8,128)(2,1)S(1)} %bitcast.32), channel_id=1, replica_groups=mesh['zh'=2,'x'=4,'b4'=2,'b2'=2,'b1'=2,'y'=4,'c'=2] {'y'}, dimensions={0} | all-to-all | bytes 2097152 | tf_op jit(solution)/shard_map/all_to_all | solution.py:567
  219.8 0.9 reduce_sum.23
  220.7 5.2 %all-to-all-start.1 = ((bf16[8,8,2048]{2,1,0:T(8,128)(2,1)}), bf16[8,8,2048]{2,1,0:T(8,128)(2,1)S(1)}, u32[]{:S(2)}, u32[]{:S(2)}) async-start(bf16[8,8,2048]{2,1,0:T(8,128)(2,1)} %bitcast.10), calls=%async_computation.1 | async-start | bytes 524288 | tf_op jit(solution)/shard_map/all_to_all | solution.py:569
  225.9 15.5 %all-to-all-done.1 = bf16[8,8,2048]{2,1,0:T(8,128)(2,1)S(1)} async-done(((bf16[8,8,2048]{2,1,0:T(8,128)(2,1)}), bf16[8,8,2048]{2,1,0:T(8,128)(2,1)S(1)}, u32[]{:S(2)}, u32[]{:S(2)}) %all-to-all-start.1) | async-done | bytes 262176 | tf_op jit(solution)/shard_map/all_to_all | solution.py:569
  (116 shorter events, 20.5 us)
Async XLA Ops:
  0.0 37.4 %copy-start.3 = (bf16[1,8,2048]{2,1,0:T(8,128)(2,1)S(1)}, bf16[1,8,2048]{2,1,0:T(8,128)(2,1)}, u32[]{:S(2)}) copy-start(bf16[1,8,2048]{2,1,0:T(8,128)(2,1)} %param.7) | copy-start | bytes 98308
  0.8 11.8 %collective-permute-start.6 = (bf16[32,512]{1,0:T(8,128)(2,1)S(1)}, bf16[32,512]{1,0:T(8,128)(2,1)S(1)}, u32[]{:S(2)}, u32[]{:S(2)}) collective-permute-start(bf16[32,512]{1,0:T(8,128)(2,1)S(1)} %settled.1), channel_id=1, source_target_pairs={{0,32},{1,33},{2,34},{3,35},{4,36},{5,37},{6,38},{7,39},{8,40},{9,... | collective-permute-start | bytes 98312 | tf_op jit(solution)/shard_map/ppermute | solution.py:52
  9.9 10.3 %collective-permute-start = (bf16[8,2048]{1,0:T(8,128)(2,1)}, bf16[8,2048]{1,0:T(8,128)(2,1)S(1)}, u32[]{:S(2)}, u32[]{:S(2)}) collective-permute-start(bf16[8,2048]{1,0:T(8,128)(2,1)} %bitcast.33), channel_id=1, source_target_pairs={{0,32},{1,33},{2,34},{3,35},{4,36},{5,37},{6,38},{7,39},{8,40},{9,... | collective-permute-start | bytes 98312 | tf_op jit(solution)/shard_map/ppermute | solution.py:52
  12.6 13.6 %collective-permute-start.7 = (bf16[64,512]{1,0:T(8,128)(2,1)S(1)}, bf16[64,512]{1,0:T(8,128)(2,1)S(1)}, u32[]{:S(2)}, u32[]{:S(2)}) collective-permute-start(bf16[64,512]{1,0:T(8,128)(2,1)S(1)} %pad_maximum_fusion.5), channel_id=1, source_target_pairs={{0,16},{1,17},{2,18},{3,19},{4,20},{5,21},{6,22},{7,23},{8,24},{9,... | collective-permute-start | bytes 196616 | tf_op jit(solution)/shard_map/ppermute | solution.py:52
  20.9 8.8 %collective-permute-start.1 = (bf16[16,2048]{1,0:T(8,128)(2,1)S(1)}, bf16[16,2048]{1,0:T(8,128)(2,1)S(1)}, u32[]{:S(2)}, u32[]{:S(2)}) collective-permute-start(bf16[16,2048]{1,0:T(8,128)(2,1)S(1)} %pad_maximum_fusion.4), channel_id=1, source_target_pairs={{0,16},{1,17},{2,18},{3,19},{4,20},{5,21},{6,22},{7,23},{8,24},{9,... | collective-permute-start | bytes 196616 | tf_op jit(solution)/shard_map/ppermute | solution.py:52
  26.2 7.2 %collective-permute-start.8 = (bf16[128,512]{1,0:T(8,128)(2,1)S(1)}, bf16[128,512]{1,0:T(8,128)(2,1)S(1)}, u32[]{:S(2)}, u32[]{:S(2)}) collective-permute-start(bf16[128,512]{1,0:T(8,128)(2,1)S(1)} %pad_maximum_fusion.3), channel_id=1, source_target_pairs={{0,8},{1,9},{2,10},{3,11},{4,12},{5,13},{6,14},{7,15},{8,0},{9,1},... | collective-permute-start | bytes 393224 | tf_op jit(solution)/shard_map/ppermute | solution.py:52
  30.5 6.9 %collective-permute-start.2 = (bf16[32,2048]{1,0:T(8,128)(2,1)S(1)}, bf16[32,2048]{1,0:T(8,128)(2,1)S(1)}, u32[]{:S(2)}, u32[]{:S(2)}) collective-permute-start(bf16[32,2048]{1,0:T(8,128)(2,1)S(1)} %pad_maximum_fusion.2), channel_id=1, source_target_pairs={{0,8},{1,9},{2,10},{3,11},{4,12},{5,13},{6,14},{7,15},{8,0},{9,1},... | collective-permute-start | bytes 393224 | tf_op jit(solution)/shard_map/ppermute | solution.py:52
  33.4 8.3 %collective-permute-start.9 = (bf16[256,512]{1,0:T(8,128)(2,1)S(1)}, bf16[256,512]{1,0:T(8,128)(2,1)S(1)}, u32[]{:S(2)}, u32[]{:S(2)}) collective-permute-start(bf16[256,512]{1,0:T(8,128)(2,1)S(1)} %pad_maximum_fusion.1), channel_id=1, source_target_pairs={{0,6},{1,7},{2,4},{3,5},{4,2},{5,3},{6,0},{7,1},{8,14},{9,15},{10,... | collective-permute-start | bytes 786440 | tf_op jit(solution)/shard_map/ppermute | solution.py:52
  37.4 11.0 %collective-permute-start.3 = (bf16[64,2048]{1,0:T(8,128)(2,1)S(1)}, bf16[64,2048]{1,0:T(8,128)(2,1)S(1)}, u32[]{:S(2)}, u32[]{:S(2)}) collective-permute-start(bf16[64,2048]{1,0:T(8,128)(2,1)S(1)} %pad_maximum_fusion), channel_id=1, source_target_pairs={{0,2},{1,3},{2,0},{3,1},{4,6},{5,7},{6,4},{7,5},{8,10},{9,11},{10,... | collective-permute-start | bytes 786440 | tf_op jit(solution)/shard_map/ppermute | solution.py:52
  41.7 14.5 %collective-permute-start.10 = (bf16[512,512]{1,0:T(8,128)(2,1)S(1)}, bf16[512,512]{1,0:T(8,128)(2,1)S(1)}, u32[]{:S(2)}, u32[]{:S(2)}) collective-permute-start(bf16[512,512]{1,0:T(8,128)(2,1)S(1)} %get-tuple-element.203), channel_id=1, source_target_pairs={{0,2},{1,3},{2,0},{3,1},{4,6},{5,7},{6,4},{7,5},{8,10},{9,11},{10,... | collective-permute-start | bytes 1572872 | tf_op jit(solution)/shard_map/ppermute | solution.py:52
  48.5 11.1 %collective-permute-start.4 = (bf16[128,2048]{1,0:T(8,128)(2,1)S(1)}, bf16[128,2048]{1,0:T(8,128)(2,1)S(1)}, u32[]{:S(2)}, u32[]{:S(2)}) collective-permute-start(bf16[128,2048]{1,0:T(8,128)(2,1)S(1)} %get-tuple-element.205), channel_id=1, source_target_pairs={{0,6},{1,7},{2,4},{3,5},{4,2},{5,3},{6,0},{7,1},{8,14},{9,15},{10,... | collective-permute-start | bytes 1572872 | tf_op jit(solution)/shard_map/ppermute | solution.py:52
  56.2 6.6 %collective-permute-start.11 = (bf16[1024,512]{1,0:T(8,128)(2,1)S(1)}, bf16[1024,512]{1,0:T(8,128)(2,1)S(1)}, u32[]{:S(2)}, u32[]{:S(2)}) collective-permute-start(bf16[1024,512]{1,0:T(8,128)(2,1)S(1)} %constant_dynamic-update-slice_fusion.16.refs_6_), channel_id=1, source_target_pairs={{0,1},{1,0},{2,3},{3,2},{4,5},{5,4},{6,7},{7,6},{8,9},{9,8},{10,11... | collective-permute-start | bytes 3145736 | tf_op jit(solution)/shard_map/ppermute | solution.py:52
  59.6 4.6 %collective-permute-start.5 = (bf16[256,2048]{1,0:T(8,128)(2,1)S(1)}, bf16[256,2048]{1,0:T(8,128)(2,1)S(1)}, u32[]{:S(2)}, u32[]{:S(2)}) collective-permute-start(bf16[256,2048]{1,0:T(8,128)(2,1)S(1)} %constant_dynamic-update-slice_fusion.5.own_in.refs_1_), channel_id=1, source_target_pairs={{0,1},{1,0},{2,3},{3,2},{4,5},{5,4},{6,7},{7,6},{8,9},{9,8},{10,11... | collective-permute-start | bytes 3145736 | tf_op jit(solution)/shard_map/ppermute | solution.py:52
  65.4 5.7 %collective-permute-start.29 = (bf16[2,64,512]{2,1,0:T(8,128)(2,1)S(1)}, bf16[2,64,512]{2,1,0:T(8,128)(2,1)S(1)}, u32[]{:S(2)}, u32[]{:S(2)}) collective-permute-start(bf16[2,64,512]{2,1,0:T(8,128)(2,1)S(1)} %get-tuple-element.155), channel_id=1, source_target_pairs={{0,65},{1,64},{2,67},{3,66},{4,69},{5,68},{6,71},{7,70},{8,73},{9,... | collective-permute-start | bytes 393224 | tf_op jit(solution)/shard_map/ppermute | solution.py:52
  68.5 5.1 %collective-permute-start.12 = (bf16[2,64,512]{2,1,0:T(8,128)(2,1)S(1)}, bf16[2,64,512]{2,1,0:T(8,128)(2,1)S(1)}, u32[]{:S(2)}, u32[]{:S(2)}) collective-permute-start(bf16[2,64,512]{2,1,0:T(8,128)(2,1)S(1)} %get-tuple-element.107), channel_id=1, source_target_pairs={{0,65},{1,64},{2,67},{3,66},{4,69},{5,68},{6,71},{7,70},{8,73},{9,... | collective-permute-start | bytes 393224 | tf_op jit(solution)/shard_map/ppermute | solution.py:52
  71.1 3.3 %collective-permute-start.30 = (bf16[2,64,512]{2,1,0:T(8,128)(2,1)S(1)}, bf16[2,64,512]{2,1,0:T(8,128)(2,1)S(1)}, u32[]{:S(2)}, u32[]{:S(2)}) collective-permute-start(bf16[2,64,512]{2,1,0:T(8,128)(2,1)S(1)} %get-tuple-element.156), channel_id=1, source_target_pairs={{64,129},{65,128},{66,131},{67,130},{68,133},{69,132},{70,135},{71... | collective-permute-start | bytes 393224 | tf_op jit(solution)/shard_map/ppermute | solution.py:52
  73.7 1.4 collective-permute-start.13
  74.4 1.4 collective-permute-start.31
  75.1 1.4 collective-permute-start.14
  75.8 1.4 collective-permute-start.32
  76.5 1.4 collective-permute-start.15
  77.2 1.4 collective-permute-start.33
  77.8 10.4 %collective-permute-start.16 = (bf16[2,64,512]{2,1,0:T(8,128)(2,1)S(1)}, bf16[2,64,512]{2,1,0:T(8,128)(2,1)S(1)}, u32[]{:S(2)}, u32[]{:S(2)}) collective-permute-start(bf16[2,64,512]{2,1,0:T(8,128)(2,1)S(1)} %collective-permute-done.15.refs_6_), channel_id=1, source_target_pairs={{1,313},{3,315},{5,317},{7,319},{9,305},{11,307},{13,309},{15,311}... | collective-permute-start | bytes 393224 | tf_op jit(solution)/shard_map/ppermute | solution.py:52
  78.6 12.2 %collective-permute-start.34 = (bf16[2,64,512]{2,1,0:T(8,128)(2,1)S(1)}, bf16[2,64,512]{2,1,0:T(8,128)(2,1)S(1)}, u32[]{:S(2)}, u32[]{:S(2)}) collective-permute-start(bf16[2,64,512]{2,1,0:T(8,128)(2,1)S(1)} %get-tuple-element.159), channel_id=1, source_target_pairs={{0,65},{1,64},{2,67},{3,66},{4,69},{5,68},{6,71},{7,70},{8,73},{9,... | collective-permute-start | bytes 393224 | tf_op jit(solution)/shard_map/ppermute | solution.py:52
  88.3 3.8 %collective-permute-start.17 = (bf16[2,64,512]{2,1,0:T(8,128)(2,1)S(1)}, bf16[2,64,512]{2,1,0:T(8,128)(2,1)S(1)}, u32[]{:S(2)}, u32[]{:S(2)}) collective-permute-start(bf16[2,64,512]{2,1,0:T(8,128)(2,1)S(1)} %get-tuple-element.111), channel_id=1, source_target_pairs={{0,65},{1,64},{2,67},{3,66},{4,69},{5,68},{6,71},{7,70},{8,73},{9,... | collective-permute-start | bytes 393224 | tf_op jit(solution)/shard_map/ppermute | solution.py:52
  90.7 2.7 %collective-permute-start.35 = (bf16[2,64,512]{2,1,0:T(8,128)(2,1)S(1)}, bf16[2,64,512]{2,1,0:T(8,128)(2,1)S(1)}, u32[]{:S(2)}, u32[]{:S(2)}) collective-permute-start(bf16[2,64,512]{2,1,0:T(8,128)(2,1)S(1)} %get-tuple-element.160), channel_id=1, source_target_pairs={{64,129},{65,128},{66,131},{67,130},{68,133},{69,132},{70,135},{71... | collective-permute-start | bytes 393224 | tf_op jit(solution)/shard_map/ppermute | solution.py:52
  92.1 2.1 collective-permute-start.18
  92.8 2.1 collective-permute-start.20
  93.5 3.5 %collective-permute-start.36 = (bf16[2,64,512]{2,1,0:T(8,128)(2,1)S(1)}, bf16[2,64,512]{2,1,0:T(8,128)(2,1)S(1)}, u32[]{:S(2)}, u32[]{:S(2)}) collective-permute-start(bf16[2,64,512]{2,1,0:T(8,128)(2,1)S(1)} %get-tuple-element.161), channel_id=1, source_target_pairs={{128,193},{129,192},{130,195},{131,194},{132,197},{133,196},{134,1... | collective-permute-start | bytes 393224 | tf_op jit(solution)/shard_map/ppermute | solution.py:52
  94.2 3.5 %collective-permute-start.19 = (bf16[2,64,512]{2,1,0:T(8,128)(2,1)S(1)}, bf16[2,64,512]{2,1,0:T(8,128)(2,1)S(1)}, u32[]{:S(2)}, u32[]{:S(2)}) collective-permute-start(bf16[2,64,512]{2,1,0:T(8,128)(2,1)S(1)} %get-tuple-element.113), channel_id=1, source_target_pairs={{128,193},{129,192},{130,195},{131,194},{132,197},{133,196},{134,1... | collective-permute-start | bytes 393224 | tf_op jit(solution)/shard_map/ppermute | solution.py:52
  97.0 1.4 collective-permute-start.37
  97.7 1.4 collective-permute-start.21
  98.4 1.4 collective-permute-start.38
  99.1 2.0 collective-permute-start.22
  99.8 22.9 %collective-permute-start.39 = (bf16[2,64,512]{2,1,0:T(8,128)(2,1)S(1)}, bf16[2,64,512]{2,1,0:T(8,128)(2,1)S(1)}, u32[]{:S(2)}, u32[]{:S(2)}) collective-permute-start(bf16[2,64,512]{2,1,0:T(8,128)(2,1)S(1)} %get-tuple-element.174), channel_id=1, source_target_pairs={{64,1},{65,0},{66,3},{67,2},{68,5},{69,4},{70,7},{71,6},{72,9},{73... | collective-permute-start | bytes 393224 | tf_op jit(solution)/shard_map/ppermute | solution.py:52
  101.2 23.0 %collective-permute-start.23 = (bf16[2,64,512]{2,1,0:T(8,128)(2,1)S(1)}, bf16[2,64,512]{2,1,0:T(8,128)(2,1)S(1)}, u32[]{:S(2)}, u32[]{:S(2)}) collective-permute-start(bf16[2,64,512]{2,1,0:T(8,128)(2,1)S(1)} %get-tuple-element.130), channel_id=1, source_target_pairs={{64,1},{65,0},{66,3},{67,2},{68,5},{69,4},{70,7},{71,6},{72,9},{73... | collective-permute-start | bytes 393224 | tf_op jit(solution)/shard_map/ppermute | solution.py:52
  122.8 2.1 collective-permute-start.40
  124.2 1.4 collective-permute-start.24
  124.8 1.4 collective-permute-start.41
  125.5 1.4 collective-permute-start.25
  126.2 1.4 collective-permute-start.42
  126.9 1.4 collective-permute-start.26
  127.6 1.4 collective-permute-start.43
  128.3 2.0 collective-permute-start.27
  129.1 62.9 %collective-permute-start.44 = (bf16[2,64,512]{2,1,0:T(8,128)(2,1)S(1)}, bf16[2,64,512]{2,1,0:T(8,128)(2,1)S(1)}, u32[]{:S(2)}, u32[]{:S(2)}) collective-permute-start(bf16[2,64,512]{2,1,0:T(8,128)(2,1)S(1)} %get-tuple-element.190), channel_id=1, source_target_pairs={{64,1},{65,0},{66,3},{67,2},{68,5},{69,4},{70,7},{71,6},{72,9},{73... | collective-permute-start | bytes 393224 | tf_op jit(solution)/shard_map/ppermute | solution.py:52
  130.4 64.4 %collective-permute-start.28 = (bf16[2,64,512]{2,1,0:T(8,128)(2,1)S(1)}, bf16[2,64,512]{2,1,0:T(8,128)(2,1)S(1)}, u32[]{:S(2)}, u32[]{:S(2)}) collective-permute-start(bf16[2,64,512]{2,1,0:T(8,128)(2,1)S(1)} %get-tuple-element.145), channel_id=1, source_target_pairs={{64,1},{65,0},{66,3},{67,2},{68,5},{69,4},{70,7},{71,6},{72,9},{73... | collective-permute-start | bytes 393224 | tf_op jit(solution)/shard_map/ppermute | solution.py:52
  196.1 4.6 %collective-permute-start.45 = (bf16[256,2048]{1,0:T(8,128)(2,1)S(1)}, bf16[256,2048]{1,0:T(8,128)(2,1)S(1)}, u32[]{:S(2)}, u32[]{:S(2)}) collective-permute-start(bf16[256,2048]{1,0:T(8,128)(2,1)S(1)} %get-tuple-element.202), channel_id=1, source_target_pairs={{0,1},{1,0},{2,3},{3,2},{4,5},{5,4},{6,7},{7,6},{8,9},{9,8},{10,11... | collective-permute-start | bytes 3145736 | tf_op jit(solution)/shard_map/ppermute | solution.py:52
  220.7 20.8 %all-to-all-start.1 = ((bf16[8,8,2048]{2,1,0:T(8,128)(2,1)}), bf16[8,8,2048]{2,1,0:T(8,128)(2,1)S(1)}, u32[]{:S(2)}, u32[]{:S(2)}) async-start(bf16[8,8,2048]{2,1,0:T(8,128)(2,1)} %bitcast.10), calls=%async_computation.1 | async-start | bytes 524288 | tf_op jit(solution)/shard_map/all_to_all | solution.py:569
  (4 other events, 44.3 us)

commit v6 on v2

--- a/solution.py
+++ b/solution.py
@@ -81,24 +81,32 @@
 
 def up_from(section):
     def route(zh, x, b4, b2, b1, y, c):
-        if x != section % 4 or (x == 3 and zh == 1):
-            return None
-        if x == 3:
-            return (1, 0, 1 - b4, 1 - b2, 1 - b1, y, c)
-        return (zh, x + 1, b4, b2, b1, y, c)
+        return (zh, x + 1, b4, b2, b1, y, c) if x == section % 4 else None
 
     return route
 
 
 def down_from(section):
     def route(zh, x, b4, b2, b1, y, c):
-        if x != section % 4 or (x == 0 and zh == 0):
+        return (zh, x - 1, b4, b2, b1, y, c) if x == section % 4 else None
+
+    return route
+
+
+def crossing(half, x_from, x_to):
+    def first(zh, x, b4, b2, b1, y, c):
+        if (zh, x) != (half, x_from):
             return None
-        if x == 0:
-            return (0, 3, 1 - b4, 1 - b2, 1 - b1, y, c)
-        return (zh, x - 1, b4, b2, b1, y, c)
-
-    return route
+        return (zh, x_to, b4, b2, b1, y, c) if c else (1 - zh, x, 1 - b4, 1 - b2, 1 - b1, y, c)
+
+    def second(zh, x, b4, b2, b1, y, c):
+        if (zh, x, c) == (1 - half, x_from, 0):
+            return (zh, x_to, b4, b2, b1, y, c)
+        if (zh, x, c) == (half, x_to, 1):
+            return (1 - zh, x, 1 - b4, 1 - b2, 1 - b1, y, c)
+        return None
+
+    return lambda pair: routed(routed(pair, first), second)
 
 
 def doubled(block, route):
@@ -517,7 +525,9 @@
                     tick, section, pairs[micro], own_in, other_in, probe, full_out, order, goal_now
                 )
                 kept[micro].append(stores)
-            if tick < LAYERS - 1:
+            if tick + 1 == LAYERS // 2:
+                pairs[micro] = crossing(0, 3, 0)(pairs[micro])
+            elif tick < LAYERS - 1:
                 pairs[micro] = routed(pairs[micro], up_from(tick))
         if tick == TURN_TICK:
             turned = turned_call(own_in, other_in, probe, full_out, order, kept[-1][-1][0])
@@ -527,7 +537,10 @@
                 tick, section, pairs[micro], *turned, kept[micro][LAYERS - 2 - tick]
             )
             grads[micro].append(low_grads)
-            pairs[micro] = routed(pairs[micro], down_from(LAYERS - 1 - tick))
+            if tick + 1 == LAYERS // 2:
+                pairs[micro] = crossing(1, 0, 3)(pairs[micro])
+            else:
+                pairs[micro] = routed(pairs[micro], down_from(LAYERS - 1 - tick))
     sums = ()
     for micro in range(MICRO):
         norms = [stores[0] for stores in kept[micro]]

time: 241 us -> 245 us (1.017)
  starting transfers between devices: 85.3 us -> 90.8 us
    ppermute x42 -> x46, starting transfers between devices: 80.8 us -> 85.7 us  [routed(): return lax.ppermute(value, NAMES, pairs)]
    ppermute x42 -> x46, waiting for transfers between devices: 104 us -> 102 us  [routed(): return lax.ppermute(value, NAMES, pairs)]
  transfers between devices with their start and end apart: 43 -> 47, of which waited for: 18 -> 22; matrix products, arithmetic and copies ran while one was open for 1% -> 1% of each run, Pallas kernels for 3% -> 3%
where the time goes in v6:
time: 245 us; the launch traced here: 244 us
  waiting for transfers between devices  118 us (48%)
  starting transfers between devices  90.8 us (37%)
  blocking collectives  19.8 us (8%)
  Pallas kernels  8.95 us (4%)
  other arithmetic  3.51 us (1%)
    ppermute x46, waiting for transfers between devices, routed(): return lax.ppermute(value, NAMES, pairs)  102 us
    ppermute x46, starting transfers between devices, routed(): return lax.ppermute(value, NAMES, pairs)  85.7 us
    all_to_all x1, blocking collectives, shards(): lax.all_to_all(summed.reshape(4, 64, HIDDEN), 'y', 0, 0, tiled=True)  19.8 us
    all_to_all x1, waiting for transfers between devices, shards(): lax.all_to_all(summed.reshape(8, 8, HIDDEN), ('b1', 'b2', 'b4'), 0, 0, ti...  16.2 us
    all_to_all x1, starting transfers between devices, shards(): lax.all_to_all(summed.reshape(8, 8, HIDDEN), ('b1', 'b2', 'b4'), 0, 0, ti...  5.1 us
  transfers between devices with their start and end apart: 47, of which 22 were waited for; matrix products, arithmetic and copies ran while one was open for 1% of the time, Pallas kernels for 3%

profile of v6, /device:TPU:8, one launch (start us, length us, event | category | flops | bytes accessed | tf_op | source)
XLA Modules:
  0.0 243.9 jit_solution(9344969600193952279)
XLA Ops:
  0.8 9.1 %collective-permute-start.6 = (bf16[32,512]{1,0:T(8,128)(2,1)S(1)}, bf16[32,512]{1,0:T(8,128)(2,1)S(1)}, u32[]{:S(2)}, u32[]{:S(2)}) collective-permute-start(bf16[32,512]{1,0:T(8,128)(2,1)S(1)} %settled.1), channel_id=1, source_target_pairs={{0,32},{1,33},{2,34},{3,35},{4,36},{5,37},{6,38},{7,39},{8,40},{9,... | collective-permute-start | bytes 98312 | tf_op jit(solution)/shard_map/ppermute | solution.py:51
  9.9 1.9 collective-permute-start
  12.6 5.2 %collective-permute-start.7 = (bf16[64,512]{1,0:T(8,128)(2,1)S(1)}, bf16[64,512]{1,0:T(8,128)(2,1)S(1)}, u32[]{:S(2)}, u32[]{:S(2)}) collective-permute-start(bf16[64,512]{1,0:T(8,128)(2,1)S(1)} %pad_maximum_fusion.5), channel_id=1, source_target_pairs={{0,16},{1,17},{2,18},{3,19},{4,20},{5,21},{6,22},{7,23},{8,24},{9,... | collective-permute-start | bytes 196616 | tf_op jit(solution)/shard_map/ppermute | solution.py:51
  17.8 2.4 collective-permute-done
  20.9 5.2 %collective-permute-start.1 = (bf16[16,2048]{1,0:T(8,128)(2,1)S(1)}, bf16[16,2048]{1,0:T(8,128)(2,1)S(1)}, u32[]{:S(2)}, u32[]{:S(2)}) collective-permute-start(bf16[16,2048]{1,0:T(8,128)(2,1)S(1)} %pad_maximum_fusion.4), channel_id=1, source_target_pairs={{0,16},{1,17},{2,18},{3,19},{4,20},{5,21},{6,22},{7,23},{8,24},{9,... | collective-permute-start | bytes 196616 | tf_op jit(solution)/shard_map/ppermute | solution.py:51
  26.2 3.5 %collective-permute-start.8 = (bf16[128,512]{1,0:T(8,128)(2,1)S(1)}, bf16[128,512]{1,0:T(8,128)(2,1)S(1)}, u32[]{:S(2)}, u32[]{:S(2)}) collective-permute-start(bf16[128,512]{1,0:T(8,128)(2,1)S(1)} %pad_maximum_fusion.3), channel_id=1, source_target_pairs={{0,8},{1,9},{2,10},{3,11},{4,12},{5,13},{6,14},{7,15},{8,0},{9,1},... | collective-permute-start | bytes 393224 | tf_op jit(solution)/shard_map/ppermute | solution.py:51
  30.5 2.8 %collective-permute-start.2 = (bf16[32,2048]{1,0:T(8,128)(2,1)S(1)}, bf16[32,2048]{1,0:T(8,128)(2,1)S(1)}, u32[]{:S(2)}, u32[]{:S(2)}) collective-permute-start(bf16[32,2048]{1,0:T(8,128)(2,1)S(1)} %pad_maximum_fusion.2), channel_id=1, source_target_pairs={{0,8},{1,9},{2,10},{3,11},{4,12},{5,13},{6,14},{7,15},{8,0},{9,1},... | collective-permute-start | bytes 393224 | tf_op jit(solution)/shard_map/ppermute | solution.py:51
  33.4 3.5 %collective-permute-start.9 = (bf16[256,512]{1,0:T(8,128)(2,1)S(1)}, bf16[256,512]{1,0:T(8,128)(2,1)S(1)}, u32[]{:S(2)}, u32[]{:S(2)}) collective-permute-start(bf16[256,512]{1,0:T(8,128)(2,1)S(1)} %pad_maximum_fusion.1), channel_id=1, source_target_pairs={{0,6},{1,7},{2,4},{3,5},{4,2},{5,3},{6,0},{7,1},{8,14},{9,15},{10,... | collective-permute-start | bytes 786440 | tf_op jit(solution)/shard_map/ppermute | solution.py:51
  37.4 3.3 %collective-permute-start.3 = (bf16[64,2048]{1,0:T(8,128)(2,1)S(1)}, bf16[64,2048]{1,0:T(8,128)(2,1)S(1)}, u32[]{:S(2)}, u32[]{:S(2)}) collective-permute-start(bf16[64,2048]{1,0:T(8,128)(2,1)S(1)} %pad_maximum_fusion), channel_id=1, source_target_pairs={{0,2},{1,3},{2,0},{3,1},{4,6},{5,7},{6,4},{7,5},{8,10},{9,11},{10,... | collective-permute-start | bytes 786440 | tf_op jit(solution)/shard_map/ppermute | solution.py:51
  41.7 3.6 %collective-permute-start.10 = (bf16[512,512]{1,0:T(8,128)(2,1)S(1)}, bf16[512,512]{1,0:T(8,128)(2,1)S(1)}, u32[]{:S(2)}, u32[]{:S(2)}) collective-permute-start(bf16[512,512]{1,0:T(8,128)(2,1)S(1)} %get-tuple-element.203), channel_id=1, source_target_pairs={{0,2},{1,3},{2,0},{3,1},{4,6},{5,7},{6,4},{7,5},{8,10},{9,11},{10,... | collective-permute-start | bytes 1572872 | tf_op jit(solution)/shard_map/ppermute | solution.py:51
  45.3 3.1 %collective-permute-done.3 = bf16[64,2048]{1,0:T(8,128)(2,1)S(1)} collective-permute-done((bf16[64,2048]{1,0:T(8,128)(2,1)S(1)}, bf16[64,2048]{1,0:T(8,128)(2,1)S(1)}, u32[]{:S(2)}, u32[]{:S(2)}) %collective-permute-start.3) | collective-permute-done | bytes 262176 | tf_op jit(solution)/shard_map/ppermute | solution.py:51
  48.5 3.5 %collective-permute-start.4 = (bf16[128,2048]{1,0:T(8,128)(2,1)S(1)}, bf16[128,2048]{1,0:T(8,128)(2,1)S(1)}, u32[]{:S(2)}, u32[]{:S(2)}) collective-permute-start(bf16[128,2048]{1,0:T(8,128)(2,1)S(1)} %get-tuple-element.205), channel_id=1, source_target_pairs={{0,6},{1,7},{2,4},{3,5},{4,2},{5,3},{6,0},{7,1},{8,14},{9,15},{10,... | collective-permute-start | bytes 1572872 | tf_op jit(solution)/shard_map/ppermute | solution.py:51
  52.0 4.2 %collective-permute-done.10 = bf16[512,512]{1,0:T(8,128)(2,1)S(1)} collective-permute-done((bf16[512,512]{1,0:T(8,128)(2,1)S(1)}, bf16[512,512]{1,0:T(8,128)(2,1)S(1)}, u32[]{:S(2)}, u32[]{:S(2)}) %collective-permute-start.10) | collective-permute-done | bytes 524320 | tf_op jit(solution)/shard_map/ppermute | solution.py:51
  56.2 1.9 collective-permute-start.11
  58.2 1.4 collective-permute-done.4
  59.6 1.9 collective-permute-start.5
  61.5 1.3 opening.1
  63.1 1.1 collective-permute-done.5.other_in.refs_3_
  64.2 1.2 layer_up_0.3
  65.4 2.2 collective-permute-start.29
  67.6 1.2 layer_up_0.2
  68.8 1.3 collective-permute-start.12
  71.5 1.9 collective-permute-done.12.refs_1_
  78.3 9.2 %collective-permute-start.34 = (bf16[2,64,512]{2,1,0:T(8,128)(2,1)S(1)}, bf16[2,64,512]{2,1,0:T(8,128)(2,1)S(1)}, u32[]{:S(2)}, u32[]{:S(2)}) collective-permute-start(bf16[2,64,512]{2,1,0:T(8,128)(2,1)S(1)} %get-tuple-element.159), channel_id=1, source_target_pairs={{0,64},{1,65},{2,66},{3,67},{4,68},{5,69},{6,70},{7,71},{8,72},{9,... | collective-permute-start | bytes 393224 | tf_op jit(solution)/shard_map/ppermute | solution.py:51
  87.5 1.3 collective-permute-start.17
  88.8 1.2 collective-permute-done.34.refs_1_
  94.1 2.0 turned_weights.1
  99.1 1.3 collective-permute-start.39
  100.4 1.3 collective-permute-start.23
  101.7 33.0 %collective-permute-done.39.refs_1_ = bf16[2,64,512]{2,1,0:T(8,128)(2,1)S(1)} collective-permute-done((bf16[2,64,512]{2,1,0:T(8,128)(2,1)S(1)}, bf16[2,64,512]{2,1,0:T(8,128)(2,1)S(1)}, u32[]{:S(2)}, u32[]{:S(2)}) %collective-permute-start.39) | collective-permute-done | bytes 131104 | tf_op jit(solution)/shard_map/ppermute | solution.py:51
  134.7 1.3 collective-permute-start.40
  136.0 1.2 collective-permute-done.23.refs_1_
  137.2 1.3 collective-permute-start.24
  138.5 28.2 %collective-permute-done.40 = bf16[2,64,512]{2,1,0:T(8,128)(2,1)S(1)} collective-permute-done((bf16[2,64,512]{2,1,0:T(8,128)(2,1)S(1)}, bf16[2,64,512]{2,1,0:T(8,128)(2,1)S(1)}, u32[]{:S(2)}, u32[]{:S(2)}) %collective-permute-start.40) | collective-permute-done | bytes 131104 | tf_op jit(solution)/shard_map/ppermute | solution.py:51
  166.8 1.3 collective-permute-start.41
  168.2 1.3 collective-permute-start.25
  169.5 1.1 collective-permute-done.41.refs_1_
  174.1 1.3 collective-permute-start.44
  175.4 1.3 collective-permute-start.28
  176.7 15.6 %collective-permute-done.44.refs_1_ = bf16[2,64,512]{2,1,0:T(8,128)(2,1)S(1)} collective-permute-done((bf16[2,64,512]{2,1,0:T(8,128)(2,1)S(1)}, bf16[2,64,512]{2,1,0:T(8,128)(2,1)S(1)}, u32[]{:S(2)}, u32[]{:S(2)}) %collective-permute-start.44) | collective-permute-done | bytes 131104 | tf_op jit(solution)/shard_map/ppermute | solution.py:51
  192.3 1.4 curvature_first.1
  193.7 1.3 collective-permute-done.28.refs_1_
  194.9 1.4 curvature_last.1
  196.3 1.9 collective-permute-start.45
  198.3 2.6 %collective-permute-done.45 = bf16[256,2048]{1,0:T(8,128)(2,1)S(1)} collective-permute-done((bf16[256,2048]{1,0:T(8,128)(2,1)S(1)}, bf16[256,2048]{1,0:T(8,128)(2,1)S(1)}, u32[]{:S(2)}, u32[]{:S(2)}) %collective-permute-start.45) | collective-permute-done | bytes 1048608 | tf_op jit(solution)/shard_map/ppermute | solution.py:51
  201.2 19.8 %all_to_all.10 = bf16[4,64,2048]{2,1,0:T(8,128)(2,1)S(1)} all-to-all(bf16[4,64,2048]{2,1,0:T(8,128)(2,1)S(1)} %bitcast.32), channel_id=1, replica_groups=mesh['zh'=2,'x'=4,'b4'=2,'b2'=2,'b1'=2,'y'=4,'c'=2] {'y'}, dimensions={0} | all-to-all | bytes 2097152 | tf_op jit(solution)/shard_map/all_to_all | solution.py:553
  221.9 5.1 %all-to-all-start.1 = ((bf16[8,8,2048]{2,1,0:T(8,128)(2,1)}), bf16[8,8,2048]{2,1,0:T(8,128)(2,1)S(1)}, u32[]{:S(2)}, u32[]{:S(2)}) async-start(bf16[8,8,2048]{2,1,0:T(8,128)(2,1)} %bitcast.10), calls=%async_computation.1 | async-start | bytes 524288 | tf_op jit(solution)/shard_map/all_to_all | solution.py:555
  227.0 16.2 %all-to-all-done.1 = bf16[8,8,2048]{2,1,0:T(8,128)(2,1)S(1)} async-done(((bf16[8,8,2048]{2,1,0:T(8,128)(2,1)}), bf16[8,8,2048]{2,1,0:T(8,128)(2,1)S(1)}, u32[]{:S(2)}, u32[]{:S(2)}) %all-to-all-start.1) | async-done | bytes 262176 | tf_op jit(solution)/shard_map/all_to_all | solution.py:555
  (116 shorter events, 23.5 us)
Async XLA Ops:
  0.0 37.4 %copy-start.3 = (bf16[1,8,2048]{2,1,0:T(8,128)(2,1)S(1)}, bf16[1,8,2048]{2,1,0:T(8,128)(2,1)}, u32[]{:S(2)}) copy-start(bf16[1,8,2048]{2,1,0:T(8,128)(2,1)} %param.7) | copy-start | bytes 98308
  0.8 11.8 %collective-permute-start.6 = (bf16[32,512]{1,0:T(8,128)(2,1)S(1)}, bf16[32,512]{1,0:T(8,128)(2,1)S(1)}, u32[]{:S(2)}, u32[]{:S(2)}) collective-permute-start(bf16[32,512]{1,0:T(8,128)(2,1)S(1)} %settled.1), channel_id=1, source_target_pairs={{0,32},{1,33},{2,34},{3,35},{4,36},{5,37},{6,38},{7,39},{8,40},{9,... | collective-permute-start | bytes 98312 | tf_op jit(solution)/shard_map/ppermute | solution.py:51
  9.9 10.3 %collective-permute-start = (bf16[8,2048]{1,0:T(8,128)(2,1)}, bf16[8,2048]{1,0:T(8,128)(2,1)S(1)}, u32[]{:S(2)}, u32[]{:S(2)}) collective-permute-start(bf16[8,2048]{1,0:T(8,128)(2,1)} %bitcast.33), channel_id=1, source_target_pairs={{0,32},{1,33},{2,34},{3,35},{4,36},{5,37},{6,38},{7,39},{8,40},{9,... | collective-permute-start | bytes 98312 | tf_op jit(solution)/shard_map/ppermute | solution.py:51
  12.6 13.6 %collective-permute-start.7 = (bf16[64,512]{1,0:T(8,128)(2,1)S(1)}, bf16[64,512]{1,0:T(8,128)(2,1)S(1)}, u32[]{:S(2)}, u32[]{:S(2)}) collective-permute-start(bf16[64,512]{1,0:T(8,128)(2,1)S(1)} %pad_maximum_fusion.5), channel_id=1, source_target_pairs={{0,16},{1,17},{2,18},{3,19},{4,20},{5,21},{6,22},{7,23},{8,24},{9,... | collective-permute-start | bytes 196616 | tf_op jit(solution)/shard_map/ppermute | solution.py:51
  20.9 8.8 %collective-permute-start.1 = (bf16[16,2048]{1,0:T(8,128)(2,1)S(1)}, bf16[16,2048]{1,0:T(8,128)(2,1)S(1)}, u32[]{:S(2)}, u32[]{:S(2)}) collective-permute-start(bf16[16,2048]{1,0:T(8,128)(2,1)S(1)} %pad_maximum_fusion.4), channel_id=1, source_target_pairs={{0,16},{1,17},{2,18},{3,19},{4,20},{5,21},{6,22},{7,23},{8,24},{9,... | collective-permute-start | bytes 196616 | tf_op jit(solution)/shard_map/ppermute | solution.py:51
  26.2 7.2 %collective-permute-start.8 = (bf16[128,512]{1,0:T(8,128)(2,1)S(1)}, bf16[128,512]{1,0:T(8,128)(2,1)S(1)}, u32[]{:S(2)}, u32[]{:S(2)}) collective-permute-start(bf16[128,512]{1,0:T(8,128)(2,1)S(1)} %pad_maximum_fusion.3), channel_id=1, source_target_pairs={{0,8},{1,9},{2,10},{3,11},{4,12},{5,13},{6,14},{7,15},{8,0},{9,1},... | collective-permute-start | bytes 393224 | tf_op jit(solution)/shard_map/ppermute | solution.py:51
  30.5 6.9 %collective-permute-start.2 = (bf16[32,2048]{1,0:T(8,128)(2,1)S(1)}, bf16[32,2048]{1,0:T(8,128)(2,1)S(1)}, u32[]{:S(2)}, u32[]{:S(2)}) collective-permute-start(bf16[32,2048]{1,0:T(8,128)(2,1)S(1)} %pad_maximum_fusion.2), channel_id=1, source_target_pairs={{0,8},{1,9},{2,10},{3,11},{4,12},{5,13},{6,14},{7,15},{8,0},{9,1},... | collective-permute-start | bytes 393224 | tf_op jit(solution)/shard_map/ppermute | solution.py:51
  33.4 8.3 %collective-permute-start.9 = (bf16[256,512]{1,0:T(8,128)(2,1)S(1)}, bf16[256,512]{1,0:T(8,128)(2,1)S(1)}, u32[]{:S(2)}, u32[]{:S(2)}) collective-permute-start(bf16[256,512]{1,0:T(8,128)(2,1)S(1)} %pad_maximum_fusion.1), channel_id=1, source_target_pairs={{0,6},{1,7},{2,4},{3,5},{4,2},{5,3},{6,0},{7,1},{8,14},{9,15},{10,... | collective-permute-start | bytes 786440 | tf_op jit(solution)/shard_map/ppermute | solution.py:51
  37.4 11.0 %collective-permute-start.3 = (bf16[64,2048]{1,0:T(8,128)(2,1)S(1)}, bf16[64,2048]{1,0:T(8,128)(2,1)S(1)}, u32[]{:S(2)}, u32[]{:S(2)}) collective-permute-start(bf16[64,2048]{1,0:T(8,128)(2,1)S(1)} %pad_maximum_fusion), channel_id=1, source_target_pairs={{0,2},{1,3},{2,0},{3,1},{4,6},{5,7},{6,4},{7,5},{8,10},{9,11},{10,... | collective-permute-start | bytes 786440 | tf_op jit(solution)/shard_map/ppermute | solution.py:51
  41.7 14.5 %collective-permute-start.10 = (bf16[512,512]{1,0:T(8,128)(2,1)S(1)}, bf16[512,512]{1,0:T(8,128)(2,1)S(1)}, u32[]{:S(2)}, u32[]{:S(2)}) collective-permute-start(bf16[512,512]{1,0:T(8,128)(2,1)S(1)} %get-tuple-element.203), channel_id=1, source_target_pairs={{0,2},{1,3},{2,0},{3,1},{4,6},{5,7},{6,4},{7,5},{8,10},{9,11},{10,... | collective-permute-start | bytes 1572872 | tf_op jit(solution)/shard_map/ppermute | solution.py:51
  48.5 11.1 %collective-permute-start.4 = (bf16[128,2048]{1,0:T(8,128)(2,1)S(1)}, bf16[128,2048]{1,0:T(8,128)(2,1)S(1)}, u32[]{:S(2)}, u32[]{:S(2)}) collective-permute-start(bf16[128,2048]{1,0:T(8,128)(2,1)S(1)} %get-tuple-element.205), channel_id=1, source_target_pairs={{0,6},{1,7},{2,4},{3,5},{4,2},{5,3},{6,0},{7,1},{8,14},{9,15},{10,... | collective-permute-start | bytes 1572872 | tf_op jit(solution)/shard_map/ppermute | solution.py:51
  56.2 6.6 %collective-permute-start.11 = (bf16[1024,512]{1,0:T(8,128)(2,1)S(1)}, bf16[1024,512]{1,0:T(8,128)(2,1)S(1)}, u32[]{:S(2)}, u32[]{:S(2)}) collective-permute-start(bf16[1024,512]{1,0:T(8,128)(2,1)S(1)} %constant_dynamic-update-slice_fusion.16.refs_6_), channel_id=1, source_target_pairs={{0,1},{1,0},{2,3},{3,2},{4,5},{5,4},{6,7},{7,6},{8,9},{9,8},{10,11... | collective-permute-start | bytes 3145736 | tf_op jit(solution)/shard_map/ppermute | solution.py:51
  59.6 4.6 %collective-permute-start.5 = (bf16[256,2048]{1,0:T(8,128)(2,1)S(1)}, bf16[256,2048]{1,0:T(8,128)(2,1)S(1)}, u32[]{:S(2)}, u32[]{:S(2)}) collective-permute-start(bf16[256,2048]{1,0:T(8,128)(2,1)S(1)} %constant_dynamic-update-slice_fusion.5.own_in.refs_2_), channel_id=1, source_target_pairs={{0,1},{1,0},{2,3},{3,2},{4,5},{5,4},{6,7},{7,6},{8,9},{9,8},{10,11... | collective-permute-start | bytes 3145736 | tf_op jit(solution)/shard_map/ppermute | solution.py:51
  65.4 5.4 %collective-permute-start.29 = (bf16[2,64,512]{2,1,0:T(8,128)(2,1)S(1)}, bf16[2,64,512]{2,1,0:T(8,128)(2,1)S(1)}, u32[]{:S(2)}, u32[]{:S(2)}) collective-permute-start(bf16[2,64,512]{2,1,0:T(8,128)(2,1)S(1)} %get-tuple-element.155), channel_id=1, source_target_pairs={{0,64},{1,65},{2,66},{3,67},{4,68},{5,69},{6,70},{7,71},{8,72},{9,... | collective-permute-start | bytes 393224 | tf_op jit(solution)/shard_map/ppermute | solution.py:51
  68.8 4.6 %collective-permute-start.12 = (bf16[2,64,512]{2,1,0:T(8,128)(2,1)S(1)}, bf16[2,64,512]{2,1,0:T(8,128)(2,1)S(1)}, u32[]{:S(2)}, u32[]{:S(2)}) collective-permute-start(bf16[2,64,512]{2,1,0:T(8,128)(2,1)S(1)} %get-tuple-element.107), channel_id=1, source_target_pairs={{0,64},{1,65},{2,66},{3,67},{4,68},{5,69},{6,70},{7,71},{8,72},{9,... | collective-permute-start | bytes 393224 | tf_op jit(solution)/shard_map/ppermute | solution.py:51
  70.8 3.3 %collective-permute-start.30 = (bf16[2,64,512]{2,1,0:T(8,128)(2,1)S(1)}, bf16[2,64,512]{2,1,0:T(8,128)(2,1)S(1)}, u32[]{:S(2)}, u32[]{:S(2)}) collective-permute-start(bf16[2,64,512]{2,1,0:T(8,128)(2,1)S(1)} %get-tuple-element.156), channel_id=1, source_target_pairs={{64,128},{65,129},{66,130},{67,131},{68,132},{69,133},{70,134},{71... | collective-permute-start | bytes 393224 | tf_op jit(solution)/shard_map/ppermute | solution.py:51
  73.4 1.4 collective-permute-start.13
  74.1 1.4 collective-permute-start.31
  74.8 1.4 collective-permute-start.14
  75.5 1.4 collective-permute-start.32
  76.2 1.4 collective-permute-start.15
  76.9 1.4 collective-permute-start.33
  77.6 9.9 %collective-permute-start.16 = (bf16[2,64,512]{2,1,0:T(8,128)(2,1)S(1)}, bf16[2,64,512]{2,1,0:T(8,128)(2,1)S(1)}, u32[]{:S(2)}, u32[]{:S(2)}) collective-permute-start(bf16[2,64,512]{2,1,0:T(8,128)(2,1)S(1)} %collective-permute-done.15), channel_id=1, source_target_pairs={{1,313},{3,315},{5,317},{7,319},{9,305},{11,307},{13,309},{15,311}... | collective-permute-start | bytes 393224 | tf_op jit(solution)/shard_map/ppermute | solution.py:51
  78.3 11.7 %collective-permute-start.34 = (bf16[2,64,512]{2,1,0:T(8,128)(2,1)S(1)}, bf16[2,64,512]{2,1,0:T(8,128)(2,1)S(1)}, u32[]{:S(2)}, u32[]{:S(2)}) collective-permute-start(bf16[2,64,512]{2,1,0:T(8,128)(2,1)S(1)} %get-tuple-element.159), channel_id=1, source_target_pairs={{0,64},{1,65},{2,66},{3,67},{4,68},{5,69},{6,70},{7,71},{8,72},{9,... | collective-permute-start | bytes 393224 | tf_op jit(solution)/shard_map/ppermute | solution.py:51
  87.5 3.8 %collective-permute-start.17 = (bf16[2,64,512]{2,1,0:T(8,128)(2,1)S(1)}, bf16[2,64,512]{2,1,0:T(8,128)(2,1)S(1)}, u32[]{:S(2)}, u32[]{:S(2)}) collective-permute-start(bf16[2,64,512]{2,1,0:T(8,128)(2,1)S(1)} %get-tuple-element.111), channel_id=1, source_target_pairs={{0,64},{1,65},{2,66},{3,67},{4,68},{5,69},{6,70},{7,71},{8,72},{9,... | collective-permute-start | bytes 393224 | tf_op jit(solution)/shard_map/ppermute | solution.py:51
  90.0 2.7 %collective-permute-start.35 = (bf16[2,64,512]{2,1,0:T(8,128)(2,1)S(1)}, bf16[2,64,512]{2,1,0:T(8,128)(2,1)S(1)}, u32[]{:S(2)}, u32[]{:S(2)}) collective-permute-start(bf16[2,64,512]{2,1,0:T(8,128)(2,1)S(1)} %get-tuple-element.160), channel_id=1, source_target_pairs={{64,128},{65,129},{66,130},{67,131},{68,132},{69,133},{70,134},{71... | collective-permute-start | bytes 393224 | tf_op jit(solution)/shard_map/ppermute | solution.py:51
  91.3 2.1 collective-permute-start.18
  92.0 2.1 collective-permute-start.20
  92.7 3.5 %collective-permute-start.36 = (bf16[2,64,512]{2,1,0:T(8,128)(2,1)S(1)}, bf16[2,64,512]{2,1,0:T(8,128)(2,1)S(1)}, u32[]{:S(2)}, u32[]{:S(2)}) collective-permute-start(bf16[2,64,512]{2,1,0:T(8,128)(2,1)S(1)} %get-tuple-element.161), channel_id=1, source_target_pairs={{128,192},{129,193},{130,194},{131,195},{132,196},{133,197},{134,1... | collective-permute-start | bytes 393224 | tf_op jit(solution)/shard_map/ppermute | solution.py:51
  93.4 3.5 %collective-permute-start.19 = (bf16[2,64,512]{2,1,0:T(8,128)(2,1)S(1)}, bf16[2,64,512]{2,1,0:T(8,128)(2,1)S(1)}, u32[]{:S(2)}, u32[]{:S(2)}) collective-permute-start(bf16[2,64,512]{2,1,0:T(8,128)(2,1)S(1)} %get-tuple-element.113), channel_id=1, source_target_pairs={{128,192},{129,193},{130,194},{131,195},{132,196},{133,197},{134,1... | collective-permute-start | bytes 393224 | tf_op jit(solution)/shard_map/ppermute | solution.py:51
  96.2 1.4 collective-permute-start.37
  97.0 1.4 collective-permute-start.21
  97.7 1.4 collective-permute-start.38
  98.4 2.0 collective-permute-start.22
  99.1 35.7 %collective-permute-start.39 = (bf16[2,64,512]{2,1,0:T(8,128)(2,1)S(1)}, bf16[2,64,512]{2,1,0:T(8,128)(2,1)S(1)}, u32[]{:S(2)}, u32[]{:S(2)}) collective-permute-start(bf16[2,64,512]{2,1,0:T(8,128)(2,1)S(1)} %get-tuple-element.174), channel_id=1, source_target_pairs={{64,0},{65,1},{66,2},{67,3},{68,4},{69,5},{70,6},{71,7},{72,8},{73... | collective-permute-start | bytes 393224 | tf_op jit(solution)/shard_map/ppermute | solution.py:51
  100.4 36.8 %collective-permute-start.23 = (bf16[2,64,512]{2,1,0:T(8,128)(2,1)S(1)}, bf16[2,64,512]{2,1,0:T(8,128)(2,1)S(1)}, u32[]{:S(2)}, u32[]{:S(2)}) collective-permute-start(bf16[2,64,512]{2,1,0:T(8,128)(2,1)S(1)} %get-tuple-element.130), channel_id=1, source_target_pairs={{64,0},{65,1},{66,2},{67,3},{68,4},{69,5},{70,6},{71,7},{72,8},{73... | collective-permute-start | bytes 393224 | tf_op jit(solution)/shard_map/ppermute | solution.py:51
  134.7 32.0 %collective-permute-start.40 = (bf16[2,64,512]{2,1,0:T(8,128)(2,1)S(1)}, bf16[2,64,512]{2,1,0:T(8,128)(2,1)S(1)}, u32[]{:S(2)}, u32[]{:S(2)}) collective-permute-start(bf16[2,64,512]{2,1,0:T(8,128)(2,1)S(1)} %get-tuple-element.178), channel_id=1, source_target_pairs={{256,56},{257,449},{258,58},{259,451},{260,60},{261,453},{262,62},... | collective-permute-start | bytes 393224 | tf_op jit(solution)/shard_map/ppermute | solution.py:51
  137.2 30.9 %collective-permute-start.24 = (bf16[2,64,512]{2,1,0:T(8,128)(2,1)S(1)}, bf16[2,64,512]{2,1,0:T(8,128)(2,1)S(1)}, u32[]{:S(2)}, u32[]{:S(2)}) collective-permute-start(bf16[2,64,512]{2,1,0:T(8,128)(2,1)S(1)} %get-tuple-element.134), channel_id=1, source_target_pairs={{256,56},{257,449},{258,58},{259,451},{260,60},{261,453},{262,62},... | collective-permute-start | bytes 393224 | tf_op jit(solution)/shard_map/ppermute | solution.py:51
  166.8 3.8 %collective-permute-start.41 = (bf16[2,64,512]{2,1,0:T(8,128)(2,1)S(1)}, bf16[2,64,512]{2,1,0:T(8,128)(2,1)S(1)}, u32[]{:S(2)}, u32[]{:S(2)}) collective-permute-start(bf16[2,64,512]{2,1,0:T(8,128)(2,1)S(1)} %collective-permute-done.40), channel_id=1, source_target_pairs={{0,192},{2,194},{4,196},{6,198},{8,200},{10,202},{12,204},{14,206}... | collective-permute-start | bytes 393224 | tf_op jit(solution)/shard_map/ppermute | solution.py:51
  168.2 3.8 %collective-permute-start.25 = (bf16[2,64,512]{2,1,0:T(8,128)(2,1)S(1)}, bf16[2,64,512]{2,1,0:T(8,128)(2,1)S(1)}, u32[]{:S(2)}, u32[]{:S(2)}) collective-permute-start(bf16[2,64,512]{2,1,0:T(8,128)(2,1)S(1)} %collective-permute-done.24), channel_id=1, source_target_pairs={{0,192},{2,194},{4,196},{6,198},{8,200},{10,202},{12,204},{14,206}... | collective-permute-start | bytes 393224 | tf_op jit(solution)/shard_map/ppermute | solution.py:51
  170.6 2.1 collective-permute-start.42
  172.0 1.4 collective-permute-start.26
  172.7 1.4 collective-permute-start.43
  173.4 2.0 collective-permute-start.27
  174.1 18.2 %collective-permute-start.44 = (bf16[2,64,512]{2,1,0:T(8,128)(2,1)S(1)}, bf16[2,64,512]{2,1,0:T(8,128)(2,1)S(1)}, u32[]{:S(2)}, u32[]{:S(2)}) collective-permute-start(bf16[2,64,512]{2,1,0:T(8,128)(2,1)S(1)} %get-tuple-element.190), channel_id=1, source_target_pairs={{64,0},{65,1},{66,2},{67,3},{68,4},{69,5},{70,6},{71,7},{72,8},{73... | collective-permute-start | bytes 393224 | tf_op jit(solution)/shard_map/ppermute | solution.py:51
  175.4 19.5 %collective-permute-start.28 = (bf16[2,64,512]{2,1,0:T(8,128)(2,1)S(1)}, bf16[2,64,512]{2,1,0:T(8,128)(2,1)S(1)}, u32[]{:S(2)}, u32[]{:S(2)}) collective-permute-start(bf16[2,64,512]{2,1,0:T(8,128)(2,1)S(1)} %get-tuple-element.145), channel_id=1, source_target_pairs={{64,0},{65,1},{66,2},{67,3},{68,4},{69,5},{70,6},{71,7},{72,8},{73... | collective-permute-start | bytes 393224 | tf_op jit(solution)/shard_map/ppermute | solution.py:51
  196.3 4.6 %collective-permute-start.45 = (bf16[256,2048]{1,0:T(8,128)(2,1)S(1)}, bf16[256,2048]{1,0:T(8,128)(2,1)S(1)}, u32[]{:S(2)}, u32[]{:S(2)}) collective-permute-start(bf16[256,2048]{1,0:T(8,128)(2,1)S(1)} %get-tuple-element.202), channel_id=1, source_target_pairs={{0,1},{1,0},{2,3},{3,2},{4,5},{5,4},{6,7},{7,6},{8,9},{9,8},{10,11... | collective-permute-start | bytes 3145736 | tf_op jit(solution)/shard_map/ppermute | solution.py:51
  221.9 21.3 %all-to-all-start.1 = ((bf16[8,8,2048]{2,1,0:T(8,128)(2,1)}), bf16[8,8,2048]{2,1,0:T(8,128)(2,1)S(1)}, u32[]{:S(2)}, u32[]{:S(2)}) async-start(bf16[8,8,2048]{2,1,0:T(8,128)(2,1)} %bitcast.10), calls=%async_computation.1 | async-start | bytes 524288 | tf_op jit(solution)/shard_map/all_to_all | solution.py:555
  (4 other events, 44.3 us)

commit v7 on v4

--- a/solution.py
+++ b/solution.py
@@ -24,7 +24,6 @@
 MICRO = 2
 ROWS = 128 // MICRO
 UNROLL_UP = 1
-UNROLL_DOWN = 2
 UNROLL_LAST = 2
 TURN_TICK = 3
 CROSS_TICK = 4
@@ -367,14 +366,14 @@
     )(own_in, other_in, probe, w_out, order, token)
 
 
-def hidden_grads(pair, w_out_t, slope, chunk):
+def hidden_grads(pair, w_out_t, slope, now):
     both = jnp.dot(
-        pair[...].reshape(2 * ROWS, FEATURES), w_out_t[:, columns(chunk)], preferred_element_type=jnp.float32
+        pair[...].reshape(2 * ROWS, FEATURES), w_out_t[:, now], preferred_element_type=jnp.float32
     )
     grad_hidden, grad_hidden_t = both[:ROWS], both[ROWS:]
-    slope_chunk = slope[0, :, columns(chunk)]
+    slope_chunk = slope[0, :, now]
     grad_pre = grad_hidden * slope_chunk
-    grad_pre_t = grad_hidden_t * slope_chunk + grad_hidden * slope[1, :, columns(chunk)]
+    grad_pre_t = grad_hidden_t * slope_chunk + grad_hidden * slope[1, :, now]
     return grad_pre.astype(jnp.bfloat16), grad_pre_t.astype(jnp.bfloat16)
 
 
@@ -396,18 +395,20 @@
         if tick == CROSS_TICK:
             adjoint = whole
             whole[...] = (pair[...].astype(jnp.float32) + other_pair[...].astype(jnp.float32)).astype(jnp.bfloat16)
-        acc[...] = jnp.zeros_like(acc)
-        acc_t[...] = jnp.zeros_like(acc_t)
-
-        def step(chunk, carry):
-            low_grad, low_grad_t = hidden_grads(adjoint, w_out_t, slope, chunk)
+        for chunk in range(CHUNKS):
+            now = slice(chunk * CHUNK, (chunk + 1) * CHUNK)
+            low_grad, low_grad_t = hidden_grads(adjoint, w_out_t, slope, now)
             both = jnp.concatenate([low_grad_t, low_grad], axis=0)
-            grads[:, columns(chunk)] = both
-            acc[...] += jnp.dot(both, w_in_t[columns(chunk), :], preferred_element_type=jnp.float32)
-            acc_t[...] += jnp.dot(low_grad, probe_t[columns(chunk), :], preferred_element_type=jnp.float32)
-            return carry
-
-        lax.fori_loop(0, CHUNKS, step, 0, unroll=UNROLL_DOWN)
+            grads[:, now] = both
+            product = jnp.dot(both, w_in_t[now, :], preferred_element_type=jnp.float32)
+            product_t = jnp.dot(low_grad, probe_t[now, :], preferred_element_type=jnp.float32)
+            if chunk:
+                acc[...] += product
+                acc_t[...] += product_t
+            else:
+                acc[...] = product
+                acc_t[...] = product_t
+
         normed, normed_t = norm[0], norm[1]
         rscale, tangent_dot = stat[0][:, :1], stat[1][:, :1]
         grad_norm = acc[ROWS:]
@@ -452,7 +453,7 @@
         lhs[ROWS:] = jnp.zeros((ROWS, FEATURES), jnp.bfloat16)
 
         def bottom(chunk, carry):
-            low_grad, low_grad_t = hidden_grads(pair, w_out_t, slope, chunk)
+            low_grad, low_grad_t = hidden_grads(pair, w_out_t, slope, columns(chunk))
             rhs[:, columns(chunk)] = jnp.concatenate([low_grad_t, low_grad], axis=0)
             return carry
 
@@ -512,6 +513,21 @@
         compiler_params=PARAMS,
         name="curvature_last" if final else "curvature_first",
     )(*operands)
+
+
+def block_sum_kernel(blocks, total):
+    total[...] = sum(blocks[index].astype(jnp.float32) for index in range(4)).astype(jnp.bfloat16)
+
+
+def block_sum_call(blocks):
+    return pl.pallas_call(
+        block_sum_kernel,
+        out_shape=jax.ShapeDtypeStruct(blocks.shape[1:], jnp.bfloat16),
+        in_specs=[WHOLE],
+        out_specs=WHOLE,
+        compiler_params=PARAMS,
+        name="block_sum",
+    )(blocks)
 
 
 def shards(inputs, targets, w_in, w_out, probes):
@@ -565,7 +581,7 @@
     other = routed(away, swap_core)
     summed = (stay + other.astype(jnp.float32)).astype(jnp.bfloat16)
     summed = lax.all_to_all(summed.reshape(4, 64, HIDDEN), "y", 0, 0, tiled=True)
-    summed = jnp.sum(summed.astype(jnp.float32), axis=0).astype(jnp.bfloat16)
+    summed = block_sum_call(summed)
     summed = lax.all_to_all(summed.reshape(8, 8, HIDDEN), ("b1", "b2", "b4"), 0, 0, tiled=True)
     summed = jnp.sum(summed.astype(jnp.float32), axis=0)
     probe_own = lax.dynamic_slice_in_dim(probe, lax.axis_index(DP) * 8, 8, 0)

time: 239 us -> 239 us (level)
  no operation moved by 1% of the time
where the time goes in v7:
time: 239 us; the launch traced here: 237 us
  waiting for transfers between devices  114 us (48%)
  starting transfers between devices  89.1 us (37%)
  blocking collectives  19 us (8%)
  Pallas kernels  9.77 us (4%)
  other arithmetic  2.59 us (1%)
    ppermute x46, waiting for transfers between devices, routed(): return lax.ppermute(value, NAMES, pairs)  98.7 us
    ppermute x46, starting transfers between devices, routed(): return lax.ppermute(value, NAMES, pairs)  83.3 us
    all_to_all x1, blocking collectives, shards(): lax.all_to_all(summed.reshape(4, 64, HIDDEN), 'y', 0, 0, tiled=True)  19 us
    all_to_all x1, waiting for transfers between devices, shards(): lax.all_to_all(summed.reshape(8, 8, HIDDEN), ('b1', 'b2', 'b4'), 0, 0, ti...  15.5 us
    all_to_all x1, starting transfers between devices, shards(): lax.all_to_all(summed.reshape(8, 8, HIDDEN), ('b1', 'b2', 'b4'), 0, 0, ti...  5.8 us
  transfers between devices with their start and end apart: 47, of which 18 were waited for; matrix products, arithmetic and copies ran while one was open for 1% of the time, Pallas kernels for 3%

profile of v7, /device:TPU:8, one launch (start us, length us, event | category | flops | bytes accessed | tf_op | source)
XLA Modules:
  0.0 237.5 jit_solution(13920402368779915199)
XLA Ops:
  0.0 0.8 copy-done.2
  0.8 9.1 %collective-permute-start.6 = (bf16[32,512]{1,0:T(8,128)(2,1)S(1)}, bf16[32,512]{1,0:T(8,128)(2,1)S(1)}, u32[]{:S(2)}, u32[]{:S(2)}) collective-permute-start(bf16[32,512]{1,0:T(8,128)(2,1)S(1)} %settled.1), channel_id=1, source_target_pairs={{0,32},{1,33},{2,34},{3,35},{4,36},{5,37},{6,38},{7,39},{8,40},{9,... | collective-permute-start | bytes 98312 | tf_op jit(solution)/shard_map/ppermute | solution.py:51
  9.9 1.9 collective-permute-start
  11.8 0.8 constant_dynamic-update-slice_fusion.4
  12.6 5.2 %collective-permute-start.7 = (bf16[64,512]{1,0:T(8,128)(2,1)S(1)}, bf16[64,512]{1,0:T(8,128)(2,1)S(1)}, u32[]{:S(2)}, u32[]{:S(2)}) collective-permute-start(bf16[64,512]{1,0:T(8,128)(2,1)S(1)} %pad_maximum_fusion.5), channel_id=1, source_target_pairs={{0,16},{1,17},{2,18},{3,19},{4,20},{5,21},{6,22},{7,23},{8,24},{9,... | collective-permute-start | bytes 196616 | tf_op jit(solution)/shard_map/ppermute | solution.py:51
  17.8 2.4 %collective-permute-done = bf16[8,2048]{1,0:T(8,128)(2,1)S(1)} collective-permute-done((bf16[8,2048]{1,0:T(8,128)(2,1)}, bf16[8,2048]{1,0:T(8,128)(2,1)S(1)}, u32[]{:S(2)}, u32[]{:S(2)}) %collective-permute-start) | collective-permute-done | bytes 32800 | tf_op jit(solution)/shard_map/ppermute | solution.py:51
  20.9 5.2 %collective-permute-start.1 = (bf16[16,2048]{1,0:T(8,128)(2,1)S(1)}, bf16[16,2048]{1,0:T(8,128)(2,1)S(1)}, u32[]{:S(2)}, u32[]{:S(2)}) collective-permute-start(bf16[16,2048]{1,0:T(8,128)(2,1)S(1)} %pad_maximum_fusion.4), channel_id=1, source_target_pairs={{0,16},{1,17},{2,18},{3,19},{4,20},{5,21},{6,22},{7,23},{8,24},{9,... | collective-permute-start | bytes 196616 | tf_op jit(solution)/shard_map/ppermute | solution.py:51
  26.2 3.5 %collective-permute-start.8 = (bf16[128,512]{1,0:T(8,128)(2,1)S(1)}, bf16[128,512]{1,0:T(8,128)(2,1)S(1)}, u32[]{:S(2)}, u32[]{:S(2)}) collective-permute-start(bf16[128,512]{1,0:T(8,128)(2,1)S(1)} %pad_maximum_fusion.3), channel_id=1, source_target_pairs={{0,8},{1,9},{2,10},{3,11},{4,12},{5,13},{6,14},{7,15},{8,0},{9,1},... | collective-permute-start | bytes 393224 | tf_op jit(solution)/shard_map/ppermute | solution.py:51
  29.7 0.8 pad_maximum_fusion.2
  30.5 2.8 %collective-permute-start.2 = (bf16[32,2048]{1,0:T(8,128)(2,1)S(1)}, bf16[32,2048]{1,0:T(8,128)(2,1)S(1)}, u32[]{:S(2)}, u32[]{:S(2)}) collective-permute-start(bf16[32,2048]{1,0:T(8,128)(2,1)S(1)} %pad_maximum_fusion.2), channel_id=1, source_target_pairs={{0,8},{1,9},{2,10},{3,11},{4,12},{5,13},{6,14},{7,15},{8,0},{9,1},... | collective-permute-start | bytes 393224 | tf_op jit(solution)/shard_map/ppermute | solution.py:51
  33.4 3.5 %collective-permute-start.9 = (bf16[256,512]{1,0:T(8,128)(2,1)S(1)}, bf16[256,512]{1,0:T(8,128)(2,1)S(1)}, u32[]{:S(2)}, u32[]{:S(2)}) collective-permute-start(bf16[256,512]{1,0:T(8,128)(2,1)S(1)} %pad_maximum_fusion.1), channel_id=1, source_target_pairs={{0,6},{1,7},{2,4},{3,5},{4,2},{5,3},{6,0},{7,1},{8,14},{9,15},{10,... | collective-permute-start | bytes 786440 | tf_op jit(solution)/shard_map/ppermute | solution.py:51
  37.4 3.3 %collective-permute-start.3 = (bf16[64,2048]{1,0:T(8,128)(2,1)S(1)}, bf16[64,2048]{1,0:T(8,128)(2,1)S(1)}, u32[]{:S(2)}, u32[]{:S(2)}) collective-permute-start(bf16[64,2048]{1,0:T(8,128)(2,1)S(1)} %pad_maximum_fusion), channel_id=1, source_target_pairs={{0,2},{1,3},{2,0},{3,1},{4,6},{5,7},{6,4},{7,5},{8,10},{9,11},{10,... | collective-permute-start | bytes 786440 | tf_op jit(solution)/shard_map/ppermute | solution.py:51
  40.8 0.8 collective-permute-done.9
  41.7 3.6 %collective-permute-start.10 = (bf16[512,512]{1,0:T(8,128)(2,1)S(1)}, bf16[512,512]{1,0:T(8,128)(2,1)S(1)}, u32[]{:S(2)}, u32[]{:S(2)}) collective-permute-start(bf16[512,512]{1,0:T(8,128)(2,1)S(1)} %get-tuple-element.203), channel_id=1, source_target_pairs={{0,2},{1,3},{2,0},{3,1},{4,6},{5,7},{6,4},{7,5},{8,10},{9,11},{10,... | collective-permute-start | bytes 1572872 | tf_op jit(solution)/shard_map/ppermute | solution.py:51
  45.3 3.1 %collective-permute-done.3 = bf16[64,2048]{1,0:T(8,128)(2,1)S(1)} collective-permute-done((bf16[64,2048]{1,0:T(8,128)(2,1)S(1)}, bf16[64,2048]{1,0:T(8,128)(2,1)S(1)}, u32[]{:S(2)}, u32[]{:S(2)}) %collective-permute-start.3) | collective-permute-done | bytes 262176 | tf_op jit(solution)/shard_map/ppermute | solution.py:51
  48.5 3.5 %collective-permute-start.4 = (bf16[128,2048]{1,0:T(8,128)(2,1)S(1)}, bf16[128,2048]{1,0:T(8,128)(2,1)S(1)}, u32[]{:S(2)}, u32[]{:S(2)}) collective-permute-start(bf16[128,2048]{1,0:T(8,128)(2,1)S(1)} %get-tuple-element.205), channel_id=1, source_target_pairs={{0,6},{1,7},{2,4},{3,5},{4,2},{5,3},{6,0},{7,1},{8,14},{9,15},{10,... | collective-permute-start | bytes 1572872 | tf_op jit(solution)/shard_map/ppermute | solution.py:51
  52.0 4.2 %collective-permute-done.10 = bf16[512,512]{1,0:T(8,128)(2,1)S(1)} collective-permute-done((bf16[512,512]{1,0:T(8,128)(2,1)S(1)}, bf16[512,512]{1,0:T(8,128)(2,1)S(1)}, u32[]{:S(2)}, u32[]{:S(2)}) %collective-permute-start.10) | collective-permute-done | bytes 524320 | tf_op jit(solution)/shard_map/ppermute | solution.py:51
  56.2 1.9 collective-permute-start.11
  58.2 1.4 collective-permute-done.4
  59.6 1.9 collective-permute-start.5
  61.6 1.3 opening.1
  63.1 1.1 collective-permute-done.5.other_in.refs_2_
  64.2 1.2 layer_up_0.3
  65.4 2.2 collective-permute-start.29
  67.6 1.2 layer_up_0.2
  68.8 1.3 collective-permute-start.12
  71.5 1.9 collective-permute-done.12.refs_6_
  78.3 9.2 %collective-permute-start.34 = (bf16[2,64,512]{2,1,0:T(8,128)(2,1)S(1)}, bf16[2,64,512]{2,1,0:T(8,128)(2,1)S(1)}, u32[]{:S(2)}, u32[]{:S(2)}) collective-permute-start(bf16[2,64,512]{2,1,0:T(8,128)(2,1)S(1)} %get-tuple-element.159), channel_id=1, source_target_pairs={{0,64},{1,65},{2,66},{3,67},{4,68},{5,69},{6,70},{7,71},{8,72},{9,... | collective-permute-start | bytes 393224 | tf_op jit(solution)/shard_map/ppermute | solution.py:51
  87.5 1.3 collective-permute-start.17
  88.8 1.2 collective-permute-done.34.refs_6_
  90.0 0.8 collective-permute-start.35
  94.2 2.0 turned_weights.1
  99.1 1.3 collective-permute-start.39
  100.4 1.3 collective-permute-start.23
  101.7 29.3 %collective-permute-done.39.refs_1_ = bf16[2,64,512]{2,1,0:T(8,128)(2,1)S(1)} collective-permute-done((bf16[2,64,512]{2,1,0:T(8,128)(2,1)S(1)}, bf16[2,64,512]{2,1,0:T(8,128)(2,1)S(1)}, u32[]{:S(2)}, u32[]{:S(2)}) %collective-permute-start.39) | collective-permute-done | bytes 131104 | tf_op jit(solution)/shard_map/ppermute | solution.py:51
  131.7 4.7 %collective-permute-done.23.refs_1_ = bf16[2,64,512]{2,1,0:T(8,128)(2,1)S(1)} collective-permute-done((bf16[2,64,512]{2,1,0:T(8,128)(2,1)S(1)}, bf16[2,64,512]{2,1,0:T(8,128)(2,1)S(1)}, u32[]{:S(2)}, u32[]{:S(2)}) %collective-permute-start.23) | collective-permute-done | bytes 131104 | tf_op jit(solution)/shard_map/ppermute | solution.py:51
  141.3 1.3 collective-permute-start.44
  142.6 1.3 collective-permute-start.28
  143.9 42.7 %collective-permute-done.44.refs_1_ = bf16[2,64,512]{2,1,0:T(8,128)(2,1)S(1)} collective-permute-done((bf16[2,64,512]{2,1,0:T(8,128)(2,1)S(1)}, bf16[2,64,512]{2,1,0:T(8,128)(2,1)S(1)}, u32[]{:S(2)}, u32[]{:S(2)}) %collective-permute-start.44) | collective-permute-done | bytes 131104 | tf_op jit(solution)/shard_map/ppermute | solution.py:51
  186.7 1.4 curvature_first.1
  188.0 1.3 collective-permute-done.28.refs_1_
  189.3 1.4 curvature_last.1
  190.7 1.9 collective-permute-start.45
  192.6 2.6 %collective-permute-done.45 = bf16[256,2048]{1,0:T(8,128)(2,1)S(1)} collective-permute-done((bf16[256,2048]{1,0:T(8,128)(2,1)S(1)}, bf16[256,2048]{1,0:T(8,128)(2,1)S(1)}, u32[]{:S(2)}, u32[]{:S(2)}) %collective-permute-start.45) | collective-permute-done | bytes 1048608 | tf_op jit(solution)/shard_map/ppermute | solution.py:51
  195.6 19.0 %all_to_all.10.blocks = bf16[4,64,2048]{2,1,0:T(8,128)(2,1)S(1)} all-to-all(bf16[4,64,2048]{2,1,0:T(8,128)(2,1)S(1)} %bitcast.32), channel_id=1, replica_groups=mesh['zh'=2,'x'=4,'b4'=2,'b2'=2,'b1'=2,'y'=4,'c'=2] {'y'}, dimensions={0} | all-to-all | bytes 2097152 | tf_op jit(solution)/shard_map/all_to_all | solution.py:583
  214.6 0.8 block_sum.1
  215.5 5.8 %all-to-all-start.1 = ((bf16[8,8,2048]{2,1,0:T(8,128)(2,1)}), bf16[8,8,2048]{2,1,0:T(8,128)(2,1)S(1)}, u32[]{:S(2)}, u32[]{:S(2)}) async-start(bf16[8,8,2048]{2,1,0:T(8,128)(2,1)} %bitcast.10), calls=%async_computation.1 | async-start | bytes 524288 | tf_op jit(solution)/shard_map/all_to_all | solution.py:585
  221.3 15.5 %all-to-all-done.1 = bf16[8,8,2048]{2,1,0:T(8,128)(2,1)S(1)} async-done(((bf16[8,8,2048]{2,1,0:T(8,128)(2,1)}), bf16[8,8,2048]{2,1,0:T(8,128)(2,1)S(1)}, u32[]{:S(2)}, u32[]{:S(2)}) %all-to-all-start.1) | async-done | bytes 262176 | tf_op jit(solution)/shard_map/all_to_all | solution.py:585
  (116 shorter events, 20.5 us)
Async XLA Ops:
  0.0 37.4 %copy-start.3 = (bf16[1,8,2048]{2,1,0:T(8,128)(2,1)S(1)}, bf16[1,8,2048]{2,1,0:T(8,128)(2,1)}, u32[]{:S(2)}) copy-start(bf16[1,8,2048]{2,1,0:T(8,128)(2,1)} %param.7) | copy-start | bytes 98308
  0.8 11.8 %collective-permute-start.6 = (bf16[32,512]{1,0:T(8,128)(2,1)S(1)}, bf16[32,512]{1,0:T(8,128)(2,1)S(1)}, u32[]{:S(2)}, u32[]{:S(2)}) collective-permute-start(bf16[32,512]{1,0:T(8,128)(2,1)S(1)} %settled.1), channel_id=1, source_target_pairs={{0,32},{1,33},{2,34},{3,35},{4,36},{5,37},{6,38},{7,39},{8,40},{9,... | collective-permute-start | bytes 98312 | tf_op jit(solution)/shard_map/ppermute | solution.py:51
  9.9 10.3 %collective-permute-start = (bf16[8,2048]{1,0:T(8,128)(2,1)}, bf16[8,2048]{1,0:T(8,128)(2,1)S(1)}, u32[]{:S(2)}, u32[]{:S(2)}) collective-permute-start(bf16[8,2048]{1,0:T(8,128)(2,1)} %bitcast.33), channel_id=1, source_target_pairs={{0,32},{1,33},{2,34},{3,35},{4,36},{5,37},{6,38},{7,39},{8,40},{9,... | collective-permute-start | bytes 98312 | tf_op jit(solution)/shard_map/ppermute | solution.py:51
  12.6 13.6 %collective-permute-start.7 = (bf16[64,512]{1,0:T(8,128)(2,1)S(1)}, bf16[64,512]{1,0:T(8,128)(2,1)S(1)}, u32[]{:S(2)}, u32[]{:S(2)}) collective-permute-start(bf16[64,512]{1,0:T(8,128)(2,1)S(1)} %pad_maximum_fusion.5), channel_id=1, source_target_pairs={{0,16},{1,17},{2,18},{3,19},{4,20},{5,21},{6,22},{7,23},{8,24},{9,... | collective-permute-start | bytes 196616 | tf_op jit(solution)/shard_map/ppermute | solution.py:51
  20.9 8.8 %collective-permute-start.1 = (bf16[16,2048]{1,0:T(8,128)(2,1)S(1)}, bf16[16,2048]{1,0:T(8,128)(2,1)S(1)}, u32[]{:S(2)}, u32[]{:S(2)}) collective-permute-start(bf16[16,2048]{1,0:T(8,128)(2,1)S(1)} %pad_maximum_fusion.4), channel_id=1, source_target_pairs={{0,16},{1,17},{2,18},{3,19},{4,20},{5,21},{6,22},{7,23},{8,24},{9,... | collective-permute-start | bytes 196616 | tf_op jit(solution)/shard_map/ppermute | solution.py:51
  26.2 7.2 %collective-permute-start.8 = (bf16[128,512]{1,0:T(8,128)(2,1)S(1)}, bf16[128,512]{1,0:T(8,128)(2,1)S(1)}, u32[]{:S(2)}, u32[]{:S(2)}) collective-permute-start(bf16[128,512]{1,0:T(8,128)(2,1)S(1)} %pad_maximum_fusion.3), channel_id=1, source_target_pairs={{0,8},{1,9},{2,10},{3,11},{4,12},{5,13},{6,14},{7,15},{8,0},{9,1},... | collective-permute-start | bytes 393224 | tf_op jit(solution)/shard_map/ppermute | solution.py:51
  30.5 6.9 %collective-permute-start.2 = (bf16[32,2048]{1,0:T(8,128)(2,1)S(1)}, bf16[32,2048]{1,0:T(8,128)(2,1)S(1)}, u32[]{:S(2)}, u32[]{:S(2)}) collective-permute-start(bf16[32,2048]{1,0:T(8,128)(2,1)S(1)} %pad_maximum_fusion.2), channel_id=1, source_target_pairs={{0,8},{1,9},{2,10},{3,11},{4,12},{5,13},{6,14},{7,15},{8,0},{9,1},... | collective-permute-start | bytes 393224 | tf_op jit(solution)/shard_map/ppermute | solution.py:51
  33.4 8.3 %collective-permute-start.9 = (bf16[256,512]{1,0:T(8,128)(2,1)S(1)}, bf16[256,512]{1,0:T(8,128)(2,1)S(1)}, u32[]{:S(2)}, u32[]{:S(2)}) collective-permute-start(bf16[256,512]{1,0:T(8,128)(2,1)S(1)} %pad_maximum_fusion.1), channel_id=1, source_target_pairs={{0,6},{1,7},{2,4},{3,5},{4,2},{5,3},{6,0},{7,1},{8,14},{9,15},{10,... | collective-permute-start | bytes 786440 | tf_op jit(solution)/shard_map/ppermute | solution.py:51
  37.4 11.0 %collective-permute-start.3 = (bf16[64,2048]{1,0:T(8,128)(2,1)S(1)}, bf16[64,2048]{1,0:T(8,128)(2,1)S(1)}, u32[]{:S(2)}, u32[]{:S(2)}) collective-permute-start(bf16[64,2048]{1,0:T(8,128)(2,1)S(1)} %pad_maximum_fusion), channel_id=1, source_target_pairs={{0,2},{1,3},{2,0},{3,1},{4,6},{5,7},{6,4},{7,5},{8,10},{9,11},{10,... | collective-permute-start | bytes 786440 | tf_op jit(solution)/shard_map/ppermute | solution.py:51
  41.7 14.5 %collective-permute-start.10 = (bf16[512,512]{1,0:T(8,128)(2,1)S(1)}, bf16[512,512]{1,0:T(8,128)(2,1)S(1)}, u32[]{:S(2)}, u32[]{:S(2)}) collective-permute-start(bf16[512,512]{1,0:T(8,128)(2,1)S(1)} %get-tuple-element.203), channel_id=1, source_target_pairs={{0,2},{1,3},{2,0},{3,1},{4,6},{5,7},{6,4},{7,5},{8,10},{9,11},{10,... | collective-permute-start | bytes 1572872 | tf_op jit(solution)/shard_map/ppermute | solution.py:51
  48.5 11.1 %collective-permute-start.4 = (bf16[128,2048]{1,0:T(8,128)(2,1)S(1)}, bf16[128,2048]{1,0:T(8,128)(2,1)S(1)}, u32[]{:S(2)}, u32[]{:S(2)}) collective-permute-start(bf16[128,2048]{1,0:T(8,128)(2,1)S(1)} %get-tuple-element.205), channel_id=1, source_target_pairs={{0,6},{1,7},{2,4},{3,5},{4,2},{5,3},{6,0},{7,1},{8,14},{9,15},{10,... | collective-permute-start | bytes 1572872 | tf_op jit(solution)/shard_map/ppermute | solution.py:51
  56.2 6.6 %collective-permute-start.11 = (bf16[1024,512]{1,0:T(8,128)(2,1)S(1)}, bf16[1024,512]{1,0:T(8,128)(2,1)S(1)}, u32[]{:S(2)}, u32[]{:S(2)}) collective-permute-start(bf16[1024,512]{1,0:T(8,128)(2,1)S(1)} %constant_dynamic-update-slice_fusion.16.refs_6_), channel_id=1, source_target_pairs={{0,1},{1,0},{2,3},{3,2},{4,5},{5,4},{6,7},{7,6},{8,9},{9,8},{10,11... | collective-permute-start | bytes 3145736 | tf_op jit(solution)/shard_map/ppermute | solution.py:51
  59.6 4.6 %collective-permute-start.5 = (bf16[256,2048]{1,0:T(8,128)(2,1)S(1)}, bf16[256,2048]{1,0:T(8,128)(2,1)S(1)}, u32[]{:S(2)}, u32[]{:S(2)}) collective-permute-start(bf16[256,2048]{1,0:T(8,128)(2,1)S(1)} %constant_dynamic-update-slice_fusion.5.own_in.refs_1_), channel_id=1, source_target_pairs={{0,1},{1,0},{2,3},{3,2},{4,5},{5,4},{6,7},{7,6},{8,9},{9,8},{10,11... | collective-permute-start | bytes 3145736 | tf_op jit(solution)/shard_map/ppermute | solution.py:51
  65.4 5.4 %collective-permute-start.29 = (bf16[2,64,512]{2,1,0:T(8,128)(2,1)S(1)}, bf16[2,64,512]{2,1,0:T(8,128)(2,1)S(1)}, u32[]{:S(2)}, u32[]{:S(2)}) collective-permute-start(bf16[2,64,512]{2,1,0:T(8,128)(2,1)S(1)} %get-tuple-element.155), channel_id=1, source_target_pairs={{0,64},{1,65},{2,66},{3,67},{4,68},{5,69},{6,70},{7,71},{8,72},{9,... | collective-permute-start | bytes 393224 | tf_op jit(solution)/shard_map/ppermute | solution.py:51
  68.8 4.6 %collective-permute-start.12 = (bf16[2,64,512]{2,1,0:T(8,128)(2,1)S(1)}, bf16[2,64,512]{2,1,0:T(8,128)(2,1)S(1)}, u32[]{:S(2)}, u32[]{:S(2)}) collective-permute-start(bf16[2,64,512]{2,1,0:T(8,128)(2,1)S(1)} %get-tuple-element.107), channel_id=1, source_target_pairs={{0,64},{1,65},{2,66},{3,67},{4,68},{5,69},{6,70},{7,71},{8,72},{9,... | collective-permute-start | bytes 393224 | tf_op jit(solution)/shard_map/ppermute | solution.py:51
  70.8 3.3 %collective-permute-start.30 = (bf16[2,64,512]{2,1,0:T(8,128)(2,1)S(1)}, bf16[2,64,512]{2,1,0:T(8,128)(2,1)S(1)}, u32[]{:S(2)}, u32[]{:S(2)}) collective-permute-start(bf16[2,64,512]{2,1,0:T(8,128)(2,1)S(1)} %get-tuple-element.156), channel_id=1, source_target_pairs={{64,128},{65,129},{66,130},{67,131},{68,132},{69,133},{70,134},{71... | collective-permute-start | bytes 393224 | tf_op jit(solution)/shard_map/ppermute | solution.py:51
  73.4 1.4 collective-permute-start.13
  74.1 1.4 collective-permute-start.31
  74.8 1.4 collective-permute-start.14
  75.5 1.4 collective-permute-start.32
  76.2 1.4 collective-permute-start.15
  76.9 1.4 collective-permute-start.33
  77.6 9.9 %collective-permute-start.16 = (bf16[2,64,512]{2,1,0:T(8,128)(2,1)S(1)}, bf16[2,64,512]{2,1,0:T(8,128)(2,1)S(1)}, u32[]{:S(2)}, u32[]{:S(2)}) collective-permute-start(bf16[2,64,512]{2,1,0:T(8,128)(2,1)S(1)} %collective-permute-done.15.refs_6_), channel_id=1, source_target_pairs={{1,313},{3,315},{5,317},{7,319},{9,305},{11,307},{13,309},{15,311}... | collective-permute-start | bytes 393224 | tf_op jit(solution)/shard_map/ppermute | solution.py:51
  78.3 11.7 %collective-permute-start.34 = (bf16[2,64,512]{2,1,0:T(8,128)(2,1)S(1)}, bf16[2,64,512]{2,1,0:T(8,128)(2,1)S(1)}, u32[]{:S(2)}, u32[]{:S(2)}) collective-permute-start(bf16[2,64,512]{2,1,0:T(8,128)(2,1)S(1)} %get-tuple-element.159), channel_id=1, source_target_pairs={{0,64},{1,65},{2,66},{3,67},{4,68},{5,69},{6,70},{7,71},{8,72},{9,... | collective-permute-start | bytes 393224 | tf_op jit(solution)/shard_map/ppermute | solution.py:51
  87.5 3.8 %collective-permute-start.17 = (bf16[2,64,512]{2,1,0:T(8,128)(2,1)S(1)}, bf16[2,64,512]{2,1,0:T(8,128)(2,1)S(1)}, u32[]{:S(2)}, u32[]{:S(2)}) collective-permute-start(bf16[2,64,512]{2,1,0:T(8,128)(2,1)S(1)} %get-tuple-element.111), channel_id=1, source_target_pairs={{0,64},{1,65},{2,66},{3,67},{4,68},{5,69},{6,70},{7,71},{8,72},{9,... | collective-permute-start | bytes 393224 | tf_op jit(solution)/shard_map/ppermute | solution.py:51
  90.0 2.7 %collective-permute-start.35 = (bf16[2,64,512]{2,1,0:T(8,128)(2,1)S(1)}, bf16[2,64,512]{2,1,0:T(8,128)(2,1)S(1)}, u32[]{:S(2)}, u32[]{:S(2)}) collective-permute-start(bf16[2,64,512]{2,1,0:T(8,128)(2,1)S(1)} %get-tuple-element.160), channel_id=1, source_target_pairs={{64,128},{65,129},{66,130},{67,131},{68,132},{69,133},{70,134},{71... | collective-permute-start | bytes 393224 | tf_op jit(solution)/shard_map/ppermute | solution.py:51
  91.4 2.1 collective-permute-start.18
  92.0 2.1 collective-permute-start.20
  92.7 3.5 %collective-permute-start.36 = (bf16[2,64,512]{2,1,0:T(8,128)(2,1)S(1)}, bf16[2,64,512]{2,1,0:T(8,128)(2,1)S(1)}, u32[]{:S(2)}, u32[]{:S(2)}) collective-permute-start(bf16[2,64,512]{2,1,0:T(8,128)(2,1)S(1)} %get-tuple-element.161), channel_id=1, source_target_pairs={{128,192},{129,193},{130,194},{131,195},{132,196},{133,197},{134,1... | collective-permute-start | bytes 393224 | tf_op jit(solution)/shard_map/ppermute | solution.py:51
  93.5 3.5 %collective-permute-start.19 = (bf16[2,64,512]{2,1,0:T(8,128)(2,1)S(1)}, bf16[2,64,512]{2,1,0:T(8,128)(2,1)S(1)}, u32[]{:S(2)}, u32[]{:S(2)}) collective-permute-start(bf16[2,64,512]{2,1,0:T(8,128)(2,1)S(1)} %get-tuple-element.113), channel_id=1, source_target_pairs={{128,192},{129,193},{130,194},{131,195},{132,196},{133,197},{134,1... | collective-permute-start | bytes 393224 | tf_op jit(solution)/shard_map/ppermute | solution.py:51
  96.3 1.4 collective-permute-start.37
  97.0 1.4 collective-permute-start.21
  97.7 1.4 collective-permute-start.38
  98.4 2.0 collective-permute-start.22
  99.1 31.9 %collective-permute-start.39 = (bf16[2,64,512]{2,1,0:T(8,128)(2,1)S(1)}, bf16[2,64,512]{2,1,0:T(8,128)(2,1)S(1)}, u32[]{:S(2)}, u32[]{:S(2)}) collective-permute-start(bf16[2,64,512]{2,1,0:T(8,128)(2,1)S(1)} %get-tuple-element.174), channel_id=1, source_target_pairs={{64,0},{65,1},{66,2},{67,3},{68,4},{69,5},{70,6},{71,7},{72,8},{73... | collective-permute-start | bytes 393224 | tf_op jit(solution)/shard_map/ppermute | solution.py:51
  100.4 36.0 %collective-permute-start.23 = (bf16[2,64,512]{2,1,0:T(8,128)(2,1)S(1)}, bf16[2,64,512]{2,1,0:T(8,128)(2,1)S(1)}, u32[]{:S(2)}, u32[]{:S(2)}) collective-permute-start(bf16[2,64,512]{2,1,0:T(8,128)(2,1)S(1)} %get-tuple-element.130), channel_id=1, source_target_pairs={{64,0},{65,1},{66,2},{67,3},{68,4},{69,5},{70,6},{71,7},{72,8},{73... | collective-permute-start | bytes 393224 | tf_op jit(solution)/shard_map/ppermute | solution.py:51
  131.0 6.0 %collective-permute-start.40 = (bf16[2,64,512]{2,1,0:T(8,128)(2,1)S(1)}, bf16[2,64,512]{2,1,0:T(8,128)(2,1)S(1)}, u32[]{:S(2)}, u32[]{:S(2)}) collective-permute-start(bf16[2,64,512]{2,1,0:T(8,128)(2,1)S(1)} %get-tuple-element.178), channel_id=1, source_target_pairs={{256,248},{257,449},{258,250},{259,451},{260,252},{261,453},{262,2... | collective-permute-start | bytes 393224 | tf_op jit(solution)/shard_map/ppermute | solution.py:51
  136.4 1.4 collective-permute-start.24
  137.1 1.4 collective-permute-start.41
  137.8 1.4 collective-permute-start.25
  138.5 1.4 collective-permute-start.42
  139.2 1.4 collective-permute-start.26
  139.9 1.4 collective-permute-start.43
  140.6 2.0 collective-permute-start.27
  141.3 45.4 %collective-permute-start.44 = (bf16[2,64,512]{2,1,0:T(8,128)(2,1)S(1)}, bf16[2,64,512]{2,1,0:T(8,128)(2,1)S(1)}, u32[]{:S(2)}, u32[]{:S(2)}) collective-permute-start(bf16[2,64,512]{2,1,0:T(8,128)(2,1)S(1)} %get-tuple-element.190), channel_id=1, source_target_pairs={{64,0},{65,1},{66,2},{67,3},{68,4},{69,5},{70,6},{71,7},{72,8},{73... | collective-permute-start | bytes 393224 | tf_op jit(solution)/shard_map/ppermute | solution.py:51
  142.6 46.7 %collective-permute-start.28 = (bf16[2,64,512]{2,1,0:T(8,128)(2,1)S(1)}, bf16[2,64,512]{2,1,0:T(8,128)(2,1)S(1)}, u32[]{:S(2)}, u32[]{:S(2)}) collective-permute-start(bf16[2,64,512]{2,1,0:T(8,128)(2,1)S(1)} %get-tuple-element.145), channel_id=1, source_target_pairs={{64,0},{65,1},{66,2},{67,3},{68,4},{69,5},{70,6},{71,7},{72,8},{73... | collective-permute-start | bytes 393224 | tf_op jit(solution)/shard_map/ppermute | solution.py:51
  190.7 4.6 %collective-permute-start.45 = (bf16[256,2048]{1,0:T(8,128)(2,1)S(1)}, bf16[256,2048]{1,0:T(8,128)(2,1)S(1)}, u32[]{:S(2)}, u32[]{:S(2)}) collective-permute-start(bf16[256,2048]{1,0:T(8,128)(2,1)S(1)} %get-tuple-element.202), channel_id=1, source_target_pairs={{0,1},{1,0},{2,3},{3,2},{4,5},{5,4},{6,7},{7,6},{8,9},{9,8},{10,11... | collective-permute-start | bytes 3145736 | tf_op jit(solution)/shard_map/ppermute | solution.py:51
  215.5 21.3 %all-to-all-start.1 = ((bf16[8,8,2048]{2,1,0:T(8,128)(2,1)}), bf16[8,8,2048]{2,1,0:T(8,128)(2,1)S(1)}, u32[]{:S(2)}, u32[]{:S(2)}) async-start(bf16[8,8,2048]{2,1,0:T(8,128)(2,1)} %bitcast.10), calls=%async_computation.1 | async-start | bytes 524288 | tf_op jit(solution)/shard_map/all_to_all | solution.py:585
  (4 other events, 44.3 us)
